TPU v7x, 32 devices: a whole 2x2x4 slice. The times are simulated.
32 devices in a mesh: seq: 4 (over y, x), blk: 8 (over z, core).
Axes of the slice: x: 2, y: 2, z: 4, core: 2. Of those that a mesh axis runs over, the one named last changes fastest.
Arguments:
- tokens: bfloat16 [4096, 1024], P(('seq', 'blk')), may hold values from -6 to 6
- first_values: bfloat16 [4096, 1024], P(('seq', 'blk')), may hold values from -6 to 6
- doc_lengths: int32 [4, 4], P('seq'), may hold values from 1 to 897, as said below
- attn_gain: float32 [1024], replicated, may hold values from 0.2 to 4.5
- query_weight: bfloat16 [1024, 1024], replicated, may hold values from -0.1875 to 0.1875
- key_weight: bfloat16 [1024, 1024], replicated, may hold values from -0.1875 to 0.1875
- value_weight: bfloat16 [1024, 1024], replicated, may hold values from -0.1875 to 0.1875
- out_weight: bfloat16 [1024, 1024], replicated, may hold values from -3 to 3
- ffn_gain: float32 [1024], replicated, may hold values from 0.2 to 4.5
- gate_weight: bfloat16 [1024, 2816], replicated, may hold values from -0.1875 to 0.1875
- up_weight: bfloat16 [1024, 2816], replicated, may hold values from -0.1875 to 0.1875
- down_weight: bfloat16 [2816, 1024], replicated, may hold values from -0.109375 to 0.109375
- cotangent: bfloat16 [4096, 1024], P(('seq', 'blk')), may hold values from -6 to 6
Outputs:
- layer_output: float32 [4096, 1024], P(('seq', 'blk'))
- grad_tokens: float32 [4096, 1024], P(('seq', 'blk'))
- grad_first: float32 [4096, 1024], P(('seq', 'blk'))
- grad_attn_gain: float32 [1024], P('blk')
- grad_query: float32 [1024, 1024], P('blk')
- grad_key: float32 [1024, 1024], P('blk')
- grad_value: float32 [1024, 1024], P('blk')
- grad_out_weight: float32 [1024, 1024], P('blk')
- grad_ffn_gain: float32 [1024], P('blk')
- grad_gate: float32 [1024, 2816], P('blk')
- grad_up: float32 [1024, 2816], P('blk')
- grad_down: float32 [2816, 1024], P('blk')
Inputs may be any that keep to these rules, and one draw needn't show every extreme that they name: `doc_lengths`: each row sums to 1024.
All inputs are finite; a program needn't handle non-finite values.
Results may differ from a plain program's by a relative error of at most 0.022.
Values may be sent and summed in bfloat16 or wider, within the bound.
A program may use at most 256 MiB of HBM per device.

v0:
```python
import math

import jax
import jax.numpy as jnp
from jax import lax
from jax.sharding import PartitionSpec as P

HEAD_DIM = 64


EPS = 1e-05
THETA = 10000.0
MIX = 0.5
NEG = -1e30


def doc_layout(lengths, index):
    ends = jnp.cumsum(lengths, axis=-1)
    past = (index[:, None] >= ends).astype(jnp.int32)
    return (jnp.sum(past, axis=1), index - jnp.sum(past * lengths, axis=1))


def tables(position):
    half = HEAD_DIM // 2
    freq = THETA ** (-(jnp.arange(half).astype(jnp.float32) * 2.0 / HEAD_DIM))
    angle = position.astype(jnp.float32)[:, None] * freq[None, :]
    return (jnp.cos(angle)[:, None, :], jnp.sin(angle)[:, None, :])


def rotate(values, cosine, sine):
    half = values.shape[-1] // 2
    first = values[..., :half]
    second = values[..., half:]
    return jnp.concatenate(
        [first * cosine - second * sine, second * cosine + first * sine], axis=-1
    )


def by_blocks(step, carry, pieces, start):
    rows = pieces[0].shape[0]
    size = math.gcd(rows, 1024)
    count = rows // size
    if count == 1:
        return step(carry, pieces, start)
    stacked = tuple((piece.reshape((count, size) + piece.shape[1:]) for piece in pieces))
    offsets = jnp.arange(count, dtype=jnp.int32) * size

    def turn(state, inputs):
        return (step(state, inputs[1], start + inputs[0]), None)

    result, unused = lax.scan(turn, carry, (offsets, stacked))
    return result


def outer(left, right):
    return lax.dot_general(
        left, right, (((0,), (0,)), ((), ())), preferred_element_type=jnp.float32
    )


def back(left, weight):
    return lax.dot_general(
        left, weight, (((1,), (1,)), ((), ())), preferred_element_type=jnp.float32
    )


def local(
    tokens,
    first_values,
    doc_lengths,
    attn_gain,
    query_weight,
    key_weight,
    value_weight,
    out_weight,
    ffn_gain,
    gate_weight,
    up_weight,
    down_weight,
    cotangent,
):
    rows, width = tokens.shape
    heads = width // HEAD_DIM
    scale = HEAD_DIM ** (-0.5)
    shape3 = (rows, heads, HEAD_DIM)
    my_start = lax.axis_index("blk") * rows
    my_index = my_start + jnp.arange(rows, dtype=jnp.int32)
    my_doc, my_pos = doc_layout(doc_lengths, my_index)
    cosine, sine = tables(my_pos)
    source = tokens.astype(jnp.float32)
    inv_first = lax.rsqrt(jnp.mean(source * source, axis=-1, keepdims=True) + EPS)
    normed = (source * inv_first * attn_gain).astype(jnp.bfloat16)
    query_pre = jnp.dot(normed, query_weight, preferred_element_type=jnp.float32)
    key_pre = jnp.dot(normed, key_weight, preferred_element_type=jnp.float32)
    value_pre = jnp.dot(normed, value_weight, preferred_element_type=jnp.float32)
    queries = rotate(query_pre.reshape(shape3), cosine, sine).astype(jnp.bfloat16)
    keys = rotate(key_pre.reshape(shape3), cosine, sine).astype(jnp.bfloat16).reshape(rows, width)
    mixed = (MIX * value_pre + MIX * first_values.astype(jnp.float32)).astype(jnp.bfloat16)
    keys_local = keys.reshape(shape3)
    mixed_local = mixed.reshape(shape3)

    def allowed_mask(query_index, query_doc, key_index, key_doc):
        return (query_doc[:, None] == key_doc[None, :]) & (
            key_index[None, :] <= query_index[:, None]
        )

    def forward_step(state, pieces, start):
        count = pieces[0].shape[0]
        keys_piece = pieces[0].reshape(count, heads, HEAD_DIM)
        values_piece = pieces[1].reshape(count, heads, HEAD_DIM)
        key_index = start + jnp.arange(count, dtype=jnp.int32)

        def forward_compute(state):
            high, total, accum = state
            key_doc, unused = doc_layout(doc_lengths, key_index)
            allowed = allowed_mask(my_index, my_doc, key_index, key_doc)[None]
            score = (
                jnp.einsum("qhd,khd->hqk", queries, keys_piece, preferred_element_type=jnp.float32)
                * scale
            )
            score = jnp.where(allowed, score, NEG)
            new_high = jnp.maximum(high, jnp.max(score, axis=-1))
            weight = jnp.where(allowed, jnp.exp(score - new_high[:, :, None]), 0.0)
            factor = jnp.exp(high - new_high)
            total = total * factor + jnp.sum(weight, axis=-1)
            accum = accum * factor.T[:, :, None] + jnp.einsum(
                "hqk,khd->qhd",
                weight.astype(jnp.bfloat16),
                values_piece,
                preferred_element_type=jnp.float32,
            )
            return (new_high, total, accum)

        return lax.cond(start <= my_index[-1], forward_compute, lambda kept: kept, state)

    def query_grad_step(grad_q, pieces, start):
        count = pieces[0].shape[0]
        keys_piece = pieces[0].reshape(count, heads, HEAD_DIM)
        values_piece = pieces[1].reshape(count, heads, HEAD_DIM)
        key_index = start + jnp.arange(count, dtype=jnp.int32)

        def query_compute(grad_q):
            key_doc, unused = doc_layout(doc_lengths, key_index)
            allowed = allowed_mask(my_index, my_doc, key_index, key_doc)[None]
            score = (
                jnp.einsum("qhd,khd->hqk", queries, keys_piece, preferred_element_type=jnp.float32)
                * scale
            )
            prob = jnp.where(allowed, jnp.exp(score - logsum[:, :, None]), 0.0)
            prob_grad = jnp.einsum(
                "qhd,khd->hqk", outgrad_local, values_piece, preferred_element_type=jnp.float32
            )
            score_grad = (prob * (prob_grad - delta[:, :, None])).astype(jnp.bfloat16)
            return (
                grad_q
                + jnp.einsum(
                    "hqk,khd->qhd", score_grad, keys_piece, preferred_element_type=jnp.float32
                )
                * scale
            )

        return lax.cond(start <= my_index[-1], query_compute, lambda kept: kept, grad_q)

    init = (
        jnp.full((heads, rows), NEG, jnp.float32),
        jnp.zeros((heads, rows), jnp.float32),
        jnp.zeros(shape3, jnp.float32),
    )
    state = by_blocks(
        forward_step,
        init,
        (
            lax.all_gather(keys, "blk", axis=0, tiled=True),
            lax.all_gather(mixed, "blk", axis=0, tiled=True),
        ),
        jnp.int32(0),
    )
    high, total, accum = state
    logsum = high + jnp.log(total)
    attended = accum / total.T[:, :, None]
    attended_b = attended.astype(jnp.bfloat16).reshape(rows, width)
    mid = source + jnp.dot(attended_b, out_weight, preferred_element_type=jnp.float32)
    inv_second = lax.rsqrt(jnp.mean(mid * mid, axis=-1, keepdims=True) + EPS)
    normed_two = (mid * inv_second * ffn_gain).astype(jnp.bfloat16)
    gate = jnp.dot(normed_two, gate_weight, preferred_element_type=jnp.float32)
    up = jnp.dot(normed_two, up_weight, preferred_element_type=jnp.float32)
    act = (jax.nn.silu(gate) * up).astype(jnp.bfloat16)
    layer_output = mid + jnp.dot(act, down_weight, preferred_element_type=jnp.float32)
    cot_float = cotangent.astype(jnp.float32)
    grad_down = outer(act, cotangent)
    act_grad = back(cotangent, down_weight)
    sigma = jax.nn.sigmoid(gate)
    gate_grad = (act_grad * up * sigma * (1.0 + gate * (1.0 - sigma))).astype(jnp.bfloat16)
    up_grad = (act_grad * gate * sigma).astype(jnp.bfloat16)
    grad_gate = outer(normed_two, gate_grad)
    grad_up = outer(normed_two, up_grad)
    normed_two_grad = back(gate_grad, gate_weight) + back(up_grad, up_weight)
    grad_ffn_gain = jnp.sum(normed_two_grad * mid * inv_second, axis=0)
    scaled_two = normed_two_grad * ffn_gain
    mid_grad = (
        cot_float
        + inv_second * scaled_two
        - mid * inv_second**3 * jnp.mean(scaled_two * mid, axis=-1, keepdims=True)
    )
    mid_grad_b = mid_grad.astype(jnp.bfloat16)
    grad_out_weight = outer(attended_b, mid_grad_b)
    attended_grad = back(mid_grad_b, out_weight).astype(jnp.bfloat16)
    outgrad_local = attended_grad.reshape(shape3)
    delta = jnp.sum(outgrad_local.astype(jnp.float32) * attended, axis=-1).T
    zeros3 = jnp.zeros(shape3, jnp.float32)
    grad_q = by_blocks(
        query_grad_step,
        zeros3,
        (
            lax.all_gather(keys, "blk", axis=0, tiled=True),
            lax.all_gather(mixed, "blk", axis=0, tiled=True),
        ),
        jnp.int32(0),
    )
    all_logsum, all_delta = (
        lax.all_gather(logsum.T, "blk", axis=0, tiled=True),
        lax.all_gather(delta.T, "blk", axis=0, tiled=True),
    )

    def key_grad_step(state, pieces, start):
        count = pieces[0].shape[0]
        query_piece = pieces[0].reshape(count, heads, HEAD_DIM)
        outgrad_piece = pieces[1].reshape(count, heads, HEAD_DIM)
        query_index = start + jnp.arange(count, dtype=jnp.int32)

        def key_compute(state):
            grad_k, grad_v = state
            logsum_piece = lax.dynamic_slice_in_dim(all_logsum, start, count, 0).T
            delta_piece = lax.dynamic_slice_in_dim(all_delta, start, count, 0).T
            query_doc, unused = doc_layout(doc_lengths, query_index)
            allowed = allowed_mask(query_index, query_doc, my_index, my_doc)[None]
            score = (
                jnp.einsum(
                    "qhd,khd->hqk", query_piece, keys_local, preferred_element_type=jnp.float32
                )
                * scale
            )
            prob = jnp.where(allowed, jnp.exp(score - logsum_piece[:, :, None]), 0.0)
            grad_v = grad_v + jnp.einsum(
                "hqk,qhd->khd",
                prob.astype(jnp.bfloat16),
                outgrad_piece,
                preferred_element_type=jnp.float32,
            )
            prob_grad = jnp.einsum(
                "qhd,khd->hqk", outgrad_piece, mixed_local, preferred_element_type=jnp.float32
            )
            score_grad = (prob * (prob_grad - delta_piece[:, :, None])).astype(jnp.bfloat16)
            grad_k = (
                grad_k
                + jnp.einsum(
                    "hqk,qhd->khd", score_grad, query_piece, preferred_element_type=jnp.float32
                )
                * scale
            )
            return (grad_k, grad_v)

        return lax.cond(query_index[-1] >= my_start, key_compute, lambda kept: kept, state)

    grad_k, grad_v = by_blocks(
        key_grad_step,
        (zeros3, zeros3),
        (
            lax.all_gather(queries.reshape(rows, width), "blk", axis=0, tiled=True),
            lax.all_gather(attended_grad, "blk", axis=0, tiled=True),
        ),
        jnp.int32(0),
    )
    queries_grad = grad_q.astype(jnp.bfloat16)
    keys_grad = grad_k.astype(jnp.bfloat16)
    mixed_grad = grad_v.astype(jnp.bfloat16).reshape(rows, width)
    q_pre_grad = (
        rotate(queries_grad.astype(jnp.float32), cosine, -sine)
        .astype(jnp.bfloat16)
        .reshape(rows, width)
    )
    k_pre_grad = (
        rotate(keys_grad.astype(jnp.float32), cosine, -sine)
        .astype(jnp.bfloat16)
        .reshape(rows, width)
    )
    grad_first = MIX * mixed_grad.astype(jnp.float32)
    value_grad = grad_first.astype(jnp.bfloat16)
    grad_query = outer(normed, q_pre_grad)
    grad_key = outer(normed, k_pre_grad)
    grad_value = outer(normed, value_grad)
    normed_grad = (
        back(q_pre_grad, query_weight)
        + back(k_pre_grad, key_weight)
        + back(value_grad, value_weight)
    )
    grad_attn_gain = jnp.sum(normed_grad * source * inv_first, axis=0)
    scaled_one = normed_grad * attn_gain
    grad_tokens = (
        mid_grad
        + inv_first * scaled_one
        - source * inv_first**3 * jnp.mean(scaled_one * source, axis=-1, keepdims=True)
    )
    summed = (
        lax.psum_scatter(grad_attn_gain, "blk", scatter_dimension=0, tiled=True),
        lax.psum_scatter(grad_query, "blk", scatter_dimension=0, tiled=True),
        lax.psum_scatter(grad_key, "blk", scatter_dimension=0, tiled=True),
        lax.psum_scatter(grad_value, "blk", scatter_dimension=0, tiled=True),
        lax.psum_scatter(grad_out_weight, "blk", scatter_dimension=0, tiled=True),
        lax.psum_scatter(grad_ffn_gain, "blk", scatter_dimension=0, tiled=True),
        lax.psum_scatter(grad_gate, "blk", scatter_dimension=0, tiled=True),
        lax.psum_scatter(grad_up, "blk", scatter_dimension=0, tiled=True),
        lax.psum_scatter(grad_down, "blk", scatter_dimension=0, tiled=True),
    )
    summed = (
        lax.psum(summed[0].astype(jnp.bfloat16), "seq").astype(jnp.float32),
        lax.psum(summed[1].astype(jnp.bfloat16), "seq").astype(jnp.float32),
        lax.psum(summed[2].astype(jnp.bfloat16), "seq").astype(jnp.float32),
        lax.psum(summed[3].astype(jnp.bfloat16), "seq").astype(jnp.float32),
        lax.psum(summed[4].astype(jnp.bfloat16), "seq").astype(jnp.float32),
        lax.psum(summed[5].astype(jnp.bfloat16), "seq").astype(jnp.float32),
        lax.psum(summed[6].astype(jnp.bfloat16), "seq").astype(jnp.float32),
        lax.psum(summed[7].astype(jnp.bfloat16), "seq").astype(jnp.float32),
        lax.psum(summed[8].astype(jnp.bfloat16), "seq").astype(jnp.float32),
    )
    return (
        layer_output,
        grad_tokens,
        grad_first,
        summed[0],
        summed[1],
        summed[2],
        summed[3],
        summed[4],
        summed[5],
        summed[6],
        summed[7],
        summed[8],
    )


def solution(mesh):
    return jax.shard_map(
        local,
        mesh=mesh,
        in_specs=(
            P(("seq", "blk"), None),
            P(("seq", "blk"), None),
            P("seq", None),
            P(),
            P(),
            P(),
            P(),
            P(),
            P(),
            P(),
            P(),
            P(),
            P(("seq", "blk"), None),
        ),
        out_specs=(
            P(("seq", "blk"), None),
            P(("seq", "blk"), None),
            P(("seq", "blk"), None),
            P("blk"),
            P("blk", None),
            P("blk", None),
            P("blk", None),
            P("blk", None),
            P("blk"),
            P("blk", None),
            P("blk", None),
            P("blk", None),
        ),
        check_vma=False,
    )
```

profile of v0, /device:TPU:8, one launch (start us, length us, event | category | flops | bytes accessed | tf_op | source)
XLA Modules:
  0.0 821.1 jit_solution(9121658077916730343)
XLA Ops:
  21.4 20.3 %all-gather.7.cloned.1.call-done = bf16[1024,1024]{1,0:T(8,128)(2,1)} async-done(((bf16[128,1024]{1,0:T(8,128)(2,1)}), bf16[1024,1024]{1,0:T(8,128)(2,1)}) %all-gather.7.cloned.1.call-update) | async-done | bytes 2097168 | tf_op jit(solution)/shard_map/all_gather | solution.py:174
  41.7 4.0 copy.54
  45.6 30.4 %all-gather.5.cloned.1.call-done = bf16[1024,1024]{0,1:T(8,128)(2,1)} async-done(((bf16[128,1024]{0,1:T(8,128)(2,1)}), bf16[1024,1024]{0,1:T(8,128)(2,1)}) %all-gather.5.cloned.1.call-update) | async-done | bytes 2097168 | tf_op jit(solution)/shard_map/all_gather | solution.py:173
  76.1 11.9 %conditional.3 = (f32[16,128]{1,0:T(8,128)}, f32[16,128]{1,0:T(8,128)S(1)}, f32[128,16,64]{0,2,1:T(8,128)S(1)}, f32[16,128]{1,0:T(8,128)S(1)}) conditional(s32[]{:T(128)} %bitcast.17, () %tuple.34, (s32[128]{0:T(128)S(1)}, s32[1024]{0:T(1024)S(1)}, s32[1,4]{1,0:T(1,128)S(1)}, s32[1024]{0:T(1024)S(1)}, s32[128]{0:T(128)S(1)}, ...), branch_computations={%region_4.5_spmd, %region_5.10_spmd} | conditional | flops 564677632 | bytes 39175280 | solution.py:134
  76.5 3.3 fusion
  83.6 3.2 fusion.2
  91.2 3.7 fusion.80
  97.3 3.3 multiply_convert_fusion.12
  107.4 3.9 fusion.59
  116.3 16.1 %conditional.4 = (bf16[128,16,64]{0,2,1:T(8,128)(2,1)S(1)}) conditional(s32[]{:T(128)} %bitcast.17, () %tuple.36, (s32[128]{0:T(128)S(1)}, s32[1024]{0:T(1024)S(1)}, s32[1,4]{1,0:T(1,128)S(1)}, s32[1024]{0:T(1024)S(1)}, s32[128]{0:T(128)S(1)}, /*index=5*/bf16[128,16,64]{0,2,1:T(8,128)(2,1)S(1)}, bf16[1024,16,64]{0,2,1:T(8,128)(2,1)}, ...), branch_computations={%region_13.14_spmd, %region_14.17_spmd} | conditional | flops 818555904 | bytes 24151100 | solution.py:162
  117.6 6.1 fusion.77
  123.7 8.7 %fusion.22 = bf16[128,16,64]{0,2,1:T(8,128)(2,1)S(1)} fusion(bf16[1024,16,64]{0,2,1:T(8,128)(2,1)} %get-tuple-element.79, f32[16,128,1024]{2,1,0:T(8,128)} %fusion.77, f32[16,128]{1,0:T(8,128)S(1)} %get-tuple-element.83, f32[16,128]{1,0:T(8,128)S(1)} %get-tuple-element.80, pred[128,1024]{1,0:T(8,128)(4,1)} %compare_and_fusion.1, ...), kind=kOutput, calls=%fused_computation.23 | convolution fusion | flops 549715968 | bytes 13254656 | tf_op jit(solution)/shard_map/cond/branch_1_fun/hqk,khd->qhd/dot_general | solution.py:156
  133.3 12.2 %all_gather.25 = f32[1024,16]{0,1:T(8,128)S(1)} all-gather(f32[128,16]{0,1:T(8,128)S(1)} %multiply_reduce_fusion.1), channel_id=1, replica_groups=mesh['seq'=4,'blk'=8] {'blk'}, dimensions={0}, use_global_device_ids=true | all-gather | bytes 73728 | tf_op jit(solution)/shard_map/all_gather | solution.py:222
  145.5 15.6 %all_gather.23 = f32[1024,16]{0,1:T(8,128)} all-gather(f32[128,16]{0,1:T(8,128)S(1)} %bitcast.123), channel_id=1, replica_groups=mesh['seq'=4,'blk'=8] {'blk'}, dimensions={0}, use_global_device_ids=true | all-gather | bytes 73728 | tf_op jit(solution)/shard_map/all_gather | solution.py:221
  161.0 33.0 %conditional.5 = (bf16[128,16,64]{0,2,1:T(8,128)(2,1)}, f32[128,1024]{1,0:T(8,128)}) conditional(s32[]{:T(128)} %convert_element_type.223, () %tuple.38, (s32[1024]{0:T(1024)S(1)}, s32[1,4]{1,0:T(1,128)S(1)}, s32[128]{0:T(128)S(1)}, s32[128]{0:T(128)S(1)}, s32[1024]{0:T(1024)S(1)}, /*index=5*/bf16[1024,1024]{0,1:T(8,128)(2,1)}, ...), branch_computations={%region_17.18_spmd, %region_18.21_spmd} | conditional | flops 1095642112 | bytes 43074712 | solution.py:263
  164.3 4.0 copy.56
  168.3 6.2 fusion.78
  174.5 11.3 %fusion.34 = bf16[128,16,64]{0,2,1:T(8,128)(2,1)} fusion(bf16[1024,16,64]{0,2,1:T(8,128)(2,1)} %bitcast.113, f32[16,1024,128]{2,1,0:T(8,128)} %fusion.78, f32[16,1024]{1,0:T(8,128)S(1)} %bitcast.119, f32[16,1024]{1,0:T(8,128)} %bitcast.120, pred[1024,128]{1,0:T(8,128)(4,1)} %compare_and_fusion.2, bf16[1024,16,64]{0,2,1:T(8,128)(2,1)} %bitcast.110, ...), kind=kOutput, calls=%fused_computation.37 | convolution fusion | flops 549715968 | bytes 13369344 | tf_op jit(solution)/shard_map/cond/branch_1_fun/hqk,qhd->khd/dot_general | solution.py:256
  185.8 6.2 fusion.38
  207.5 7.0 fusion.85
  214.9 7.0 fusion.84
  222.0 7.1 fusion.83
  231.0 14.2 %reduce-scatter.10.cloned.1.call-done = f32[128,1024]{1,0:T(8,128)} async-done(((f32[1024,1024]{1,0:T(8,128)}), f32[128,1024]{1,0:T(8,128)}) %reduce-scatter.10.cloned.1.call-update) | async-done | bytes 524304 | tf_op jit(solution)/shard_map/reduce_scatter | solution.py:307
  247.0 48.7 %reduce-scatter.8.cloned.1.call-done = f32[128,1024]{1,0:T(8,128)} async-done(((f32[1024,1024]{1,0:T(8,128)}), f32[128,1024]{1,0:T(8,128)}) %reduce-scatter.8.cloned.1.call-update) | async-done | bytes 524304 | tf_op jit(solution)/shard_map/reduce_scatter | solution.py:306
  297.5 48.7 %reduce-scatter.12.cloned.1.call-done = f32[128,1024]{1,0:T(8,128)} async-done(((f32[1024,1024]{1,0:T(8,128)}), f32[128,1024]{1,0:T(8,128)}) %reduce-scatter.12.cloned.1.call-update) | async-done | bytes 524304 | tf_op jit(solution)/shard_map/reduce_scatter | solution.py:308
  347.9 119.0 %reduce-scatter.20.cloned.1.call-done = f32[352,1024]{1,0:T(8,128)} async-done(((f32[2816,1024]{1,0:T(8,128)}), f32[352,1024]{1,0:T(8,128)}) %reduce-scatter.20.cloned.1.call-update) | async-done | bytes 1441808 | tf_op jit(solution)/shard_map/reduce_scatter | solution.py:313
  469.2 117.5 %reduce-scatter.18.cloned.1.call-done = f32[128,2816]{1,0:T(8,128)} async-done(((f32[1024,2816]{1,0:T(8,128)}), f32[128,2816]{1,0:T(8,128)}) %reduce-scatter.18.cloned.1.call-update) | async-done | bytes 1441808 | tf_op jit(solution)/shard_map/reduce_scatter | solution.py:312
  589.0 117.7 %reduce-scatter.16.cloned.1.call-done = f32[128,2816]{1,0:T(8,128)} async-done(((f32[1024,2816]{1,0:T(8,128)}), f32[128,2816]{1,0:T(8,128)}) %reduce-scatter.16.cloned.1.call-update) | async-done | bytes 1441808 | tf_op jit(solution)/shard_map/reduce_scatter | solution.py:311
  710.4 4.7 convolution_add_fusion.5
  719.5 13.3 %all-reduce.2 = (bf16[1024]{0:T(1024)(128)(2,1)S(1)}, bf16[1024]{0:T(1024)(128)(2,1)S(1)}) all-reduce(f32[1024]{0:T(1024)S(1)} %get-tuple-element.196, f32[1024]{0:T(1024)S(1)} %get-tuple-element.194), channel_id=2, replica_groups=mesh['seq'=4,'blk'=8] {'blk'}, use_global_device_ids=true, to_apply=%region_23.24.clone | all-reduce | flops 2048 | bytes 12288
  733.0 9.8 %all-reduce.3 = (bf16[128]{0:T(256)(128)(2,1)S(1)}, bf16[128]{0:T(256)(128)(2,1)S(1)}) all-reduce(bf16[128]{0:T(256)(128)(2,1)S(1)} %dynamic-slice.7, bf16[128]{0:T(256)(128)(2,1)S(1)} %dynamic-slice.6), channel_id=1, replica_groups=mesh['seq'=4,'blk'=8] {'seq'}, use_global_device_ids=true, to_apply=%region_24.25 | all-reduce | flops 256 | bytes 1024 | tf_op jit(solution)/shard_map/psum | solution.py:316
  745.9 56.1 %all-reduce.7.cloned.1.call-done = (bf16[128,1024]{1,0:T(8,128)(2,1)}, bf16[128,1024]{1,0:T(8,128)(2,1)}, bf16[128,1024]{1,0:T(8,128)(2,1)}, bf16[128,1024]{1,0:...) async-done(((bf16[128,1024]{1,0:T(8,128)(2,1)}, bf16[128,1024]{1,0:T(8,128)(2,1)}, bf16[128,1024]{1,0:T(8,128)(2,1)}, ...) | async-done | bytes 3211280 | tf_op jit(solution)/shard_map/psum | solution.py:317
  (181 shorter events, 90.0 us)
Async XLA Ops:
  7.2 8.6 %copy-start.1 = (bf16[128,1024]{1,0:T(8,128)(2,1)S(1)}, bf16[128,1024]{1,0:T(8,128)(2,1)}, u32[]{:S(2)}) copy-start(bf16[128,1024]{1,0:T(8,128)(2,1)} %param.19) | copy-start | bytes 786436
  7.2 8.6 %copy-start.23 = (f32[1024]{0:T(1024)S(1)}, f32[1024]{0:T(1024)}, u32[]{:S(2)}) copy-start(f32[1024]{0:T(1024)} %param.22) | copy-start | bytes 12292
  7.2 34.5 %all-gather.7.cloned.1.call-start = ((), (), s32[]{:S(2)}) async-start(), calls=%async_computation.8 | async-start | bytes 2359296 | tf_op jit(solution)/shard_map/all_gather | solution.py:174
  11.3 64.8 %all-gather.5.cloned.1.call-start = ((), (), s32[]{:S(2)}) async-start(), calls=%async_computation.7 | async-start | bytes 2359296 | tf_op jit(solution)/shard_map/all_gather | solution.py:173
  18.4 57.7 %copy-start.27 = (s32[1,4]{1,0:T(1,128)S(1)}, s32[1,4]{1,0:T(1,128)}, u32[]{:S(2)}) copy-start(s32[1,4]{1,0:T(1,128)} %param.21) | copy-start | bytes 52
  19.3 141.7 %all-gather.9.cloned.1.call-start = ((), (), s32[]{:S(2)}) async-start(), calls=%async_computation.9 | async-start | bytes 2359296 | tf_op jit(solution)/shard_map/all_gather | solution.py:269
  20.1 56.0 %copy-start.10 = (bf16[128,16,64]{0,2,1:T(8,128)(2,1)S(1)}, bf16[128,16,64]{0,2,1:T(8,128)(2,1)}, u32[]{:S(2)}) copy-start(bf16[128,16,64]{0,2,1:T(8,128)(2,1)} %maximum_convert_fusion) | copy-start | bytes 786436
  20.1 140.9 %all-gather.11.cloned.1.call-start = ((), (), s32[]{:S(2)}) async-start(), calls=%async_computation.10 | async-start | bytes 2359296 | tf_op jit(solution)/shard_map/all_gather | solution.py:270
  76.1 15.0 %copy-start.26 = (f32[1024]{0:T(1024)S(1)}, f32[1024]{0:T(1024)}, u32[]{:S(2)}) copy-start(f32[1024]{0:T(1024)} %param.27) | copy-start | bytes 12292
  91.2 4.3 slice-start.1
  91.2 5.5 slice-start.4
  95.5 7.1 slice-start.2
  97.3 5.3 slice-start.3
  107.3 121.9 %reduce-scatter.14.cloned.1.call-start = ((), (), s32[]{:S(2)}) async-start(), calls=%async_computation.14 | async-start | bytes 4718592 | tf_op jit(solution)/shard_map/reduce_scatter | solution.py:309
  111.3 133.9 %reduce-scatter.10.cloned.1.call-start = ((), (), s32[]{:S(2)}) async-start(), calls=%async_computation.12 | async-start | bytes 4718592 | tf_op jit(solution)/shard_map/reduce_scatter | solution.py:307
  161.2 7.0 copy-start.17
  174.5 11.3 %copy-start.24 = (pred[1024,128]{1,0:T(8,128)(4,1)S(1)}, pred[1024,128]{1,0:T(8,128)(4,1)}, u32[]{:S(2)}) copy-start(pred[1024,128]{1,0:T(8,128)(4,1)} %compare_and_fusion.2) | copy-start | bytes 393220 | tf_op jit(solution)/shard_map/cond
  174.5 11.3 %copy-start.25 = (f32[1024,16]{0,1:T(8,128)S(1)}, f32[1024,16]{0,1:T(8,128)}, u32[]{:S(2)}) copy-start(f32[1024,16]{0,1:T(8,128)} %get-tuple-element.91) | copy-start | bytes 196612 | tf_op jit(solution)/shard_map/cond
  199.7 95.9 %reduce-scatter.8.cloned.1.call-start = ((), (), s32[]{:S(2)}) async-start(), calls=%async_computation.11 | async-start | bytes 4718592 | tf_op jit(solution)/shard_map/reduce_scatter | solution.py:306
  202.7 143.4 %reduce-scatter.12.cloned.1.call-start = ((), (), s32[]{:S(2)}) async-start(), calls=%async_computation.13 | async-start | bytes 4718592 | tf_op jit(solution)/shard_map/reduce_scatter | solution.py:308
  207.5 259.4 %reduce-scatter.20.cloned.1.call-start = ((), (), s32[]{:S(2)}) async-start(), calls=%async_computation.17 | async-start | bytes 12976128 | tf_op jit(solution)/shard_map/reduce_scatter | solution.py:313
  214.6 372.1 %reduce-scatter.18.cloned.1.call-start = ((), (), s32[]{:S(2)}) async-start(), calls=%async_computation.16 | async-start | bytes 12976128 | tf_op jit(solution)/shard_map/reduce_scatter | solution.py:312
  221.9 484.8 %reduce-scatter.16.cloned.1.call-start = ((), (), s32[]{:S(2)}) async-start(), calls=%async_computation.15 | async-start | bytes 12976128 | tf_op jit(solution)/shard_map/reduce_scatter | solution.py:311
  229.1 572.8 %all-reduce.7.cloned.1.call-start = ((), (), s32[]{:S(2)}) async-start(), calls=%async_computation.18 | async-start | bytes 6422528 | tf_op jit(solution)/shard_map/psum | solution.py:317
  469.2 239.8 %copy-start.29 = (u32[32]{0:T(128)S(1)}, u32[32]{0:T(128)}, u32[]{:S(2)}) copy-start(u32[32]{0:T(128)} %constant.83) | copy-start | bytes 388
  710.3 4.8 copy-start.3
  710.3 6.6 copy-start.4
  710.3 6.6 copy-start.15
  717.0 26.9 %copy-start.6 = (f32[128,1024]{1,0:T(8,128)S(1)}, f32[128,1024]{1,0:T(8,128)}, u32[]{:S(2)}) copy-start(f32[128,1024]{1,0:T(8,128)} %copy-done.5) | copy-start | bytes 1572868
  717.0 26.9 %copy-start.28 = (f32[128]{0:T(128)S(1)}, f32[128]{0:T(128)}, u32[]{:S(2)}) copy-start(f32[128]{0:T(128)} %get-tuple-element.235) | copy-start | bytes 1540
  802.0 9.6 %copy-start.22 = (bf16[128,2816]{1,0:T(8,128)(2,1)S(1)}, bf16[128,2816]{1,0:T(8,128)(2,1)}, u32[]{:S(2)}) copy-start(bf16[128,2816]{1,0:T(8,128)(2,1)} %get-tuple-element.209) | copy-start | bytes 2162692
  802.0 10.8 %copy-start.21 = (bf16[352,1024]{1,0:T(8,128)(2,1)S(1)}, bf16[352,1024]{1,0:T(8,128)(2,1)}, u32[]{:S(2)}) copy-start(bf16[352,1024]{1,0:T(8,128)(2,1)} %get-tuple-element.210) | copy-start | bytes 2162692
  (16 other events, 39.2 us)
Sparse Core Ops, SparseCore 0:
  11.4 30.2 all-gather.6
  43.9 32.1 all-gather.4
  78.2 29.8 all-gather.8
  110.2 26.3 all-gather.10
  138.7 46.2 reduce-scatter.13
  199.9 45.2 reduce-scatter.9
  247.5 48.1 reduce-scatter.7
  298.0 48.1 reduce-scatter.11
  348.4 118.3 reduce-scatter.19
  469.0 117.6 reduce-scatter.17
  589.0 117.6 reduce-scatter.15
  711.1 90.8 all-reduce.6
where the time goes:
time: 831 us; the launch traced here: 821 us
  waiting for transfers between devices  573 us (69%)
  matrix products  111 us (13%)
  blocking collectives  50.8 us (6%)
  other arithmetic  48 us (6%)
  local copies, waits for them, and re-layouts  20 us (2%)
  between operations  16.9 us (2%)
    reduce_scatter x1, waiting for transfers between devices, local(): lax.psum_scatter(grad_down, 'blk', scatter_dimension=0, tiled=True)  119 us
    reduce_scatter x1, waiting for transfers between devices, local(): lax.psum_scatter(grad_gate, 'blk', scatter_dimension=0, tiled=True)  118 us
    reduce_scatter x1, waiting for transfers between devices, local(): lax.psum_scatter(grad_up, 'blk', scatter_dimension=0, tiled=True)  117 us
    psum x1, waiting for transfers between devices, local(): lax.psum(summed[1].astype(jnp.bfloat16), 'seq').astype(jnp.float32)  56.1 us
    reduce_scatter x1, waiting for transfers between devices, local(): lax.psum_scatter(grad_value, 'blk', scatter_dimension=0, tiled=True)  48.7 us
    reduce_scatter x1, waiting for transfers between devices, local(): lax.psum_scatter(grad_query, 'blk', scatter_dimension=0, tiled=True)  48.7 us
    dot_general x7, matrix products, outer(): lax.dot_general(left, right, (((0,), (0,)), ((), ())), preferred_element_...  33.5 us
    all_gather x1, waiting for transfers between devices, local(): lax.all_gather(keys, 'blk', axis=0, tiled=True)  30.4 us
  transfers between devices with their start and end apart: 12, of which 9 were waited for; matrix products, arithmetic and copies ran while one was open for 19% of the time, Pallas kernels for 0%

commit v1 on v0

--- a/solution.py
+++ b/solution.py
@@ -1,8 +1,11 @@
+import functools
 import math
 
 import jax
 import jax.numpy as jnp
 from jax import lax
+from jax.experimental import pallas as pl
+from jax.experimental.pallas import tpu as pltpu
 from jax.sharding import PartitionSpec as P
 
 HEAD_DIM = 64
@@ -61,6 +64,425 @@
 def back(left, weight):
     return lax.dot_general(
         left, weight, (((1,), (1,)), ((), ())), preferred_element_type=jnp.float32
+    )
+
+
+TILE = 256
+MESH = pl.DeviceIdType.MESH
+F32 = jnp.float32
+BF16 = jnp.bfloat16
+
+
+def remote(src, dst, send, recv, where):
+    return pltpu.make_async_remote_copy(
+        src_ref=src, dst_ref=dst, send_sem=send, recv_sem=recv, device_id=where, device_id_type=MESH
+    )
+
+
+def multiple(value, unit):
+    return pl.multiple_of(value, unit)
+
+
+class Reducer:
+    def __init__(self, rows, ff, n_seq, n_blk):
+        self.rows, self.ff, self.n_seq, self.n_blk = rows, ff, n_seq, n_blk
+        self.seq = lax.axis_index("seq")
+        self.blk = lax.axis_index("blk")
+        self.core = lax.rem(self.blk, 2)
+        self.chip = lax.div(self.blk, 2)
+        self.chips = n_blk // 2
+
+    def give(self, owner, kind, src, dst, send, recv):
+        here = dst.at[pl.ds(multiple(self.seq * self.rows, self.rows), self.rows)]
+
+        @pl.when(self.seq != owner)
+        def _():
+            remote(src, here, send.at[kind, owner], recv.at[kind, self.seq], {"seq": owner}).start()
+
+        @pl.when(self.seq == owner)
+        def _():
+            pltpu.make_async_copy(src, here, recv.at[kind, self.seq]).start()
+
+    def given(self, owner, kind, src, dst, send, recv):
+        for other in range(self.n_seq):
+            there = dst.at[pl.ds(other * self.rows, self.rows)]
+            if other == owner:
+                pltpu.make_async_copy(src, there, recv.at[kind, other]).wait()
+            else:
+                remote(src, there, send.at[kind, other], recv.at[kind, other], {"seq": other}).wait_recv()
+
+    def sent(self, owner, kind, src, dst, send, recv):
+        here = dst.at[pl.ds(multiple(self.seq * self.rows, self.rows), self.rows)]
+
+        @pl.when(self.seq != owner)
+        def _():
+            remote(src, here, send.at[kind, owner], recv.at[kind, self.seq], {"seq": owner}).wait_send()
+
+    def turned(self, step):
+        return lax.rem(self.chip + step, self.chips)
+
+    def swap(self, part, size, chip, got, send, recv):
+        src = part.at[pl.ds(multiple((2 * chip + 1 - self.core) * size, 32), size)]
+        dst = got.at[pl.ds(multiple(chip * size, 32), size)]
+        return remote(src, dst, send.at[chip], recv.at[chip], {"blk": 2 * self.chip + 1 - self.core})
+
+    def forward(self, part, size, step, got, send, recv):
+        chip = self.turned(step)
+        src = part.at[pl.ds(multiple((2 * chip + self.core) * size, 32), size)]
+        dst = got.at[pl.ds(multiple((step - 1) * size, 32), size)]
+        return remote(src, dst, send.at[step - 1], recv.at[step - 1], {"blk": 2 * chip + self.core})
+
+    def reduce_begin(self, part, size, cgot, zgot, sems):
+        csend, crecv, zsend, zrecv = sems
+
+        def one(step, unused):
+            chip = self.turned(step)
+            self.swap(part, size, chip, cgot, csend, crecv).wait()
+            mine = (2 * chip + self.core) * size
+
+            def add(group, unused):
+                at = pl.ds(multiple(mine + group * 32, 32), 32)
+                other = pl.ds(multiple(chip * size + group * 32, 32), 32)
+                part[at, :] = (part[at, :].astype(F32) + cgot[other, :].astype(F32)).astype(BF16)
+                return unused
+
+            lax.fori_loop(0, size // 32, add, 0)
+            self.forward(part, size, step, zgot, zsend, zrecv).start()
+            return unused
+
+        lax.fori_loop(1, self.chips, one, 0)
+        self.swap(part, size, self.chip, cgot, csend, crecv).wait()
+
+    def reduce_end(self, part, size, cgot, zgot, total, sems):
+        csend, crecv, zsend, zrecv = sems
+
+        def arrived(step, unused):
+            self.forward(part, size, step, zgot, zsend, zrecv).wait()
+            return unused
+
+        lax.fori_loop(1, self.chips, arrived, 0)
+        mine = self.blk * size
+
+        def add(group, unused):
+            at = pl.ds(multiple(mine + group * 32, 32), 32)
+            other = pl.ds(multiple(self.chip * size + group * 32, 32), 32)
+            value = part[at, :].astype(F32) + cgot[other, :].astype(F32)
+            for step in range(1, self.chips):
+                there = pl.ds(multiple((step - 1) * size + group * 32, 32), 32)
+                value = value + zgot[there, :].astype(F32)
+            total[pl.ds(multiple(group * 32, 32), 32), :] = value.astype(BF16)
+            return unused
+
+        lax.fori_loop(0, size // 32, add, 0)
+
+    def spread(self, owner_static, src, dst, kind, send, recv, local):
+        for other in range(self.n_seq):
+            if other != owner_static:
+                remote(src, dst, send.at[kind, other], recv.at[kind], {"seq": other}).start()
+        pltpu.make_async_copy(src, dst, local.at[kind]).start()
+
+    def spread_wait(self, owner, src, dst, kind, send, recv, local):
+        @pl.when(self.seq == owner)
+        def _():
+            for other in range(self.n_seq):
+                if other != owner:
+                    remote(src, dst, send.at[kind, other], recv.at[kind], {"seq": other}).wait_send()
+            pltpu.make_async_copy(src, dst, local.at[kind]).wait()
+
+        @pl.when(self.seq != owner)
+        def _():
+            remote(src, dst, send.at[kind, owner], recv.at[kind], {"seq": owner}).wait_recv()
+
+
+def outer_tiles(lhs, rhs, part, turned, chip, tiles, part_at):
+    turned[...] = lhs[:, pl.ds(multiple(chip * TILE, TILE), TILE)].T
+
+    def tile(index, unused):
+        value = jnp.dot(turned[...], rhs[:, pl.ds(multiple(index * TILE, TILE), TILE)], preferred_element_type=F32)
+        part[pl.ds(multiple(chip * TILE, TILE), TILE), pl.ds(multiple(part_at + index * TILE, TILE), TILE)] = (
+            value.astype(BF16)
+        )
+        return unused
+
+    lax.fori_loop(0, tiles, tile, 0)
+
+
+def grad_kernel(
+    sizes,
+    normed, q_grad, k_grad, v_grad, att, mid, two, gate_up, act, cot, gains,
+    out_gu, out_down, out_out, out_query, out_key, out_value, out_gain,
+    buf_a, buf_b, buf_att, buf_mid, buf_n, buf_t,
+    turned, part, part_down, part_tail, cgot, cgot_down, cgot_tail, zgot, zgot_down, zgot_tail,
+    total, total_down, total_tail, gain_got, gain_sum,
+    xsend, xrecv, csend, crecv, zsend, zrecv, csend_t, crecv_t, zsend_t, zrecv_t,
+    gsend, grecv, glocal, hsend, hrecv, isend, irecv,
+):
+    rows, width, ff, n_seq, n_blk, split = sizes
+    run = Reducer(rows, ff, n_seq, n_blk)
+    barrier = pltpu.get_barrier_semaphore()
+    for step in range(1, n_seq):
+        pl.semaphore_signal(barrier, inc=1, device_id={"seq": lax.rem(run.seq + step, n_seq)}, device_id_type=MESH)
+    for step in range(1, n_blk):
+        pl.semaphore_signal(barrier, inc=1, device_id={"blk": lax.rem(run.blk + step, n_blk)}, device_id_type=MESH)
+    pl.semaphore_wait(barrier, n_seq + n_blk - 2)
+
+    cuts = [0]
+    for tiles in split:
+        cuts.append(cuts[-1] + tiles * TILE)
+    wide = max(split) * TILE
+    chunk = width // n_blk
+    down = ff // n_blk
+    first = [
+        [(0, two, buf_a), (1, gate_up.at[:, cuts[0] : cuts[1]], buf_b.at[:, : cuts[1] - cuts[0]])],
+        [(0, two, buf_a), (1, gate_up.at[:, cuts[1] : cuts[2]], buf_b.at[:, : cuts[2] - cuts[1]])],
+        [
+            (0, two, buf_a),
+            (1, gate_up.at[:, cuts[2] : cuts[3]], buf_b.at[:, : cuts[3] - cuts[2]]),
+            (2, att, buf_att),
+            (3, mid, buf_mid),
+        ],
+        [(0, cot, buf_a), (1, act, buf_b)],
+    ]
+    last = [
+        [(4, normed, buf_n), (5, q_grad, buf_t)],
+        [(4, normed, buf_n), (5, k_grad, buf_t)],
+        [(4, normed, buf_n), (5, v_grad, buf_t)],
+        [],
+    ]
+    for owner in range(n_seq):
+        for kind, src, dst in first[owner]:
+            run.give(owner, kind, src, dst, xsend, xrecv)
+    for owner in range(n_seq):
+        for kind, src, dst in last[owner]:
+            run.give(owner, kind, src, dst, xsend, xrecv)
+
+    for step in range(1, n_blk):
+        other = lax.rem(run.blk + step, n_blk)
+        remote(gains.at[other], gain_got.at[step - 1], hsend.at[step - 1], hrecv.at[step - 1], {"blk": other}).start()
+
+    sems = (csend, crecv, zsend, zrecv)
+    tail_sems = (csend_t, crecv_t, zsend_t, zrecv_t)
+
+    for owner in range(n_seq):
+
+        @pl.when(run.seq == owner)
+        def _(owner=owner):
+            for kind, src, dst in first[owner]:
+                run.given(owner, kind, src, dst, xsend, xrecv)
+
+    @pl.when(run.seq < 3)
+    def _():
+        def one(step, unused):
+            chip = run.turned(step)
+
+            @pl.when(run.seq < 2)
+            def _():
+                outer_tiles(buf_a, buf_b, part, turned, chip, split[0], 0)
+
+            @pl.when(run.seq == 2)
+            def _():
+                spare = wide - split[2] * TILE - width
+                if spare:
+                    part[pl.ds(multiple(chip * TILE, TILE), TILE), wide - spare :] = jnp.zeros((TILE, spare), BF16)
+                outer_tiles(buf_a, buf_b, part, turned, chip, split[2], 0)
+                outer_tiles(buf_att, buf_mid, part, turned, chip, width // TILE, split[2] * TILE)
+
+            run.swap(part, chunk, chip, cgot, csend, crecv).start()
+            return unused
+
+        lax.fori_loop(1, run.chips + 1, one, 0)
+
+    @pl.when(run.seq == 3)
+    def _():
+        def one(index, unused):
+            at = pl.ds(multiple(index * TILE, TILE), TILE)
+            turned[...] = buf_b[:, at].T
+            part_down[at, :] = jnp.dot(turned[...], buf_a[...], preferred_element_type=F32).astype(BF16)
+            return unused
+
+        lax.fori_loop(0, ff // TILE, one, 0)
+
+        def swaps(step, unused):
+            run.swap(part_down, down, run.turned(step), cgot_down, csend, crecv).start()
+            return unused
+
+        lax.fori_loop(1, run.chips + 1, swaps, 0)
+
+    @pl.when(run.seq < 3)
+    def _():
+        run.reduce_begin(part, chunk, cgot, zgot, sems)
+
+    @pl.when(run.seq == 3)
+    def _():
+        run.reduce_begin(part_down, down, cgot_down, zgot_down, sems)
+
+    for owner in range(n_seq - 1):
+
+        @pl.when(run.seq == owner)
+        def _(owner=owner):
+            for kind, src, dst in last[owner]:
+                run.given(owner, kind, src, dst, xsend, xrecv)
+
+    @pl.when(run.seq < 3)
+    def _():
+        def one(step, unused):
+            chip = run.turned(step)
+            outer_tiles(buf_n, buf_t, part_tail, turned, chip, width // TILE, 0)
+            run.swap(part_tail, chunk, chip, cgot_tail, csend_t, crecv_t).start()
+            return unused
+
+        lax.fori_loop(1, run.chips + 1, one, 0)
+        run.reduce_begin(part_tail, chunk, cgot_tail, zgot_tail, tail_sems)
+
+    spreads = [
+        (0, total.at[:, : cuts[1] - cuts[0]], out_gu.at[:, cuts[0] : cuts[1]], 0),
+        (1, total.at[:, : cuts[2] - cuts[1]], out_gu.at[:, cuts[1] : cuts[2]], 1),
+        (2, total.at[:, : cuts[3] - cuts[2]], out_gu.at[:, cuts[2] : cuts[3]], 2),
+        (2, total.at[:, cuts[3] - cuts[2] : cuts[3] - cuts[2] + width], out_out, 3),
+        (3, total_down, out_down, 4),
+    ]
+    tails = [
+        (0, total_tail, out_query, 5),
+        (1, total_tail, out_key, 6),
+        (2, total_tail, out_value, 7),
+    ]
+
+    @pl.when(run.seq < 3)
+    def _():
+        run.reduce_end(part, chunk, cgot, zgot, total, sems)
+
+    @pl.when(run.seq == 3)
+    def _():
+        run.reduce_end(part_down, down, cgot_down, zgot_down, total_down, sems)
+
+    for owner, src, dst, kind in spreads:
+
+        @pl.when(run.seq == owner)
+        def _(owner=owner, src=src, dst=dst, kind=kind):
+            run.spread(owner, src, dst, kind, gsend, grecv, glocal)
+
+    value = gains[run.blk]
+    for step in range(1, n_blk):
+        other = lax.rem(run.blk + step, n_blk)
+        copy = remote(gains.at[other], gain_got.at[step - 1], hsend.at[step - 1], hrecv.at[step - 1], {"blk": other})
+        copy.wait()
+        value = value + gain_got[step - 1]
+    gain_sum[run.seq] = value
+    for step in range(1, n_seq):
+        other = lax.rem(run.seq + step, n_seq)
+        remote(gain_sum.at[run.seq], gain_sum.at[run.seq], isend.at[step - 1], irecv.at[run.seq], {"seq": other}).start()
+
+    @pl.when(run.seq < 3)
+    def _():
+        run.reduce_end(part_tail, chunk, cgot_tail, zgot_tail, total_tail, tail_sems)
+
+    for owner, src, dst, kind in tails:
+
+        @pl.when(run.seq == owner)
+        def _(owner=owner, src=src, dst=dst, kind=kind):
+            run.spread(owner, src, dst, kind, gsend, grecv, glocal)
+
+    for step in range(1, n_seq):
+        other = lax.rem(run.seq + step, n_seq)
+        remote(gain_sum.at[other], gain_sum.at[other], isend.at[step - 1], irecv.at[other], {"seq": other}).wait()
+    value = gain_sum[0]
+    for group in range(1, n_seq):
+        value = value + gain_sum[group]
+    half = value.shape[0] // 2
+    out_gain[...] = jnp.concatenate(
+        [
+            jnp.broadcast_to(jnp.sum(value[:half], axis=0, keepdims=True), (half, value.shape[1])),
+            jnp.broadcast_to(jnp.sum(value[half:], axis=0, keepdims=True), (half, value.shape[1])),
+        ],
+        axis=0,
+    )
+
+    for owner, src, dst, kind in spreads + tails:
+        run.spread_wait(owner, src, dst, kind, gsend, grecv, glocal)
+    for owner in range(n_seq):
+        for kind, src, dst in first[owner] + last[owner]:
+            run.sent(owner, kind, src, dst, xsend, xrecv)
+
+
+def reduce_grads(sizes, operands):
+    rows, width, ff, n_seq, n_blk, split = sizes
+    wide = max(split) * TILE
+    chunk, down = width // n_blk, ff // n_blk
+    all_rows = n_seq * rows
+    chips = n_blk // 2
+    vmem = pl.BlockSpec(memory_space=pltpu.VMEM)
+    hbm = pl.BlockSpec(memory_space=pl.ANY)
+    shape = jax.ShapeDtypeStruct
+    dma = pltpu.SemaphoreType.DMA
+    return pl.pallas_call(
+        functools.partial(grad_kernel, sizes),
+        out_shape=(
+            shape((chunk, 2 * ff), BF16),
+            shape((down, width), BF16),
+            shape((chunk, width), BF16),
+            shape((chunk, width), BF16),
+            shape((chunk, width), BF16),
+            shape((chunk, width), BF16),
+            shape((16, chunk), F32),
+        ),
+        in_specs=[vmem] * len(operands),
+        out_specs=(hbm,) * 6 + (vmem,),
+        scratch_shapes=[
+            pltpu.VMEM((all_rows, width), BF16),
+            pltpu.VMEM((all_rows, ff), BF16),
+            pltpu.VMEM((all_rows, width), BF16),
+            pltpu.VMEM((all_rows, width), BF16),
+            pltpu.VMEM((all_rows, width), BF16),
+            pltpu.VMEM((all_rows, width), BF16),
+            pltpu.VMEM((TILE, all_rows), BF16),
+            pltpu.VMEM((width, wide), BF16),
+            pltpu.VMEM((ff, width), BF16),
+            pltpu.VMEM((width, width), BF16),
+            pltpu.VMEM((chips * chunk, wide), BF16),
+            pltpu.VMEM((chips * down, width), BF16),
+            pltpu.VMEM((chips * chunk, width), BF16),
+            pltpu.VMEM(((chips - 1) * chunk, wide), BF16),
+            pltpu.VMEM(((chips - 1) * down, width), BF16),
+            pltpu.VMEM(((chips - 1) * chunk, width), BF16),
+            pltpu.VMEM((chunk, wide), BF16),
+            pltpu.VMEM((down, width), BF16),
+            pltpu.VMEM((chunk, width), BF16),
+            pltpu.VMEM((n_blk - 1, 16, chunk), F32),
+            pltpu.VMEM((n_seq, 16, chunk), F32),
+            dma((6, n_seq)), dma((6, n_seq)),
+            dma((chips,)), dma((chips,)), dma((chips - 1,)), dma((chips - 1,)),
+            dma((chips,)), dma((chips,)), dma((chips - 1,)), dma((chips - 1,)),
+            dma((8, n_seq)), dma((8,)), dma((8,)),
+            dma((n_blk - 1,)), dma((n_blk - 1,)),
+            dma((n_seq - 1,)), dma((n_seq,)),
+        ],
+        compiler_params=pltpu.CompilerParams(
+            collective_id=0, has_side_effects=True, vmem_limit_bytes=60 * 1024 * 1024
+        ),
+        name="weight_grads",
+    )(*operands)
+
+
+def eighths(values, n_blk):
+    rows, width = values.shape
+    part = jnp.sum(values.reshape(rows // 8, 8, width), axis=0)
+    return part.reshape(8, n_blk, width // n_blk).transpose(1, 0, 2)
+
+
+def tile_split(width, ff):
+    tiles, more = 2 * ff // TILE, width // TILE
+    each = -(-(tiles + more) // 3)
+    return (each, each, tiles - 2 * each)
+
+
+def fits(n_seq, n_blk, rows, width, ff):
+    return (
+        n_seq == 4
+        and n_blk % 2 == 0
+        and n_blk * 128 == width
+        and rows == 128
+        and ff % TILE == 0
+        and (ff // n_blk) % 32 == 0
     )
 
 
@@ -339,9 +761,283 @@
     )
 
 
+def local_fast(
+    n_seq,
+    n_blk,
+    tokens,
+    first_values,
+    doc_lengths,
+    attn_gain,
+    query_weight,
+    key_weight,
+    value_weight,
+    out_weight,
+    ffn_gain,
+    gate_weight,
+    up_weight,
+    down_weight,
+    cotangent,
+):
+    rows, width = tokens.shape
+    heads = width // HEAD_DIM
+    scale = HEAD_DIM ** (-0.5)
+    shape3 = (rows, heads, HEAD_DIM)
+    my_start = lax.axis_index("blk") * rows
+    my_index = my_start + jnp.arange(rows, dtype=jnp.int32)
+    my_doc, my_pos = doc_layout(doc_lengths, my_index)
+    cosine, sine = tables(my_pos)
+    source = tokens.astype(jnp.float32)
+    inv_first = lax.rsqrt(jnp.mean(source * source, axis=-1, keepdims=True) + EPS)
+    normed = (source * inv_first * attn_gain).astype(jnp.bfloat16)
+    query_pre = jnp.dot(normed, query_weight, preferred_element_type=jnp.float32)
+    key_pre = jnp.dot(normed, key_weight, preferred_element_type=jnp.float32)
+    value_pre = jnp.dot(normed, value_weight, preferred_element_type=jnp.float32)
+    queries = rotate(query_pre.reshape(shape3), cosine, sine).astype(jnp.bfloat16)
+    keys = rotate(key_pre.reshape(shape3), cosine, sine).astype(jnp.bfloat16).reshape(rows, width)
+    mixed = (MIX * value_pre + MIX * first_values.astype(jnp.float32)).astype(jnp.bfloat16)
+    keys_local = keys.reshape(shape3)
+    mixed_local = mixed.reshape(shape3)
+
+    def allowed_mask(query_index, query_doc, key_index, key_doc):
+        return (query_doc[:, None] == key_doc[None, :]) & (
+            key_index[None, :] <= query_index[:, None]
+        )
+
+    def forward_step(state, pieces, start):
+        count = pieces[0].shape[0]
+        keys_piece = pieces[0].reshape(count, heads, HEAD_DIM)
+        values_piece = pieces[1].reshape(count, heads, HEAD_DIM)
+        key_index = start + jnp.arange(count, dtype=jnp.int32)
+
+        def forward_compute(state):
+            high, total, accum = state
+            key_doc, unused = doc_layout(doc_lengths, key_index)
+            allowed = allowed_mask(my_index, my_doc, key_index, key_doc)[None]
+            score = (
+                jnp.einsum("qhd,khd->hqk", queries, keys_piece, preferred_element_type=jnp.float32)
+                * scale
+            )
+            score = jnp.where(allowed, score, NEG)
+            new_high = jnp.maximum(high, jnp.max(score, axis=-1))
+            weight = jnp.where(allowed, jnp.exp(score - new_high[:, :, None]), 0.0)
+            factor = jnp.exp(high - new_high)
+            total = total * factor + jnp.sum(weight, axis=-1)
+            accum = accum * factor.T[:, :, None] + jnp.einsum(
+                "hqk,khd->qhd",
+                weight.astype(jnp.bfloat16),
+                values_piece,
+                preferred_element_type=jnp.float32,
+            )
+            return (new_high, total, accum)
+
+        return lax.cond(start <= my_index[-1], forward_compute, lambda kept: kept, state)
+
+    def query_grad_step(grad_q, pieces, start):
+        count = pieces[0].shape[0]
+        keys_piece = pieces[0].reshape(count, heads, HEAD_DIM)
+        values_piece = pieces[1].reshape(count, heads, HEAD_DIM)
+        key_index = start + jnp.arange(count, dtype=jnp.int32)
+
+        def query_compute(grad_q):
+            key_doc, unused = doc_layout(doc_lengths, key_index)
+            allowed = allowed_mask(my_index, my_doc, key_index, key_doc)[None]
+            score = (
+                jnp.einsum("qhd,khd->hqk", queries, keys_piece, preferred_element_type=jnp.float32)
+                * scale
+            )
+            prob = jnp.where(allowed, jnp.exp(score - logsum[:, :, None]), 0.0)
+            prob_grad = jnp.einsum(
+                "qhd,khd->hqk", outgrad_local, values_piece, preferred_element_type=jnp.float32
+            )
+            score_grad = (prob * (prob_grad - delta[:, :, None])).astype(jnp.bfloat16)
+            return (
+                grad_q
+                + jnp.einsum(
+                    "hqk,khd->qhd", score_grad, keys_piece, preferred_element_type=jnp.float32
+                )
+                * scale
+            )
+
+        return lax.cond(start <= my_index[-1], query_compute, lambda kept: kept, grad_q)
+
+    init = (
+        jnp.full((heads, rows), NEG, jnp.float32),
+        jnp.zeros((heads, rows), jnp.float32),
+        jnp.zeros(shape3, jnp.float32),
+    )
+    state = by_blocks(
+        forward_step,
+        init,
+        (
+            lax.all_gather(keys, "blk", axis=0, tiled=True),
+            lax.all_gather(mixed, "blk", axis=0, tiled=True),
+        ),
+        jnp.int32(0),
+    )
+    high, total, accum = state
+    logsum = high + jnp.log(total)
+    attended = accum / total.T[:, :, None]
+    attended_b = attended.astype(jnp.bfloat16).reshape(rows, width)
+    mid = source + jnp.dot(attended_b, out_weight, preferred_element_type=jnp.float32)
+    inv_second = lax.rsqrt(jnp.mean(mid * mid, axis=-1, keepdims=True) + EPS)
+    normed_two = (mid * inv_second * ffn_gain).astype(jnp.bfloat16)
+    gate = jnp.dot(normed_two, gate_weight, preferred_element_type=jnp.float32)
+    up = jnp.dot(normed_two, up_weight, preferred_element_type=jnp.float32)
+    act = (jax.nn.silu(gate) * up).astype(jnp.bfloat16)
+    layer_output = mid + jnp.dot(act, down_weight, preferred_element_type=jnp.float32)
+    cot_float = cotangent.astype(jnp.float32)
+    act_grad = back(cotangent, down_weight)
+    sigma = jax.nn.sigmoid(gate)
+    gate_grad = (act_grad * up * sigma * (1.0 + gate * (1.0 - sigma))).astype(jnp.bfloat16)
+    up_grad = (act_grad * gate * sigma).astype(jnp.bfloat16)
+    normed_two_grad = back(gate_grad, gate_weight) + back(up_grad, up_weight)
+    grad_ffn_gain = eighths(normed_two_grad * mid * inv_second, n_blk)
+    scaled_two = normed_two_grad * ffn_gain
+    mid_grad = (
+        cot_float
+        + inv_second * scaled_two
+        - mid * inv_second**3 * jnp.mean(scaled_two * mid, axis=-1, keepdims=True)
+    )
+    mid_grad_b = mid_grad.astype(jnp.bfloat16)
+    attended_grad = back(mid_grad_b, out_weight).astype(jnp.bfloat16)
+    outgrad_local = attended_grad.reshape(shape3)
+    delta = jnp.sum(outgrad_local.astype(jnp.float32) * attended, axis=-1).T
+    zeros3 = jnp.zeros(shape3, jnp.float32)
+    grad_q = by_blocks(
+        query_grad_step,
+        zeros3,
+        (
+            lax.all_gather(keys, "blk", axis=0, tiled=True),
+            lax.all_gather(mixed, "blk", axis=0, tiled=True),
+        ),
+        jnp.int32(0),
+    )
+    all_logsum, all_delta = (
+        lax.all_gather(logsum.T, "blk", axis=0, tiled=True),
+        lax.all_gather(delta.T, "blk", axis=0, tiled=True),
+    )
+
+    def key_grad_step(state, pieces, start):
+        count = pieces[0].shape[0]
+        query_piece = pieces[0].reshape(count, heads, HEAD_DIM)
+        outgrad_piece = pieces[1].reshape(count, heads, HEAD_DIM)
+        query_index = start + jnp.arange(count, dtype=jnp.int32)
+
+        def key_compute(state):
+            grad_k, grad_v = state
+            logsum_piece = lax.dynamic_slice_in_dim(all_logsum, start, count, 0).T
+            delta_piece = lax.dynamic_slice_in_dim(all_delta, start, count, 0).T
+            query_doc, unused = doc_layout(doc_lengths, query_index)
+            allowed = allowed_mask(query_index, query_doc, my_index, my_doc)[None]
+            score = (
+                jnp.einsum(
+                    "qhd,khd->hqk", query_piece, keys_local, preferred_element_type=jnp.float32
+                )
+                * scale
+            )
+            prob = jnp.where(allowed, jnp.exp(score - logsum_piece[:, :, None]), 0.0)
+            grad_v = grad_v + jnp.einsum(
+                "hqk,qhd->khd",
+                prob.astype(jnp.bfloat16),
+                outgrad_piece,
+                preferred_element_type=jnp.float32,
+            )
+            prob_grad = jnp.einsum(
+                "qhd,khd->hqk", outgrad_piece, mixed_local, preferred_element_type=jnp.float32
+            )
+            score_grad = (prob * (prob_grad - delta_piece[:, :, None])).astype(jnp.bfloat16)
+            grad_k = (
+                grad_k
+                + jnp.einsum(
+                    "hqk,qhd->khd", score_grad, query_piece, preferred_element_type=jnp.float32
+                )
+                * scale
+            )
+            return (grad_k, grad_v)
+
+        return lax.cond(query_index[-1] >= my_start, key_compute, lambda kept: kept, state)
+
+    grad_k, grad_v = by_blocks(
+        key_grad_step,
+        (zeros3, zeros3),
+        (
+            lax.all_gather(queries.reshape(rows, width), "blk", axis=0, tiled=True),
+            lax.all_gather(attended_grad, "blk", axis=0, tiled=True),
+        ),
+        jnp.int32(0),
+    )
+    queries_grad = grad_q.astype(jnp.bfloat16)
+    keys_grad = grad_k.astype(jnp.bfloat16)
+    mixed_grad = grad_v.astype(jnp.bfloat16).reshape(rows, width)
+    q_pre_grad = (
+        rotate(queries_grad.astype(jnp.float32), cosine, -sine)
+        .astype(jnp.bfloat16)
+        .reshape(rows, width)
+    )
+    k_pre_grad = (
+        rotate(keys_grad.astype(jnp.float32), cosine, -sine)
+        .astype(jnp.bfloat16)
+        .reshape(rows, width)
+    )
+    grad_first = MIX * mixed_grad.astype(jnp.float32)
+    value_grad = grad_first.astype(jnp.bfloat16)
+    normed_grad = (
+        back(q_pre_grad, query_weight)
+        + back(k_pre_grad, key_weight)
+        + back(value_grad, value_weight)
+    )
+    grad_attn_gain = eighths(normed_grad * source * inv_first, n_blk)
+    scaled_one = normed_grad * attn_gain
+    grad_tokens = (
+        mid_grad
+        + inv_first * scaled_one
+        - source * inv_first**3 * jnp.mean(scaled_one * source, axis=-1, keepdims=True)
+    )
+    ff = gate_weight.shape[1]
+    sizes = (rows, width, ff, n_seq, n_blk, tile_split(width, ff))
+    out_gu, out_down, out_out, out_query, out_key, out_value, out_gain = reduce_grads(
+        sizes,
+        (
+            normed,
+            q_pre_grad,
+            k_pre_grad,
+            value_grad,
+            attended_b,
+            mid_grad_b,
+            normed_two,
+            jnp.concatenate([gate_grad, up_grad], axis=1),
+            act,
+            cotangent,
+            jnp.concatenate([grad_attn_gain, grad_ffn_gain], axis=1),
+        ),
+    )
+    return (
+        layer_output,
+        grad_tokens,
+        grad_first,
+        out_gain[0],
+        out_query.astype(F32),
+        out_key.astype(F32),
+        out_value.astype(F32),
+        out_out.astype(F32),
+        out_gain[8],
+        out_gu[:, :ff].astype(F32),
+        out_gu[:, ff:].astype(F32),
+        out_down.astype(F32),
+    )
+
+
 def solution(mesh):
+    n_seq, n_blk = mesh.shape["seq"], mesh.shape["blk"]
+
+    def chosen(*args):
+        rows, width = args[0].shape
+        if fits(n_seq, n_blk, rows, width, args[9].shape[1]):
+            return local_fast(n_seq, n_blk, *args)
+        return local(*args)
+
     return jax.shard_map(
-        local,
+        chosen,
         mesh=mesh,
         in_specs=(
             P(("seq", "blk"), None),

time: 831 us -> 384 us (0.46)
  waiting for transfers between devices: 573 us -> 53.3 us
  Pallas kernels: 0 us -> 157 us
  matrix products: 111 us -> 73.3 us
  blocking collectives: 50.8 us -> 26.5 us
  other arithmetic: 48 us -> 31.8 us
    reduce_scatter x7 -> x0, waiting for transfers between devices: 466 us -> none  [the longest x1 119 us: local(): lax.psum_scatter(grad_down, 'blk', scatter_dimension=0, tiled=True)]
    pallas_call x0 -> x1, Pallas kernels: none -> 157 us  [reduce_grads(): pl.pallas_call(functools.partial(grad_kernel, sizes), out_shape=(shape((c...]
    psum x1 -> x0, waiting for transfers between devices: 56.1 us -> none  [local(): lax.psum(summed[1].astype(jnp.bfloat16), 'seq').astype(jnp.float32)]
    dot_general x14 -> x7, matrix products: 52.6 us -> 16.1 us  [the longest x1 4.46 us: local_fast(): jnp.dot(act, down_weight, preferred_element_type=jnp.float32)]
    convert_element_type x22 -> x15, other arithmetic: 30.6 us -> 15.4 us  [the longest x1 3.16 us: local_fast(): out_gu[:, ff:].astype(F32)]
    unnamed x1 -> x0, blocking collectives: 13.3 us -> none
    psum x1 -> x0, blocking collectives: 9.83 us -> none  [local(): lax.psum(summed[0].astype(jnp.bfloat16), 'seq').astype(jnp.float32)]
  transfers between devices with their start and end apart: 12 -> 4, of which waited for: 9 -> 2; matrix products, arithmetic and copies ran while one was open for 19% -> 18% of each run, Pallas kernels for 0% -> 0%
where the time goes in v1:
time: 384 us; the launch traced here: 380 us
  Pallas kernels  157 us (41%)
  matrix products  73.3 us (19%)
  waiting for transfers between devices  53.3 us (14%)
  other arithmetic  31.8 us (8%)
  blocking collectives  26.5 us (7%)
  local copies, waits for them, and re-layouts  21 us (5%)
  between operations  15.7 us (4%)
    pallas_call x1, Pallas kernels, reduce_grads(): pl.pallas_call(functools.partial(grad_kernel, sizes), out_shape=(shape((c...  157 us
    all_gather x1, waiting for transfers between devices, local_fast(): lax.all_gather(keys, 'blk', axis=0, tiled=True)  30.4 us
    all_gather x1, waiting for transfers between devices, local_fast(): lax.all_gather(mixed, 'blk', axis=0, tiled=True)  22.8 us
    all_gather x1, blocking collectives, local_fast(): lax.all_gather(logsum.T, 'blk', axis=0, tiled=True)  14.2 us
    dot_general x7, matrix products, back(): lax.dot_general(left, weight, (((1,), (1,)), ((), ())), preferred_element...  14 us
    all_gather x1, blocking collectives, local_fast(): lax.all_gather(delta.T, 'blk', axis=0, tiled=True)  12.4 us
    dot_general x1, matrix products, key_compute(): jnp.einsum('hqk,qhd->khd', score_grad, query_piece, preferred_element_typ...  9.74 us
    dot_general x1, matrix products, query_compute(): jnp.einsum('hqk,khd->qhd', score_grad, keys_piece, preferred_element_type...  8.78 us
  transfers between devices with their start and end apart: 4, of which 2 were waited for; matrix products, arithmetic and copies ran while one was open for 18% of the time, Pallas kernels for 0%

profile of v1, /device:TPU:8, one launch (start us, length us, event | category | flops | bytes accessed | tf_op | source)
XLA Modules:
  0.0 380.0 jit_solution(2916355194772076704)
XLA Ops:
  10.6 2.8 fusion.46
  14.6 2.5 fusion.66
  21.1 22.8 %all-gather.7.cloned.1.call-done = bf16[1024,1024]{1,0:T(8,128)(2,1)} async-done(((bf16[128,1024]{1,0:T(8,128)(2,1)}), bf16[1024,1024]{1,0:T(8,128)(2,1)}) %all-gather.7.cloned.1.call-update) | async-done | bytes 2097168 | tf_op jit(solution)/shard_map/all_gather | solution.py:873
  43.9 3.9 %copy.52 = bf16[1024,1024]{0,1:T(8,128)(2,1)} copy(bf16[1024,1024]{1,0:T(8,128)(2,1)} %all-gather.7.cloned.1.call-done) | data formatting | bytes 4194304 | tf_op jit(solution)/shard_map/all_gather | solution.py:873
  47.8 30.4 %all-gather.5.cloned.1.call-done = bf16[1024,1024]{0,1:T(8,128)(2,1)} async-done(((bf16[128,1024]{0,1:T(8,128)(2,1)}), bf16[1024,1024]{0,1:T(8,128)(2,1)}) %all-gather.5.cloned.1.call-update) | async-done | bytes 2097168 | tf_op jit(solution)/shard_map/all_gather | solution.py:872
  78.2 11.5 %conditional.3 = (f32[16,128]{1,0:T(8,128)}, f32[16,128]{1,0:T(8,128)S(1)}, f32[128,16,64]{0,2,1:T(8,128)S(1)}, f32[16,128]{1,0:T(8,128)S(1)}) conditional(s32[]{:T(128)} %bitcast.17, () %tuple.34, (s32[128]{0:T(128)S(1)}, s32[1024]{0:T(1024)S(1)}, s32[1,4]{1,0:T(1,128)S(1)}, s32[1024]{0:T(1024)S(1)}, s32[128]{0:T(128)S(1)}, ...), branch_computations={%region_4.5_spmd, %region_5.10_spmd} | conditional | flops 564677632 | bytes 39175280 | solution.py:833
  78.7 3.2 fusion
  82.5 3.3 fusion.2
  86.5 3.1 fusion.9
  91.4 3.9 %fusion.68 = f32[128,2816]{1,0:T(8,128)S(1)} fusion(bf16[128,1024]{1,0:T(8,128)(2,1)S(1)} %multiply_convert_fusion.15.two, bf16[1024,2816]{1,0:T(8,128)(2,1)} %param.28), kind=kOutput, calls=%fused_computation.125 | convolution fusion | flops 738197504 | bytes 7471104 | tf_op jit(solution)/shard_map/dot_general | solution.py:884
  97.8 3.3 multiply_convert_fusion.12
  101.1 2.0 fusion.70
  103.1 2.1 multiply_reduce_fusion.1
  109.7 1.8 copy.53
  111.5 1.8 copy.59.att
  114.6 1.6 multiply_reduce_fusion
  116.3 15.7 %conditional.4 = (bf16[128,16,64]{0,2,1:T(8,128)(2,1)}) conditional(s32[]{:T(128)} %bitcast.17, () %tuple.36, (s32[128]{0:T(128)S(1)}, s32[1024]{0:T(1024)S(1)}, s32[1,4]{1,0:T(1,128)S(1)}, s32[1024]{0:T(1024)S(1)}, s32[128]{0:T(128)S(1)}, /*index=5*/bf16[128,16,64]{0,2,1:T(8,128)(2,1)}, bf16[1024,16,64]{0,2,1:T(8,128)(2,1)S(1)}, ...), branch_computations={%region_13.14_spmd, %region_14.17_spmd} | conditional | flops 818555904 | bytes 24171664 | solution.py:861
  116.5 5.5 %fusion.64 = f32[16,128,1024]{2,1,0:T(8,128)} fusion(bf16[128,16,64]{0,2,1:T(8,128)(2,1)} %get-tuple-element.78, bf16[1024,16,64]{0,2,1:T(8,128)(2,1)S(1)} %get-tuple-element.79), kind=kOutput, calls=%fused_computation.121 | convolution fusion | flops 268435456 | bytes 10747904 | tf_op jit(solution)/shard_map/cond/branch_1_fun/qhd,khd->hqk/dot_general | solution.py:845
  123.2 8.8 %fusion.22 = bf16[128,16,64]{0,2,1:T(8,128)(2,1)} fusion(bf16[1024,16,64]{0,2,1:T(8,128)(2,1)S(1)} %get-tuple-element.79, f32[16,128,1024]{2,1,0:T(8,128)} %fusion.64, f32[16,128]{1,0:T(8,128)} %get-tuple-element.83, f32[16,128]{1,0:T(8,128)} %get-tuple-element.80, pred[128,1024]{1,0:T(8,128)(4,1)S(1)} %compare_and_fusion.1, ...), kind=kOutput, calls=%fused_computation.23 | convolution fusion | flops 549715968 | bytes 13254656 | tf_op jit(solution)/shard_map/cond/branch_1_fun/hqk,khd->qhd/dot_general | solution.py:855
  132.0 1.9 convert_element_type.286
  133.9 12.4 %all_gather.25 = f32[1024,16]{0,1:T(8,128)S(1)} all-gather(f32[128,16]{0,1:T(8,128)} %multiply_reduce_fusion), channel_id=1, replica_groups=mesh['seq'=4,'blk'=8] {'blk'}, dimensions={0}, use_global_device_ids=true | all-gather | bytes 73728 | tf_op jit(solution)/shard_map/all_gather | solution.py:917
  146.2 14.2 %all_gather.23 = f32[1024,16]{0,1:T(8,128)S(1)} all-gather(f32[128,16]{0,1:T(8,128)} %bitcast.136), channel_id=1, replica_groups=mesh['seq'=4,'blk'=8] {'blk'}, dimensions={0}, use_global_device_ids=true | all-gather | bytes 73728 | tf_op jit(solution)/shard_map/all_gather | solution.py:916
  161.1 4.5 %convolution_add_fusion.5 = f32[128,1024]{1,0:T(8,128)} fusion(f32[128,1024]{1,0:T(8,128)S(1)} %get-tuple-element.236, bf16[128,2816]{1,0:T(8,128)(2,1)S(1)} %copy-done.14, bf16[2816,1024]{1,0:T(8,128)(2,1)} %param.30), kind=kOutput, calls=%fused_computation.57 | convolution fusion | flops 738328576 | bytes 7536640 | tf_op jit(solution)/shard_map/dot_general | solution.py:887
  166.9 28.9 %conditional.5 = (bf16[128,16,64]{0,2,1:T(8,128)(2,1)}, f32[128,1024]{1,0:T(8,128)S(1)}) conditional(s32[]{:T(128)} %convert_element_type.190, () %tuple.38, (s32[1024]{0:T(1024)S(1)}, s32[1,4]{1,0:T(1,128)S(1)}, s32[128]{0:T(128)S(1)}, s32[128]{0:T(128)S(1)}, s32[1024]{0:T(1024)S(1)}, /*index=5*/bf16[1024,1024]{0,1:T(8,128)(2,1)}, ...), branch_computations={%region_17.18_spmd, %region_18.21_spmd} | conditional | flops 1095642112 | bytes 50152600 | solution.py:958
  167.2 6.3 %fusion.65 = f32[16,1024,128]{2,1,0:T(8,128)} fusion(bf16[1024,16,64]{0,2,1:T(8,128)(2,1)} %bitcast.123, bf16[128,16,64]{0,2,1:T(8,128)(2,1)S(1)} %get-tuple-element.90), kind=kOutput, calls=%fused_computation.122 | convolution fusion | flops 268435456 | bytes 10747904 | tf_op jit(solution)/shard_map/cond/branch_1_fun/qhd,khd->hqk/dot_general | solution.py:933
  173.5 4.0 %copy.54 = bf16[1024,1024]{0,1:T(8,128)(2,1)} copy(bf16[1024,1024]{1,0:T(8,128)(2,1)} %get-tuple-element.193) | data formatting | bytes 4194304 | tf_op jit(solution)/shard_map
  178.2 9.7 %fusion.34 = bf16[128,16,64]{0,2,1:T(8,128)(2,1)} fusion(bf16[1024,16,64]{0,2,1:T(8,128)(2,1)} %bitcast.124, f32[16,1024,128]{2,1,0:T(8,128)} %fusion.65, f32[16,1024]{1,0:T(8,128)S(1)} %bitcast.132, f32[16,1024]{1,0:T(8,128)S(1)} %bitcast.133, pred[1024,128]{1,0:T(8,128)(4,1)S(1)} %compare_and_fusion.2, bf16[1024,16,64]{0,2,1:T(8,128)(2,1)} %bitcast.119, ...), kind=kOutput, calls=%fused_computation.37 | convolution fusion | flops 549715968 | bytes 13369344 | tf_op jit(solution)/shard_map/cond/branch_1_fun/hqk,qhd->khd/dot_general | solution.py:951
  188.0 6.6 %fusion.38 = f32[16,128,64]{1,2,0:T(8,128)} fusion(bf16[1024,16,64]{0,2,1:T(8,128)(2,1)S(1)} %bitcast.120, f32[16,1024,128]{2,1,0:T(8,128)} %fusion.65, f32[16,1024]{1,0:T(8,128)S(1)} %bitcast.134, pred[1024,128]{1,0:T(8,128)(4,1)S(1)} %compare_and_fusion.2), kind=kOutput, calls=%fused_computation.39 | convolution fusion | flops 277086208 | bytes 11206656 | tf_op jit(solution)/shard_map/cond/branch_1_fun/hqk,qhd->khd/dot_general | solution.py:939
  197.5 1.6 fusion.71
  200.8 2.6 convolution_add_fusion.1
  206.1 157.3 %weight_grads.1 = (bf16[128,5632]{1,0:T(8,128)(2,1)}, bf16[352,1024]{1,0:T(8,128)(2,1)}, bf16[128,1024]{1,0:T(8,128)(2,1)}, bf16[128,1024]{1,0:T(8,128)(2,1)}, b...) custom-call(bf16[128,1024]{1,0:T(8,128)(2,1)} %copy-done.8, ...), custom_call_target="tpu_custom_call" | custom-call | tf_op jit(solution)/shard_map/weight_grads/pallas_call | solution.py:417
  363.4 3.2 slice_convert_fusion
  (189 shorter events, 36.6 us)
Async XLA Ops:
  7.2 83.4 %copy-start = (bf16[1024,1024]{1,0:T(8,128)(2,1)S(1)}, bf16[1024,1024]{1,0:T(8,128)(2,1)}, u32[]{:S(2)}) copy-start(bf16[1024,1024]{1,0:T(8,128)(2,1)} %param.26) | copy-start | bytes 6291460
  7.2 6.3 %copy-start.49 = (s32[1,4]{1,0:T(1,128)S(1)}, s32[1,4]{1,0:T(1,128)}, u32[]{:S(2)}) copy-start(s32[1,4]{1,0:T(1,128)} %param.21) | copy-start | bytes 52
  7.2 36.6 %all-gather.7.cloned.1.call-start = ((), (), s32[]{:S(2)}) async-start(), calls=%async_computation.1 | async-start | bytes 2359296 | tf_op jit(solution)/shard_map/all_gather | solution.py:873
  10.6 6.5 %copy-start.8 = (bf16[128,1024]{1,0:T(8,128)(2,1)}, bf16[128,1024]{1,0:T(8,128)(2,1)S(1)}, u32[]{:S(2)}) copy-start(bf16[128,1024]{1,0:T(8,128)(2,1)S(1)} %fusion.49.normed) | copy-start | bytes 786436
  13.5 64.8 %all-gather.5.cloned.1.call-start = ((), (), s32[]{:S(2)}) async-start(), calls=%async_computation | async-start | bytes 2359296 | tf_op jit(solution)/shard_map/all_gather | solution.py:872
  13.7 102.5 %copy-start.40 = (s32[128]{0:T(128)}, s32[128]{0:T(128)S(1)}, u32[]{:S(2)}) copy-start(s32[128]{0:T(128)S(1)} %iota_add_fusion) | copy-start | bytes 1540
  13.8 102.5 %copy-start.43 = (s32[128]{0:T(128)}, s32[128]{0:T(128)S(1)}, u32[]{:S(2)}) copy-start(s32[128]{0:T(128)S(1)} %get-tuple-element.198) | copy-start | bytes 1540
  19.0 147.9 %all-gather.9.cloned.1.call-start = ((), (), s32[]{:S(2)}) async-start(), calls=%async_computation.2 | async-start | bytes 2359296 | tf_op jit(solution)/shard_map/all_gather | solution.py:964
  19.8 147.1 %all-gather.11.cloned.1.call-start = ((), (), s32[]{:S(2)}) async-start(), calls=%async_computation.3 | async-start | bytes 2359296 | tf_op jit(solution)/shard_map/all_gather | solution.py:965
  21.1 57.1 %copy-start.13 = (bf16[128,16,64]{0,2,1:T(8,128)(2,1)S(1)}, bf16[128,16,64]{0,2,1:T(8,128)(2,1)}, u32[]{:S(2)}) copy-start(bf16[128,16,64]{0,2,1:T(8,128)(2,1)} %maximum_convert_fusion) | copy-start | bytes 786436
  78.2 12.4 %copy-start.2 = (bf16[128,1024]{1,0:T(8,128)(2,1)S(1)}, bf16[128,1024]{1,0:T(8,128)(2,1)}, u32[]{:S(2)}) copy-start(bf16[128,1024]{1,0:T(8,128)(2,1)} %param.19) | copy-start | bytes 786436
  91.1 14.0 %copy-start.46 = (f32[128]{0:T(128)}, f32[128]{0:T(128)S(1)}, u32[]{:S(2)}) copy-start(f32[128]{0:T(128)S(1)} %get-tuple-element.234) | copy-start | bytes 1540
  91.4 4.5 %slice-start.3 = ((s8[5767168]{0:T(1024)(128)(4,1)}), s8[1572864]{0:T(1024)(128)(4,1)S(1)}, s32[]{:S(2)}) async-start(s8[5767168]{0:T(1024)(128)(4,1)} %bitcast.103), calls=%async_computation.7 | async-start | bytes 3145728
  91.4 5.8 %slice-start.4 = ((s8[5767168]{0:T(1024)(128)(4,1)}), s8[4194304]{0:T(1024)(128)(4,1)S(1)}, s32[]{:S(2)}) async-start(s8[5767168]{0:T(1024)(128)(4,1)} %bitcast.107), calls=%async_computation.8 | async-start | bytes 8388608
  95.9 5.1 %slice-start = ((s8[5767168]{0:T(1024)(128)(4,1)}), s8[4194304]{0:T(1024)(128)(4,1)S(1)}, s32[]{:S(2)}) async-start(s8[5767168]{0:T(1024)(128)(4,1)} %bitcast.101), calls=%async_computation.4 | async-start | bytes 8388608
  106.2 8.4 %copy-start.10 = (f32[128,16,64]{0,2,1:T(8,128)S(1)}, f32[128,16,64]{0,2,1:T(8,128)}, u32[]{:S(2)}) copy-start(f32[128,16,64]{0,2,1:T(8,128)} %copy-done.9) | copy-start | bytes 1572868
  108.4 7.8 %copy-start.6 = (bf16[1024,1024]{0,1:T(8,128)(2,1)S(1)}, bf16[1024,1024]{0,1:T(8,128)(2,1)}, u32[]{:S(2)}) copy-start(bf16[1024,1024]{0,1:T(8,128)(2,1)} %all-gather.5.cloned.1.call-done) | copy-start | bytes 6291460
  116.3 44.1 %copy-start.12 = (f32[128,1024]{1,0:T(8,128)S(1)}, f32[128,1024]{1,0:T(8,128)}, u32[]{:S(2)}) copy-start(f32[128,1024]{1,0:T(8,128)} %copy-done.11) | copy-start | bytes 1572868
  116.5 5.6 %copy-start.42 = (s32[128]{0:T(128)}, s32[128]{0:T(128)S(1)}, u32[]{:S(2)}) copy-start(s32[128]{0:T(128)S(1)} %get-tuple-element.77) | copy-start | bytes 1540 | tf_op jit(solution)/shard_map/cond
  116.5 5.6 %copy-start.45 = (s32[128]{0:T(128)}, s32[128]{0:T(128)S(1)}, u32[]{:S(2)}) copy-start(s32[128]{0:T(128)S(1)} %get-tuple-element.73) | copy-start | bytes 1540 | tf_op jit(solution)/shard_map/cond
  116.5 5.7 %copy-start.39 = (s32[1024]{0:T(1024)}, s32[1024]{0:T(1024)S(1)}, u32[]{:S(2)}) copy-start(s32[1024]{0:T(1024)S(1)} %get-tuple-element.76) | copy-start | bytes 12292 | tf_op jit(solution)/shard_map/cond
  132.0 29.1 %copy-start.14 = (bf16[128,2816]{1,0:T(8,128)(2,1)S(1)}, bf16[128,2816]{1,0:T(8,128)(2,1)}, u32[]{:S(2)}) copy-start(bf16[128,2816]{1,0:T(8,128)(2,1)} %get-tuple-element.211.act) | copy-start | bytes 2162692
  161.1 4.5 %copy-start.16 = (bf16[128,2816]{1,0:T(8,128)(2,1)S(1)}, bf16[128,2816]{1,0:T(8,128)(2,1)}, u32[]{:S(2)}) copy-start(bf16[128,2816]{1,0:T(8,128)(2,1)} %copy-done.15) | copy-start | bytes 2162692
  161.1 4.5 %copy-start.18 = (bf16[128,2816]{1,0:T(8,128)(2,1)S(1)}, bf16[128,2816]{1,0:T(8,128)(2,1)}, u32[]{:S(2)}) copy-start(bf16[128,2816]{1,0:T(8,128)(2,1)} %copy-done.17) | copy-start | bytes 2162692
  166.9 30.1 %copy-start.24 = (f32[128,16,64]{0,2,1:T(8,128)S(1)}, f32[128,16,64]{0,2,1:T(8,128)}, u32[]{:S(2)}) copy-start(f32[128,16,64]{0,2,1:T(8,128)} %convert_element_type.286) | copy-start | bytes 1572868
  166.9 30.1 %copy-start.34 = (f32[128,32]{0,1:T(8,128)S(1)}, f32[128,32]{0,1:T(8,128)}, u32[]{:S(2)}) copy-start(f32[128,32]{0,1:T(8,128)} %get-tuple-element.228) | copy-start | bytes 49156
  167.2 6.3 %copy-start.35 = (f32[1024,16]{0,1:T(8,128)}, f32[1024,16]{0,1:T(8,128)S(1)}, u32[]{:S(2)}) copy-start(f32[1024,16]{0,1:T(8,128)S(1)} %get-tuple-element.91) | copy-start | bytes 196612 | tf_op jit(solution)/shard_map/cond
  173.5 4.8 %copy-start.36 = (f32[1024,16]{0,1:T(8,128)S(1)}, f32[1024,16]{0,1:T(8,128)}, u32[]{:S(2)}) copy-start(f32[1024,16]{0,1:T(8,128)} %copy-done.35) | copy-start | bytes 196612 | tf_op jit(solution)/shard_map/cond
  178.2 9.8 %copy-start.26 = (bf16[1024,1024]{0,1:T(8,128)(2,1)S(1)}, bf16[1024,1024]{0,1:T(8,128)(2,1)}, u32[]{:S(2)}) copy-start(bf16[1024,1024]{0,1:T(8,128)(2,1)} %copy.54) | copy-start | bytes 6291460 | tf_op jit(solution)/shard_map/cond
  367.8 4.6 %copy-start.27 = (f32[128,1024]{1,0:T(8,128)S(1)}, f32[128,1024]{1,0:T(8,128)}, u32[]{:S(2)}) copy-start(f32[128,1024]{1,0:T(8,128)} %get-tuple-element.206) | copy-start | bytes 1572868
  367.8 4.6 %copy-start.51 = (f32[128]{0:T(128)S(1)}, f32[128]{0:T(128)}, u32[]{:S(2)}) copy-start(f32[128]{0:T(128)} %get-tuple-element.231) | copy-start | bytes 1540
  368.7 4.7 %copy-start.1 = (bf16[1024,1024]{1,0:T(8,128)(2,1)S(1)}, bf16[1024,1024]{1,0:T(8,128)(2,1)}, u32[]{:S(2)}) copy-start(bf16[1024,1024]{1,0:T(8,128)(2,1)} %param.26) | copy-start | bytes 6291460
  (30 other events, 62.2 us)
Sparse Core Ops, SparseCore 0:
  13.6 30.2 all-gather.6
  46.0 32.1 all-gather.4
  80.4 29.8 all-gather.8
  111.8 26.3 all-gather.10

commit v2 on v0

--- a/solution.py
+++ b/solution.py
@@ -1,8 +1,12 @@
+import functools
 import math
+import types
 
 import jax
 import jax.numpy as jnp
 from jax import lax
+from jax.experimental import pallas as pl
+from jax.experimental.pallas import tpu as pltpu
 from jax.sharding import PartitionSpec as P
 
 HEAD_DIM = 64
@@ -61,6 +65,847 @@
 def back(left, weight):
     return lax.dot_general(
         left, weight, (((1,), (1,)), ((), ())), preferred_element_type=jnp.float32
+    )
+
+
+TILE = 256
+LANES = 128
+GROUP = 16
+MESH = pl.DeviceIdType.MESH
+F32 = jnp.float32
+BF16 = jnp.bfloat16
+
+
+def remote(src, dst, send, recv, where):
+    return pltpu.make_async_remote_copy(
+        src_ref=src, dst_ref=dst, send_sem=send, recv_sem=recv, device_id=where, device_id_type=MESH
+    )
+
+
+def span(start, size, unit):
+    return pl.ds(pl.multiple_of(start, unit), size)
+
+
+def times(left, right):
+    return jnp.dot(left, right, preferred_element_type=F32)
+
+
+def iota(shape, dim):
+    return lax.broadcasted_iota(jnp.int32, shape, dim)
+
+
+def loop(low, high, body):
+    def turn(index, unused):
+        body(index)
+        return unused
+
+    lax.fori_loop(low, high, turn, 0)
+
+
+class Trade:
+    def __init__(self, blk, n_blk, phase, send, recv, source, place):
+        self.blk, self.n_blk = blk, n_blk
+        self.send, self.recv = send.at[phase], recv.at[phase]
+        self.source, self.place = source, place
+
+    def start(self, peer):
+        src, dst = self.source(peer), self.place(self.blk)
+
+        @pl.when(peer != self.blk)
+        def _():
+            remote(src, dst, self.send.at[peer], self.recv.at[self.blk], {"blk": peer}).start()
+
+        @pl.when(peer == self.blk)
+        def _():
+            pltpu.make_async_copy(src, dst, self.recv.at[self.blk]).start()
+
+    def arrived(self, peer):
+        src, dst = self.source(peer), self.place(peer)
+
+        @pl.when(peer != self.blk)
+        def _():
+            remote(src, dst, self.send.at[peer], self.recv.at[peer], {"blk": peer}).wait_recv()
+
+        @pl.when(peer == self.blk)
+        def _():
+            pltpu.make_async_copy(src, dst, self.recv.at[peer]).wait()
+
+    def all_arrived(self):
+        loop(0, self.n_blk, self.arrived)
+
+    def all_left(self):
+        def left(peer):
+            @pl.when(peer != self.blk)
+            def _():
+                remote(
+                    self.source(peer), self.place(self.blk), self.send.at[peer], self.recv.at[self.blk], {"blk": peer}
+                ).wait_send()
+
+        loop(0, self.n_blk, left)
+
+
+class Gift:
+    def __init__(self, seq, n_seq, rows, owner, kind, src, dst, send, recv):
+        self.seq, self.n_seq, self.rows, self.owner, self.kind = seq, n_seq, rows, owner, kind
+        self.src, self.dst, self.send, self.recv = src, dst, send, recv
+
+    def copy(self, other, send):
+        dst = self.dst.at[span(other * self.rows, self.rows, self.rows)]
+        return remote(self.src, dst, self.send.at[self.kind, send], self.recv.at[self.kind, other], {"seq": send})
+
+    def own(self):
+        dst = self.dst.at[pl.ds(self.owner * self.rows, self.rows)]
+        return pltpu.make_async_copy(self.src, dst, self.recv.at[self.kind, self.owner])
+
+    def start(self):
+        @pl.when(self.seq != self.owner)
+        def _():
+            self.copy(self.seq, self.owner).start()
+
+        @pl.when(self.seq == self.owner)
+        def _():
+            self.own().start()
+
+    def arrived(self):
+        for other in range(self.n_seq):
+            if other == self.owner:
+                self.own().wait()
+            else:
+                self.copy(other, other).wait_recv()
+
+    def left(self):
+        @pl.when(self.seq != self.owner)
+        def _():
+            self.copy(self.seq, self.owner).wait_send()
+
+
+class Sum:
+    def __init__(self, blk, n_blk, size, part, cgot, zgot, total, sems):
+        self.blk, self.chips, self.size = blk, n_blk // 2, size
+        self.core, self.chip = lax.rem(blk, 2), lax.div(blk, 2)
+        self.part, self.cgot, self.zgot, self.total = part, cgot, zgot, total
+        self.csend, self.crecv, self.zsend, self.zrecv = sems
+
+    def turned(self, step):
+        return lax.rem(self.chip + step, self.chips)
+
+    def chunk(self, index):
+        return self.part.at[span(index * self.size, self.size, 32)]
+
+    def swap(self, chip):
+        return remote(
+            self.chunk(2 * chip + 1 - self.core),
+            self.cgot(chip),
+            self.csend.at[chip],
+            self.crecv.at[chip],
+            {"blk": 2 * self.chip + 1 - self.core},
+        )
+
+    def forward(self, step):
+        chip = self.turned(step)
+        return remote(
+            self.chunk(2 * chip + self.core),
+            self.zgot(step - 1),
+            self.zsend.at[step - 1],
+            self.zrecv.at[step - 1],
+            {"blk": 2 * chip + self.core},
+        )
+
+    def begin(self):
+        def one(step):
+            chip = self.turned(step)
+            self.swap(chip).wait()
+            mine, other = self.chunk(2 * chip + self.core), self.cgot(chip)
+
+            def add(group):
+                at = span(group * 32, 32, 32)
+                mine[at, :] = (mine[at, :].astype(F32) + other[at, :].astype(F32)).astype(BF16)
+
+            loop(0, self.size // 32, add)
+            self.forward(step).start()
+
+        loop(1, self.chips, one)
+        self.swap(self.chip).wait()
+
+    def end(self):
+        loop(1, self.chips, lambda step: self.forward(step).wait())
+        mine, other = self.chunk(self.blk), self.cgot(self.chip)
+
+        def add(group):
+            at = span(group * 32, 32, 32)
+            value = mine[at, :].astype(F32) + other[at, :].astype(F32)
+            for step in range(1, self.chips):
+                value = value + self.zgot(step - 1)[at, :].astype(F32)
+            self.total[at, :] = value.astype(BF16)
+
+        loop(0, self.size // 32, add)
+
+
+class Spread:
+    def __init__(self, seq, n_seq, owner, kind, src, dst, send, recv, local):
+        self.seq, self.n_seq, self.owner, self.kind, self.src, self.dst = seq, n_seq, owner, kind, src, dst
+        self.send, self.recv, self.local = send, recv, local
+
+    def copy(self, other):
+        return remote(self.src, self.dst, self.send.at[self.kind, other], self.recv.at[self.kind], {"seq": other})
+
+    def own(self):
+        return pltpu.make_async_copy(self.src, self.dst, self.local.at[self.kind])
+
+    def start(self):
+        @pl.when(self.seq == self.owner)
+        def _():
+            for other in range(self.n_seq):
+                if other != self.owner:
+                    self.copy(other).start()
+            self.own().start()
+
+    def finish(self):
+        @pl.when(self.seq == self.owner)
+        def _():
+            for other in range(self.n_seq):
+                if other != self.owner:
+                    self.copy(other).wait_send()
+            self.own().wait()
+
+        @pl.when(self.seq != self.owner)
+        def _():
+            self.copy(self.owner).wait_recv()
+
+
+def outer_tiles(lhs, rhs, part, turned, chip, tiles, part_at):
+    turned[...] = lhs[:, span(chip * TILE, TILE, TILE)].T
+
+    def tile(index):
+        value = times(turned[...], rhs[:, span(index * TILE, TILE, TILE)])
+        part[span(chip * TILE, TILE, TILE), span(part_at + index * TILE, TILE, TILE)] = value.astype(BF16)
+
+    loop(0, tiles, tile)
+
+
+def layer_kernel(
+    sizes,
+    freq, tokens, first, lengths, attn_gain, ffn_gain, cot,
+    h_query, h_key, h_value, h_out, h_gate, h_up, h_down,
+    o_layer, o_tokens, o_first, o_gu, o_down, o_out, o_query, o_key, o_value, o_gain,
+    v, sem,
+):
+    rows, width, ff, n_seq, n_blk, split = sizes
+    v, sem = types.SimpleNamespace(**v), types.SimpleNamespace(**sem)
+    docs = lengths.shape[1]
+    chips = n_blk // 2
+    scale = HEAD_DIM ** (-0.5)
+    seq, blk = lax.axis_index("seq"), lax.axis_index("blk")
+    chip_at = lax.div(blk, 2)
+
+    def turned_chip(step):
+        return lax.rem(chip_at + step, chips)
+
+    barrier = pltpu.get_barrier_semaphore()
+    for step in range(1, n_seq):
+        pl.semaphore_signal(barrier, inc=1, device_id={"seq": lax.rem(seq + step, n_seq)}, device_id_type=MESH)
+    for step in range(1, n_blk):
+        pl.semaphore_signal(barrier, inc=1, device_id={"blk": lax.rem(blk + step, n_blk)}, device_id_type=MESH)
+
+    def load(index, src, dst):
+        copy = pltpu.make_async_copy(src, dst, sem.load.at[index])
+        copy.start()
+        return copy
+
+    load_query = load(0, h_query, v.w_query)
+    load_key = load(1, h_key, v.w_key)
+    load_value = load(2, h_value, v.w_value)
+    load_out = load(3, h_out, v.w_out)
+    load_gate = load(4, h_gate, v.w_gate)
+    load_up = load(5, h_up, v.w_up)
+    load_down = load(6, h_down, v.w_down)
+
+    def norm(group):
+        at = span(group * GROUP, GROUP, GROUP)
+        x = tokens[at, :].astype(F32)
+        inv = lax.rsqrt(jnp.mean(x * x, axis=-1, keepdims=True) + EPS)
+        v.normed[at, :] = (x * inv * attn_gain[...]).astype(BF16)
+        v.inv_first[at, :] = jnp.broadcast_to(inv, (GROUP, LANES))
+
+    loop(0, rows // GROUP, norm)
+
+    def doc_start(index):
+        start, end = jnp.zeros_like(index), jnp.int32(0)
+        for doc in range(docs):
+            end = end + lengths[0, doc]
+            start = jnp.where(index >= end, end, start)
+        return start
+
+    my_index = blk * rows + iota((rows, LANES), 0)
+    low_half = lax.rem(iota((rows, LANES), 1), HEAD_DIM) < HEAD_DIM // 2
+    angle = (my_index - doc_start(my_index)).astype(F32) * freq[...]
+    v.cos[...] = jnp.cos(angle)
+    sine = jnp.sin(angle)
+    v.sin[...] = jnp.where(low_half, -sine, sine)
+
+    def halves_changed(u):
+        half = HEAD_DIM // 2
+        return jnp.where(low_half, pltpu.roll(u, LANES - half, 1), pltpu.roll(u, half, 1))
+
+    def rotated(u):
+        return u * v.cos[...] + halves_changed(u) * v.sin[...]
+
+    def rotated_back(u):
+        return u * v.cos[...] - halves_changed(u) * v.sin[...]
+
+    cuts = [0]
+    for tiles in split:
+        cuts.append(cuts[-1] + tiles * TILE)
+    wide = max(split) * TILE
+
+    def gift(owner, kind, src, dst):
+        return Gift(seq, n_seq, rows, owner, kind, src, dst, sem.xsend, sem.xrecv)
+
+    gift_cot = gift(3, 0, cot, v.buf_a)
+    gifts_two = [gift(owner, 0, v.two, v.buf_a) for owner in range(3)]
+    gifts_gu = [
+        gift(
+            owner,
+            1,
+            v.gate_up.at[:, cuts[owner] : cuts[owner + 1]],
+            v.buf_b.at[:, : cuts[owner + 1] - cuts[owner]],
+        )
+        for owner in range(3)
+    ]
+    gift_act = gift(3, 1, v.act, v.buf_b)
+    gift_att = gift(2, 2, v.att, v.buf_att)
+    gift_mid = gift(2, 3, v.mid_b, v.buf_mid)
+    gifts_normed = [gift(owner, 4, v.normed, v.buf_n) for owner in range(3)]
+    gifts_pre = [gift(owner, 5, v.pre_grad.at[owner], v.buf_t) for owner in range(3)]
+
+    def trade(phase, source, place):
+        return Trade(blk, n_blk, phase, sem.asend, sem.arecv, source, place)
+
+    def block_rows(ref):
+        return lambda peer: ref.at[span(peer * rows, rows, rows)]
+
+    def block_columns(ref):
+        return lambda peer: ref.at[:, span(peer * LANES, LANES, LANES)]
+
+    give_qkv = trade(0, lambda peer: v.pack.at[peer], lambda peer: v.qkv.at[:, span(peer * rows, rows, rows)])
+    give_att = trade(1, block_rows(v.ob), block_columns(v.att))
+    give_out = trade(2, lambda peer: v.out_pack.at[peer], block_rows(v.out_grad))
+    give_grads = trade(
+        3, lambda peer: v.pack.at[peer], lambda peer: v.grads.at[:, :, span(peer * LANES, LANES, LANES)]
+    )
+
+    pl.semaphore_wait(barrier, n_seq + n_blk - 2)
+
+    for item in (load_query, load_key, load_value):
+        item.wait()
+
+    def project(step):
+        chip = turned_chip(step)
+        at = span(chip * TILE, TILE, TILE)
+        left = v.normed[...]
+        q, k, val = times(left, v.w_query[:, at]), times(left, v.w_key[:, at]), times(left, v.w_value[:, at])
+        old = first[:, at].astype(F32)
+        for core in range(2):
+            peer = 2 * chip + core
+            cols = slice(core * LANES, (core + 1) * LANES)
+            v.pack[peer, 0] = (rotated(q[:, cols]) * scale).astype(BF16)
+            v.pack[peer, 1] = rotated(k[:, cols]).astype(BF16)
+            v.pack[peer, 2] = (MIX * val[:, cols] + MIX * old[:, cols]).astype(BF16)
+            give_qkv.start(peer)
+
+    loop(1, chips + 1, project)
+    gift_cot.start()
+    for item in gifts_normed:
+        item.start()
+
+    first_head = iota((TILE, LANES), 1) < HEAD_DIM
+
+    def stacked(values):
+        return jnp.concatenate([jnp.where(first_head, values, 0.0), jnp.where(first_head, 0.0, values)], axis=0)
+
+    def unstacked(values):
+        return jnp.where(first_head, values[:TILE], values[TILE:])
+
+    def attend(block):
+        for core in range(2):
+            give_qkv.arrived(2 * block + core)
+        at, both = span(block * TILE, TILE, TILE), span(block * 2 * TILE, 2 * TILE, 2 * TILE)
+        v.q2[both, :] = stacked(v.qkv[0, at, :].astype(F32)).astype(BF16)
+        index = block * TILE + lax.rem(iota((2 * TILE, 1), 0), TILE)
+        start = doc_start(index)
+        v.top[...] = jnp.full((2 * TILE, LANES), NEG, F32)
+
+        def scores(tile):
+            cols = span(tile * TILE, TILE, TILE)
+            score = back(v.q2[both, :], v.qkv[1, cols, :])
+            key = tile * TILE + iota((2 * TILE, TILE), 1)
+            score = jnp.where((key <= index) & (key >= start), score, NEG)
+            v.score[:, cols] = score
+            v.top[...] = jnp.maximum(v.top[...], jnp.maximum(score[:, :LANES], score[:, LANES:]))
+
+        loop(0, block + 1, scores)
+        top = jnp.max(v.top[...], axis=1, keepdims=True)
+        v.top[...] = jnp.zeros((2 * TILE, LANES), F32)
+        v.o2[...] = jnp.zeros((2 * TILE, LANES), F32)
+
+        def weights(tile):
+            cols = span(tile * TILE, TILE, TILE)
+            weight = jnp.exp(v.score[:, cols] - top)
+            v.top[...] += weight[:, :LANES] + weight[:, LANES:]
+            weight = weight.astype(BF16)
+            v.prob[both, cols] = weight
+            v.o2[...] += times(weight, v.qkv[2, cols, :])
+
+        loop(0, block + 1, weights)
+        inv = 1.0 / jnp.sum(v.top[...], axis=1, keepdims=True)
+        v.row[both, :] = jnp.broadcast_to(inv, (2 * TILE, LANES))
+        attended = unstacked(v.o2[...] * inv)
+        v.o32[at, :] = attended
+        v.ob[at, :] = attended.astype(BF16)
+        for core in range(2):
+            give_att.start(2 * block + core)
+
+    loop(0, chips, attend)
+    give_att.all_arrived()
+    gift_att.start()
+
+    load_out.wait()
+
+    def middle(tile):
+        cols = span(tile * TILE, TILE, TILE)
+        value = tokens[:, cols].astype(F32) + times(v.att[...], v.w_out[:, cols])
+        v.mid[:, cols] = value
+        o_layer[:, cols] = value
+
+    loop(0, width // TILE, middle)
+
+    def norm_two(group):
+        at = span(group * GROUP, GROUP, GROUP)
+        x = v.mid[at, :]
+        inv = lax.rsqrt(jnp.mean(x * x, axis=-1, keepdims=True) + EPS)
+        v.two[at, :] = (x * inv * ffn_gain[...]).astype(BF16)
+        v.inv_second[at, :] = jnp.broadcast_to(inv, (GROUP, LANES))
+
+    loop(0, rows // GROUP, norm_two)
+    for item in gifts_two:
+        item.start()
+
+    for item in (load_gate, load_up, load_down):
+        item.wait()
+    v.two_grad[...] = jnp.zeros((rows, width), F32)
+
+    def feed(tile):
+        cols = span(tile * TILE, TILE, TILE)
+        gate = times(v.two[...], v.w_gate[:, cols])
+        up = times(v.two[...], v.w_up[:, cols])
+        act_grad = back(cot[...], v.w_down[cols, :])
+        sigma = jax.nn.sigmoid(gate)
+        silu = gate * sigma
+        act = (silu * up).astype(BF16)
+        gate_grad = (act_grad * up * sigma * (1.0 + gate * (1.0 - sigma))).astype(BF16)
+        up_grad = (act_grad * silu).astype(BF16)
+        v.act[:, cols] = act
+        v.gate_up[:, cols] = gate_grad
+        v.gate_up[:, span(ff + tile * TILE, TILE, TILE)] = up_grad
+        o_layer[...] += times(act, v.w_down[cols, :])
+        v.two_grad[...] += back(gate_grad, v.w_gate[:, cols]) + back(up_grad, v.w_up[:, cols])
+
+    loop(0, ff // TILE, feed)
+    v.gain_rows[...] = jnp.zeros((16, width), F32)
+
+    def norm_two_back(group):
+        at = span(group * GROUP, GROUP, GROUP)
+        x, grad, inv = v.mid[at, :], v.two_grad[at, :], v.inv_second[at, :1]
+        term = grad * x * inv
+        v.gain_rows[8:16, :] += term[:8] + term[8:]
+        scaled = grad * ffn_gain[...]
+        mean = jnp.mean(scaled * x, axis=-1, keepdims=True)
+        value = cot[at, :].astype(F32) + inv * scaled - x * (inv * inv * inv * mean)
+        v.mid_grad[at, :] = value
+        v.mid_b[at, :] = value.astype(BF16)
+
+    loop(0, rows // GROUP, norm_two_back)
+
+    def out_back(step):
+        chip = turned_chip(step)
+        value = back(v.mid_b[...], v.w_out[span(chip * TILE, TILE, TILE), :]).astype(BF16)
+        for core in range(2):
+            v.out_pack[2 * chip + core] = value[:, core * LANES : (core + 1) * LANES]
+            give_out.start(2 * chip + core)
+
+    loop(1, chips + 1, out_back)
+    for item in gifts_gu + [gift_act, gift_mid]:
+        item.start()
+
+    give_out.all_arrived()
+
+    def prepare(block):
+        at, both = span(block * TILE, TILE, TILE), span(block * 2 * TILE, 2 * TILE, 2 * TILE)
+        grad = (stacked(v.out_grad[at, :].astype(F32)) * v.row[both, :]).astype(BF16)
+        v.do2[both, :] = grad
+        attended = v.o32[at, :]
+        delta = jnp.sum(grad.astype(F32) * jnp.concatenate([attended, attended], axis=0), axis=1, keepdims=True)
+        v.row[both, :] = jnp.broadcast_to(delta, (2 * TILE, LANES))
+        v.dq[both, :] = jnp.zeros((2 * TILE, LANES), F32)
+
+    loop(0, chips, prepare)
+    give_qkv.all_left()
+
+    def key_block(block):
+        at = span(block * TILE, TILE, TILE)
+        v.dk[...] = jnp.zeros((TILE, LANES), F32)
+        v.dv[...] = jnp.zeros((TILE, LANES), F32)
+
+        def query_block(other):
+            both = span(other * 2 * TILE, 2 * TILE, 2 * TILE)
+            prob = v.prob[both, at]
+            grad = back(v.do2[both, :], v.qkv[2, at, :])
+            score_grad = (prob.astype(F32) * (grad - v.row[both, :1])).astype(BF16)
+            v.dk[...] += outer(score_grad, v.q2[both, :])
+            v.dv[...] += outer(prob, v.do2[both, :])
+            v.dq[both, :] += times(score_grad, v.qkv[1, at, :])
+
+        loop(block, chips, query_block)
+        dq = (unstacked(v.dq[span(block * 2 * TILE, 2 * TILE, 2 * TILE), :]) * scale).astype(BF16)
+        dk, dv = v.dk[...].astype(BF16), v.dv[...].astype(BF16)
+        for core in range(2):
+            peer = 2 * block + core
+            part = slice(core * rows, (core + 1) * rows)
+            v.pack[peer, 0] = dq[part]
+            v.pack[peer, 1] = dk[part]
+            v.pack[peer, 2] = dv[part]
+            give_grads.start(peer)
+
+    loop(0, chips, key_block)
+
+    chunk, down = width // n_blk, ff // n_blk
+    sems = tuple(item.at[0] for item in (sem.csend, sem.crecv, sem.zsend, sem.zrecv))
+    tail_sems = tuple(item.at[1] for item in (sem.csend, sem.crecv, sem.zsend, sem.zrecv))
+
+    def stack_in(ref, size, columns, top):
+        return lambda index: ref.at[span(top + index * size, size, 32), :columns]
+
+    def square_in(ref):
+        def place(index):
+            return ref.at[
+                span(lax.rem(index, 2) * down, down, 32), span(lax.div(index, 2) * width, width, width)
+            ]
+
+        return place
+
+    part = v.w_gate.at[:, :wide]
+    sum_gu = Sum(
+        blk, n_blk, chunk, part,
+        stack_in(v.w_up, chunk, wide, 0), stack_in(v.w_up, chunk, wide, chips * chunk), v.total, sems,
+    )
+    sum_down = Sum(
+        blk, n_blk, down, v.w_down, square_in(v.w_up), square_in(v.w_gate), v.total_down, sems
+    )
+    sum_tail = Sum(
+        blk, n_blk, chunk, v.w_out,
+        stack_in(v.got_tail, chunk, width, 0), stack_in(v.got_tail, chunk, width, chips * chunk),
+        v.total_tail, tail_sems,
+    )
+    early = [[gifts_two[0], gifts_gu[0]], [gifts_two[1], gifts_gu[1]], [gifts_two[2], gifts_gu[2], gift_att, gift_mid],
+             [gift_cot, gift_act]]
+    for owner in range(n_seq):
+
+        @pl.when(seq == owner)
+        def _(owner=owner):
+            for item in early[owner]:
+                item.arrived()
+
+    @pl.when(seq < 3)
+    def _():
+        def one(step):
+            chip = turned_chip(step)
+
+            @pl.when(seq < 2)
+            def _():
+                outer_tiles(v.buf_a, v.buf_b, v.w_gate, v.turned, chip, split[0], 0)
+
+            @pl.when(seq == 2)
+            def _():
+                spare = wide - split[2] * TILE - width
+                if spare:
+                    v.w_gate[span(chip * TILE, TILE, TILE), wide - spare : wide] = jnp.zeros((TILE, spare), BF16)
+                outer_tiles(v.buf_a, v.buf_b, v.w_gate, v.turned, chip, split[2], 0)
+                outer_tiles(
+                    v.buf_att, v.buf_mid, v.w_gate, v.turned, chip, width // TILE, split[2] * TILE
+                )
+
+            sum_gu.swap(chip).start()
+
+        loop(1, chips + 1, one)
+        sum_gu.begin()
+
+    @pl.when(seq == 3)
+    def _():
+        def one(index):
+            at = span(index * TILE, TILE, TILE)
+            v.turned[...] = v.buf_b[:, at].T
+            v.w_down[at, :] = times(v.turned[...], v.buf_a[...]).astype(BF16)
+
+        loop(0, ff // TILE, one)
+        loop(1, chips + 1, lambda step: sum_down.swap(turned_chip(step)).start())
+        sum_down.begin()
+
+    give_grads.all_arrived()
+
+    def rotate_back(index):
+        cols = span(index * LANES, LANES, LANES)
+        v.pre_grad[0, :, cols] = rotated_back(v.grads[0, :, cols].astype(F32)).astype(BF16)
+        v.pre_grad[1, :, cols] = rotated_back(v.grads[1, :, cols].astype(F32)).astype(BF16)
+        value = MIX * v.grads[2, :, cols].astype(F32)
+        v.pre_grad[2, :, cols] = value.astype(BF16)
+        o_first[:, cols] = value
+
+    loop(0, width // LANES, rotate_back)
+    for item in gifts_pre:
+        item.start()
+
+    def normed_back(tile):
+        at = span(tile * TILE, TILE, TILE)
+        o_tokens[:, at] = (
+            back(v.pre_grad[0], v.w_query[at, :])
+            + back(v.pre_grad[1], v.w_key[at, :])
+            + back(v.pre_grad[2], v.w_value[at, :])
+        )
+
+    loop(0, width // TILE, normed_back)
+
+    def norm_back(group):
+        at = span(group * GROUP, GROUP, GROUP)
+        x, grad, inv = tokens[at, :].astype(F32), o_tokens[at, :], v.inv_first[at, :1]
+        term = grad * x * inv
+        v.gain_rows[0:8, :] += term[:8] + term[8:]
+        scaled = grad * attn_gain[...]
+        mean = jnp.mean(scaled * x, axis=-1, keepdims=True)
+        o_tokens[at, :] = v.mid_grad[at, :] + inv * scaled - x * (inv * inv * inv * mean)
+
+    loop(0, rows // GROUP, norm_back)
+
+    for peer in range(n_blk):
+        v.gains[peer] = v.gain_rows[:, peer * LANES : (peer + 1) * LANES]
+
+    def gain_copy(step):
+        other = lax.rem(blk + step, n_blk)
+        return remote(
+            v.gains.at[other], v.gain_got.at[step - 1], sem.hsend.at[step - 1], sem.hrecv.at[step - 1],
+            {"blk": other},
+        )
+
+    for step in range(1, n_blk):
+        gain_copy(step).start()
+
+    for owner in range(3):
+
+        @pl.when(seq == owner)
+        def _(owner=owner):
+            gifts_normed[owner].arrived()
+            gifts_pre[owner].arrived()
+
+    @pl.when(seq < 3)
+    def _():
+        def one(step):
+            chip = turned_chip(step)
+            outer_tiles(v.buf_n, v.buf_t, v.w_out, v.turned, chip, width // TILE, 0)
+            sum_tail.swap(chip).start()
+
+        loop(1, chips + 1, one)
+        sum_tail.begin()
+
+    def spread(owner, kind, src, dst):
+        return Spread(seq, n_seq, owner, kind, src, dst, sem.gsend, sem.grecv, sem.glocal)
+
+    last = cuts[3] - cuts[2]
+    spreads = [
+        spread(0, 0, v.total.at[:, : cuts[1] - cuts[0]], o_gu.at[:, cuts[0] : cuts[1]]),
+        spread(1, 1, v.total.at[:, : cuts[2] - cuts[1]], o_gu.at[:, cuts[1] : cuts[2]]),
+        spread(2, 2, v.total.at[:, :last], o_gu.at[:, cuts[2] : cuts[3]]),
+        spread(2, 3, v.total.at[:, last : last + width], o_out),
+        spread(3, 4, v.total_down, o_down),
+    ]
+    tails = [
+        spread(0, 5, v.total_tail, o_query),
+        spread(1, 6, v.total_tail, o_key),
+        spread(2, 7, v.total_tail, o_value),
+    ]
+
+    @pl.when(seq < 3)
+    def _():
+        sum_gu.end()
+
+    @pl.when(seq == 3)
+    def _():
+        sum_down.end()
+
+    for item in spreads:
+        item.start()
+
+    value = v.gains[blk]
+    for step in range(1, n_blk):
+        gain_copy(step).wait()
+        value = value + v.gain_got[step - 1]
+    v.gain_sum[seq] = value
+    for step in range(1, n_seq):
+        other = lax.rem(seq + step, n_seq)
+        mine = v.gain_sum.at[seq]
+        remote(mine, mine, sem.isend.at[step - 1], sem.irecv.at[seq], {"seq": other}).start()
+
+    @pl.when(seq < 3)
+    def _():
+        sum_tail.end()
+
+    for item in tails:
+        item.start()
+
+    for step in range(1, n_seq):
+        other = lax.rem(seq + step, n_seq)
+        theirs = v.gain_sum.at[other]
+        remote(theirs, theirs, sem.isend.at[step - 1], sem.irecv.at[other], {"seq": other}).wait()
+    value = v.gain_sum[0]
+    for group in range(1, n_seq):
+        value = value + v.gain_sum[group]
+    o_gain[0:8, :] = jnp.broadcast_to(jnp.sum(value[:8], axis=0, keepdims=True), (8, LANES))
+    o_gain[8:16, :] = jnp.broadcast_to(jnp.sum(value[8:], axis=0, keepdims=True), (8, LANES))
+
+    for item in spreads + tails:
+        item.finish()
+    for item in (
+        [gift_cot, gift_act, gift_att, gift_mid] + gifts_two + gifts_gu + gifts_normed + gifts_pre
+    ):
+        item.left()
+    for item in (give_att, give_out, give_grads):
+        item.all_left()
+
+
+def tile_split(width, ff):
+    tiles, more = 2 * ff // TILE, width // TILE
+    each = -(-(tiles + more) // 3)
+    return (each, each, tiles - 2 * each)
+
+
+def fits(n_seq, n_blk, rows, width, ff):
+    return (
+        n_seq == 4
+        and n_blk % 2 == 0
+        and n_blk * LANES == width
+        and rows == LANES
+        and ff % TILE == 0
+        and (ff // n_blk) % 32 == 0
+        and 2 * (ff // n_blk) <= width
+        and n_blk // 2 <= 4
+    )
+
+
+def local_fast(
+    n_seq,
+    n_blk,
+    tokens,
+    first_values,
+    doc_lengths,
+    attn_gain,
+    query_weight,
+    key_weight,
+    value_weight,
+    out_weight,
+    ffn_gain,
+    gate_weight,
+    up_weight,
+    down_weight,
+    cotangent,
+):
+    rows, width = tokens.shape
+    ff = gate_weight.shape[1]
+    split = tile_split(width, ff)
+    sizes = (rows, width, ff, n_seq, n_blk, split)
+    half = HEAD_DIM // 2
+    freq = THETA ** (-(jnp.arange(half).astype(jnp.float32) * 2.0 / HEAD_DIM))
+    freq = jnp.tile(freq, LANES // half)[None, :]
+    wide = max(split) * TILE
+    chunk, down, chips = width // n_blk, ff // n_blk, n_blk // 2
+    all_rows, group = n_seq * rows, n_blk * rows
+    vmem = pl.BlockSpec(memory_space=pltpu.VMEM)
+    hbm = pl.BlockSpec(memory_space=pl.ANY)
+    smem = pl.BlockSpec(memory_space=pltpu.SMEM)
+    shape = jax.ShapeDtypeStruct
+
+    def half_type(*dims):
+        return pltpu.VMEM(dims, BF16)
+
+    def full_type(*dims):
+        return pltpu.VMEM(dims, F32)
+
+    scratch = dict(
+        w_query=half_type(width, width), w_key=half_type(width, width), w_value=half_type(width, width),
+        w_out=half_type(width, width), w_gate=half_type(width, ff), w_up=half_type(width, ff),
+        w_down=half_type(ff, width),
+        normed=half_type(rows, width), inv_first=full_type(rows, LANES), inv_second=full_type(rows, LANES),
+        cos=full_type(rows, LANES), sin=full_type(rows, LANES),
+        pack=half_type(n_blk, 3, rows, LANES), qkv=half_type(3, group, LANES),
+        q2=half_type(2 * group, LANES), do2=half_type(2 * group, LANES), prob=half_type(2 * group, group),
+        score=full_type(2 * TILE, group), top=full_type(2 * TILE, LANES), o2=full_type(2 * TILE, LANES),
+        row=full_type(2 * group, LANES), o32=full_type(group, LANES), ob=half_type(group, LANES),
+        dq=full_type(2 * group, LANES), dk=full_type(TILE, LANES), dv=full_type(TILE, LANES),
+        att=half_type(rows, width), mid=full_type(rows, width), two=half_type(rows, width),
+        act=half_type(rows, ff), gate_up=half_type(rows, 2 * ff), two_grad=full_type(rows, width),
+        mid_grad=full_type(rows, width), mid_b=half_type(rows, width),
+        out_pack=half_type(n_blk, rows, LANES), out_grad=half_type(group, LANES),
+        grads=half_type(3, rows, width), pre_grad=half_type(3, rows, width),
+        buf_a=half_type(all_rows, width), buf_b=half_type(all_rows, ff), buf_att=half_type(all_rows, width),
+        buf_mid=half_type(all_rows, width), buf_n=half_type(all_rows, width), buf_t=half_type(all_rows, width),
+        turned=half_type(TILE, all_rows),
+        got_tail=half_type((2 * chips - 1) * chunk, width),
+        total=half_type(chunk, wide), total_down=half_type(down, width), total_tail=half_type(chunk, width),
+        gain_rows=full_type(16, width), gains=full_type(n_blk, 16, LANES), gain_got=full_type(n_blk - 1, 16, LANES),
+        gain_sum=full_type(n_seq, 16, LANES),
+    )
+    dma = pltpu.SemaphoreType.DMA
+    sems = dict(
+        load=dma((7,)), asend=dma((4, n_blk)), arecv=dma((4, n_blk)), xsend=dma((6, n_seq)), xrecv=dma((6, n_seq)),
+        csend=dma((2, chips)), crecv=dma((2, chips)), zsend=dma((2, chips - 1)), zrecv=dma((2, chips - 1)),
+        gsend=dma((8, n_seq)), grecv=dma((8,)), glocal=dma((8,)),
+        hsend=dma((n_blk - 1,)), hrecv=dma((n_blk - 1,)), isend=dma((n_seq - 1,)), irecv=dma((n_seq,)),
+    )
+    layer, grad_tokens, grad_first, out_gu, out_down, out_out, out_query, out_key, out_value, out_gain = pl.pallas_call(
+        functools.partial(layer_kernel, sizes),
+        out_shape=(
+            shape((rows, width), F32),
+            shape((rows, width), F32),
+            shape((rows, width), F32),
+            shape((chunk, 2 * ff), BF16),
+            shape((down, width), BF16),
+            shape((chunk, width), BF16),
+            shape((chunk, width), BF16),
+            shape((chunk, width), BF16),
+            shape((chunk, width), BF16),
+            shape((16, LANES), F32),
+        ),
+        in_specs=[vmem, vmem, vmem, smem, vmem, vmem, vmem] + [hbm] * 7,
+        out_specs=(vmem, vmem, vmem) + (hbm,) * 6 + (vmem,),
+        scratch_shapes=(scratch, sems),
+        compiler_params=pltpu.CompilerParams(
+            collective_id=0, has_side_effects=True, vmem_limit_bytes=63 * 1024 * 1024
+        ),
+        name="layer",
+    )(
+        freq, tokens, first_values, doc_lengths, attn_gain[None, :], ffn_gain[None, :], cotangent,
+        query_weight, key_weight, value_weight, out_weight, gate_weight, up_weight, down_weight,
+    )
+    return (
+        layer,
+        grad_tokens,
+        grad_first,
+        out_gain[0],
+        out_query.astype(F32),
+        out_key.astype(F32),
+        out_value.astype(F32),
+        out_out.astype(F32),
+        out_gain[8],
+        out_gu[:, :ff].astype(F32),
+        out_gu[:, ff:].astype(F32),
+        out_down.astype(F32),
     )
 
 
@@ -340,8 +1185,16 @@
 
 
 def solution(mesh):
+    n_seq, n_blk = mesh.shape["seq"], mesh.shape["blk"]
+
+    def chosen(*args):
+        rows, width = args[0].shape
+        if fits(n_seq, n_blk, rows, width, args[9].shape[1]):
+            return local_fast(n_seq, n_blk, *args)
+        return local(*args)
+
     return jax.shard_map(
-        local,
+        chosen,
         mesh=mesh,
         in_specs=(
             P(("seq", "blk"), None),

time: 831 us -> 204 us (0.25); the launches traced: 821 us -> 204 us
  waiting for transfers between devices: 573 us -> 0 us
  Pallas kernels: 0 us -> 191 us
  matrix products: 111 us -> 0 us
  blocking collectives: 50.8 us -> 0 us
  other arithmetic: 48 us -> 7.8 us
  between operations: 16.9 us -> 0.69 us
  local copies, waits for them, and re-layouts: 20 us -> 4.28 us
    reduce_scatter x7 -> x0, waiting for transfers between devices: 466 us -> none  [the longest x1 119 us: local(): lax.psum_scatter(grad_down, 'blk', scatter_dimension=0, tiled=True)]
    pallas_call x0 -> x1, Pallas kernels: none -> 191 us  [local_fast(): pl.pallas_call(functools.partial(layer_kernel, sizes), out_shape=(shape((...]
    dot_general x28 -> x0, matrix products: 111 us -> none  [the longest x7 33.5 us: outer(): lax.dot_general(left, right, (((0,), (0,)), ((), ())), preferred_element_...]
    psum x1 -> x0, waiting for transfers between devices: 56.1 us -> none  [local(): lax.psum(summed[1].astype(jnp.bfloat16), 'seq').astype(jnp.float32)]
    all_gather x4 -> x0, waiting for transfers between devices: 50.7 us -> none  [the longest x1 30.4 us: local(): lax.all_gather(keys, 'blk', axis=0, tiled=True)]
    all_gather x2 -> x0, blocking collectives: 27.7 us -> none  [the longest x1 15.6 us: local(): lax.all_gather(logsum.T, 'blk', axis=0, tiled=True)]
    convert_element_type x23 -> x6, other arithmetic: 30.6 us -> 7.79 us  [the longest x1 3.16 us: local_fast(): out_gu[:, ff:].astype(F32)]
    unnamed x1 -> x0, blocking collectives: 13.3 us -> none
  transfers between devices with their start and end apart: 12 -> 0, of which waited for: 9 -> 0; matrix products, arithmetic and copies ran while one was open for 19% -> 0% of each run, Pallas kernels for 0% -> 0%
where the time goes in v2:
time: 204 us
  Pallas kernels  191 us (94%)
  other arithmetic  7.8 us (4%)
  local copies, waits for them, and re-layouts  4.28 us (2%)
    pallas_call x1, Pallas kernels, local_fast(): pl.pallas_call(functools.partial(layer_kernel, sizes), out_shape=(shape((...  191 us

profile of v2, /device:TPU:8, one launch (start us, length us, event | category | flops | bytes accessed | tf_op | source)
XLA Modules:
  0.0 203.7 jit_solution(10405003099677304454)
XLA Ops:
  0.7 0.6 broadcast_in_dim_tile.3.freq
  1.3 191.0 %layer.1 = (f32[128,1024]{1,0:T(8,128)}, f32[128,1024]{1,0:T(8,128)}, f32[128,1024]{1,0:T(8,128)}, bf16[128,5632]{1,0:T(8,128)(2,1)}, bf16[352,1024]{1,0:T(8,128...) custom-call(f32[1,128]{1,0:T(1,128)} %broadcast_in_dim_tile.3.freq, ...), custom_call_target="tpu_custom_call" | custom-call | tf_op jit(solution)/shard_map/layer/pallas_call | solution.py:871
  192.2 0.0 copy-start
  192.2 3.2 %slice_convert_fusion = (f32[128,2816]{1,0:T(8,128)}, f32[128,2816]{1,0:T(8,128)}) fusion(bf16[128,5632]{1,0:T(8,128)(2,1)} %get-tuple-element.30), kind=kLoop, calls=%fused_computation | loop fusion | flops 720896 | bytes 4325376 | tf_op jit(solution)/shard_map/convert_element_type | solution.py:907
  195.4 0.0 copy-start.7
  195.4 0.0 copy-start.6
  195.4 0.0 copy-start.5
  195.4 1.3 slice_bitcast_fusion
  196.7 0.0 copy-done
  196.7 0.0 copy-start.4
  196.7 1.3 convert_element_type.35
  197.9 0.0 copy-start.3
  197.9 0.0 copy-done.7
  197.9 0.0 copy-start.2
  197.9 0.8 convert_element_type.29
  198.8 0.0 copy-done.6
  198.8 0.0 copy-start.1
  198.8 0.8 convert_element_type.30
  199.6 0.0 copy-done.5
  199.6 0.8 convert_element_type.31
  200.5 0.0 copy-done.4
  200.5 0.8 convert_element_type.32
  201.3 0.0 copy-done.3
  201.3 0.8 copy.28
  202.1 0.0 copy-done.2
  202.1 0.8 copy.29
  202.9 0.0 copy-done.1
  202.9 0.8 copy.30
  (2 shorter events, 0.0 us)
Async XLA Ops:
  192.2 4.5 %copy-start = (bf16[352,1024]{1,0:T(8,128)(2,1)S(1)}, bf16[352,1024]{1,0:T(8,128)(2,1)}, u32[]{:S(2)}) copy-start(bf16[352,1024]{1,0:T(8,128)(2,1)} %get-tuple-element.31) | copy-start | bytes 2162692
  195.4 2.5 %copy-start.7 = (bf16[128,1024]{1,0:T(8,128)(2,1)S(1)}, bf16[128,1024]{1,0:T(8,128)(2,1)}, u32[]{:S(2)}) copy-start(bf16[128,1024]{1,0:T(8,128)(2,1)} %get-tuple-element.26) | copy-start | bytes 786436
  195.4 3.4 %copy-start.6 = (bf16[128,1024]{1,0:T(8,128)(2,1)S(1)}, bf16[128,1024]{1,0:T(8,128)(2,1)}, u32[]{:S(2)}) copy-start(bf16[128,1024]{1,0:T(8,128)(2,1)} %get-tuple-element.27) | copy-start | bytes 786436
  195.4 4.2 %copy-start.5 = (bf16[128,1024]{1,0:T(8,128)(2,1)S(1)}, bf16[128,1024]{1,0:T(8,128)(2,1)}, u32[]{:S(2)}) copy-start(bf16[128,1024]{1,0:T(8,128)(2,1)} %get-tuple-element.28) | copy-start | bytes 786436
  196.7 3.8 %copy-start.4 = (bf16[128,1024]{1,0:T(8,128)(2,1)S(1)}, bf16[128,1024]{1,0:T(8,128)(2,1)}, u32[]{:S(2)}) copy-start(bf16[128,1024]{1,0:T(8,128)(2,1)} %get-tuple-element.29) | copy-start | bytes 786436
  197.9 3.4 %copy-start.3 = (f32[128,1024]{1,0:T(8,128)S(1)}, f32[128,1024]{1,0:T(8,128)}, u32[]{:S(2)}) copy-start(f32[128,1024]{1,0:T(8,128)} %get-tuple-element.48) | copy-start | bytes 1572868
  197.9 4.2 %copy-start.2 = (f32[128,1024]{1,0:T(8,128)S(1)}, f32[128,1024]{1,0:T(8,128)}, u32[]{:S(2)}) copy-start(f32[128,1024]{1,0:T(8,128)} %get-tuple-element.49) | copy-start | bytes 1572868
  198.8 4.1 %copy-start.1 = (f32[128,1024]{1,0:T(8,128)S(1)}, f32[128,1024]{1,0:T(8,128)}, u32[]{:S(2)}) copy-start(f32[128,1024]{1,0:T(8,128)} %get-tuple-element.50) | copy-start | bytes 1572868

commit v3 on v2

--- a/solution.py
+++ b/solution.py
@@ -4,6 +4,7 @@
 
 import jax
 import jax.numpy as jnp
+import numpy as np
 from jax import lax
 from jax.experimental import pallas as pl
 from jax.experimental.pallas import tpu as pltpu
@@ -180,17 +181,25 @@
 
 
 class Sum:
-    def __init__(self, blk, n_blk, size, part, cgot, zgot, total, sems):
-        self.blk, self.chips, self.size = blk, n_blk // 2, size
+    def __init__(self, blk, size, part, cgot, rgot, zgot, total, sems):
+        self.blk, self.size = blk, size
         self.core, self.chip = lax.rem(blk, 2), lax.div(blk, 2)
-        self.part, self.cgot, self.zgot, self.total = part, cgot, zgot, total
-        self.csend, self.crecv, self.zsend, self.zrecv = sems
-
-    def turned(self, step):
-        return lax.rem(self.chip + step, self.chips)
+        side = lax.div(self.chip, 2)
+        self.far = 2 * (1 - side)
+        self.partner = self.chip + 1 - 2 * lax.rem(self.chip, 2)
+        self.inner = lax.rem(self.chip, 2) != side
+        self.far_inner = 2 - side
+        self.part, self.cgot, self.rgot, self.zgot, self.total = part, cgot, rgot, zgot, total
+        self.csend, self.crecv, self.rsend, self.rrecv, self.zsend, self.zrecv = sems
+
+    def order(self, step):
+        return jnp.where(step < 2, self.far + step, jnp.where(step == 2, self.partner, self.chip))
 
     def chunk(self, index):
         return self.part.at[span(index * self.size, self.size, 32)]
+
+    def mine(self, chip):
+        return self.chunk(2 * chip + self.core)
 
     def swap(self, chip):
         return remote(
@@ -201,44 +210,142 @@
             {"blk": 2 * self.chip + 1 - self.core},
         )
 
-    def forward(self, step):
-        chip = self.turned(step)
+    def lend(self, index):
         return remote(
-            self.chunk(2 * chip + self.core),
-            self.zgot(step - 1),
-            self.zsend.at[step - 1],
-            self.zrecv.at[step - 1],
-            {"blk": 2 * chip + self.core},
+            self.mine(self.far + index),
+            self.rgot(index),
+            self.rsend.at[index],
+            self.rrecv.at[index],
+            {"blk": 2 * self.partner + self.core},
         )
 
+    def send_far(self, index):
+        return remote(
+            self.mine(self.far + index),
+            self.zgot(1),
+            self.zsend.at[index],
+            self.zrecv.at[1],
+            {"blk": 2 * (self.far + index) + self.core},
+        )
+
+    def send_near(self):
+        return remote(
+            self.mine(self.partner),
+            self.zgot(0),
+            self.zsend.at[2],
+            self.zrecv.at[0],
+            {"blk": 2 * self.partner + self.core},
+        )
+
+    def add(self, mine, other):
+        def group(index):
+            at = span(index * 32, 32, 32)
+            mine[at, :] = (mine[at, :].astype(F32) + other[at, :].astype(F32)).astype(BF16)
+
+        loop(0, self.size // 32, group)
+
     def begin(self):
-        def one(step):
-            chip = self.turned(step)
+        for index in range(2):
+            chip = self.far + index
             self.swap(chip).wait()
-            mine, other = self.chunk(2 * chip + self.core), self.cgot(chip)
-
-            def add(group):
-                at = span(group * 32, 32, 32)
-                mine[at, :] = (mine[at, :].astype(F32) + other[at, :].astype(F32)).astype(BF16)
-
-            loop(0, self.size // 32, add)
-            self.forward(step).start()
-
-        loop(1, self.chips, one)
+            self.add(self.mine(chip), self.cgot(chip))
+
+            @pl.when(jnp.logical_not(self.inner))
+            def _(index=index):
+                self.lend(index).start()
+
+        self.swap(self.partner).wait()
+        self.add(self.mine(self.partner), self.cgot(self.partner))
+        self.send_near().start()
         self.swap(self.chip).wait()
 
+    def relay(self):
+        @pl.when(self.inner)
+        def _():
+            for index in range(2):
+                self.lend(index).wait_recv()
+                self.add(self.mine(self.far + index), self.rgot(index))
+                self.send_far(index).start()
+
     def end(self):
-        loop(1, self.chips, lambda step: self.forward(step).wait())
-        mine, other = self.chunk(self.blk), self.cgot(self.chip)
-
-        def add(group):
-            at = span(group * 32, 32, 32)
+        self.send_near().wait_recv()
+        self.send_far(0).wait_recv()
+        mine, other = self.mine(self.chip), self.cgot(self.chip)
+
+        def group(index):
+            at = span(index * 32, 32, 32)
             value = mine[at, :].astype(F32) + other[at, :].astype(F32)
-            for step in range(1, self.chips):
-                value = value + self.zgot(step - 1)[at, :].astype(F32)
+            value = value + self.zgot(0)[at, :].astype(F32) + self.zgot(1)[at, :].astype(F32)
             self.total[at, :] = value.astype(BF16)
 
-        loop(0, self.size // 32, add)
+        loop(0, self.size // 32, group)
+
+    def left(self):
+        self.send_near().wait_send()
+
+        @pl.when(self.inner)
+        def _():
+            for index in range(2):
+                self.send_far(index).wait_send()
+
+        @pl.when(jnp.logical_not(self.inner))
+        def _():
+            for index in range(2):
+                self.lend(index).wait_send()
+
+
+class TileGift:
+    def __init__(self, seq, n_seq, rows, src, dst, send, recv, owner_of):
+        self.seq, self.n_seq, self.rows, self.src, self.dst = seq, n_seq, rows, src, dst
+        self.send, self.recv, self.owner_of = send, recv, owner_of
+
+    def place(self, other, slot):
+        return self.dst.at[span(other * self.rows, self.rows, self.rows), span(slot * TILE, TILE, TILE)]
+
+    def tile(self, index):
+        return self.src.at[:, span(index * TILE, TILE, TILE)]
+
+    def start(self, index):
+        owner, slot = self.owner_of(index)
+        src, dst, recv = self.tile(index), self.place(self.seq, slot), self.recv.at[slot, self.seq]
+
+        @pl.when(owner != self.seq)
+        def _():
+            remote(src, dst, self.send.at[index], recv, {"seq": owner}).start()
+
+        @pl.when(owner == self.seq)
+        def _():
+            pltpu.make_async_copy(src, dst, recv).start()
+
+    def arrived(self, low, high):
+        def one(slot):
+            def other_one(other):
+                dst, recv = self.place(other, slot), self.recv.at[slot, other]
+
+                @pl.when(other != self.seq)
+                def _():
+                    remote(self.tile(0), dst, self.send.at[0], recv, {"seq": other}).wait_recv()
+
+                @pl.when(other == self.seq)
+                def _():
+                    pltpu.make_async_copy(self.tile(0), dst, recv).wait()
+
+            loop(0, self.n_seq, other_one)
+
+        loop(low, high, one)
+
+    def left(self, count):
+        def one(index):
+            owner, slot = self.owner_of(index)
+
+            @pl.when(owner != self.seq)
+            def _():
+                remote(
+                    self.tile(index), self.place(self.seq, slot), self.send.at[index], self.recv.at[slot, self.seq],
+                    {"seq": owner},
+                ).wait_send()
+
+        loop(0, count, one)
 
 
 class Spread:
@@ -273,12 +380,20 @@
             self.copy(self.owner).wait_recv()
 
 
-def outer_tiles(lhs, rhs, part, turned, chip, tiles, part_at):
-    turned[...] = lhs[:, span(chip * TILE, TILE, TILE)].T
+def turn_over(src, dst):
+    def one(index):
+        at = span(index * TILE, TILE, TILE)
+        dst[at, :] = src[:, at].T
+
+    loop(0, src.shape[1] // TILE, one)
+
+
+def outer_tiles(turned, rhs, part, chip, tiles, rhs_at, part_at):
+    rows = span(chip * TILE, TILE, TILE)
 
     def tile(index):
-        value = times(turned[...], rhs[:, span(index * TILE, TILE, TILE)])
-        part[span(chip * TILE, TILE, TILE), span(part_at + index * TILE, TILE, TILE)] = value.astype(BF16)
+        value = times(turned[rows, :], rhs[:, span(rhs_at + index * TILE, TILE, TILE)])
+        part[rows, span(part_at + index * TILE, TILE, TILE)] = value.astype(BF16)
 
     loop(0, tiles, tile)
 
@@ -363,16 +478,12 @@
 
     gift_cot = gift(3, 0, cot, v.buf_a)
     gifts_two = [gift(owner, 0, v.two, v.buf_a) for owner in range(3)]
-    gifts_gu = [
-        gift(
-            owner,
-            1,
-            v.gate_up.at[:, cuts[owner] : cuts[owner + 1]],
-            v.buf_b.at[:, : cuts[owner + 1] - cuts[owner]],
-        )
-        for owner in range(3)
-    ]
-    gift_act = gift(3, 1, v.act, v.buf_b)
+    each, hidden = split[0], ff // TILE
+    gift_gu = TileGift(
+        seq, n_seq, rows, v.gate_up, v.buf_b, sem.gusend, sem.gurecv,
+        lambda index: (lax.div(index, each), lax.rem(index, each)),
+    )
+    gift_act = TileGift(seq, n_seq, rows, v.act, v.buf_b, sem.actsend, sem.actrecv, lambda index: (3, index))
     gift_att = gift(2, 2, v.att, v.buf_att)
     gift_mid = gift(2, 3, v.mid_b, v.buf_mid)
     gifts_normed = [gift(owner, 4, v.normed, v.buf_n) for owner in range(3)]
@@ -395,6 +506,9 @@
     )
 
     pl.semaphore_wait(barrier, n_seq + n_blk - 2)
+    gift_cot.start()
+    for item in gifts_normed:
+        item.start()
 
     for item in (load_query, load_key, load_value):
         item.wait()
@@ -414,9 +528,6 @@
             give_qkv.start(peer)
 
     loop(1, chips + 1, project)
-    gift_cot.start()
-    for item in gifts_normed:
-        item.start()
 
     first_head = iota((TILE, LANES), 1) < HEAD_DIM
 
@@ -494,7 +605,8 @@
         item.wait()
     v.two_grad[...] = jnp.zeros((rows, width), F32)
 
-    def feed(tile):
+    def feed(step):
+        tile = lax.rem(split[0] + step, hidden)
         cols = span(tile * TILE, TILE, TILE)
         gate = times(v.two[...], v.w_gate[:, cols])
         up = times(v.two[...], v.w_up[:, cols])
@@ -507,10 +619,15 @@
         v.act[:, cols] = act
         v.gate_up[:, cols] = gate_grad
         v.gate_up[:, span(ff + tile * TILE, TILE, TILE)] = up_grad
+        gift_gu.start(tile)
+        gift_gu.start(hidden + tile)
+        gift_act.start(tile)
         o_layer[...] += times(act, v.w_down[cols, :])
         v.two_grad[...] += back(gate_grad, v.w_gate[:, cols]) + back(up_grad, v.w_up[:, cols])
 
-    loop(0, ff // TILE, feed)
+    loop(0, hidden, feed)
+    for step in range(1, n_blk):
+        pl.semaphore_signal(sem.ready, inc=1, device_id={"blk": lax.rem(blk + step, n_blk)}, device_id_type=MESH)
     v.gain_rows[...] = jnp.zeros((16, width), F32)
 
     def norm_two_back(group):
@@ -525,6 +642,7 @@
         v.mid_b[at, :] = value.astype(BF16)
 
     loop(0, rows // GROUP, norm_two_back)
+    gift_mid.start()
 
     def out_back(step):
         chip = turned_chip(step)
@@ -534,8 +652,112 @@
             give_out.start(2 * chip + core)
 
     loop(1, chips + 1, out_back)
-    for item in gifts_gu + [gift_act, gift_mid]:
-        item.start()
+
+    pl.semaphore_wait(sem.ready, n_blk - 1)
+    chunk, down = width // n_blk, ff // n_blk
+
+    def sems_of(index):
+        return tuple(
+            item.at[index] for item in (sem.csend, sem.crecv, sem.rsend, sem.rrecv, sem.zsend, sem.zrecv)
+        )
+
+    def stack_in(ref, top, cols):
+        return lambda index: ref.at[span(top + index * chunk, chunk, 32), cols]
+
+    def square_in(ref, more):
+        def place(index):
+            index = index + more
+            return ref.at[
+                span(lax.rem(index, 2) * down, down, 32), span(lax.div(index, 2) * width, width, width)
+            ]
+
+        return place
+
+    def piece(index, low, high):
+        cols = slice(low, high)
+        return Sum(
+            blk, chunk, v.w_gate.at[:, cols], stack_in(v.w_up, 0, cols), stack_in(v.w_up, chips * chunk, cols),
+            stack_in(v.w_up, (chips + 2) * chunk, cols), v.total.at[:, cols], sems_of(index),
+        )
+
+    third = -(-each // 3)
+    edges = [0, third, 2 * third, each]
+    thirds = [piece(index, edges[index] * TILE, edges[index + 1] * TILE) for index in range(3)]
+    last = split[2] * TILE
+    halves = [piece(0, 0, last), piece(1, last, last + width)]
+    sum_down = Sum(
+        blk, down, v.w_down, square_in(v.w_up, 0), square_in(v.w_gate, 0), square_in(v.w_gate, 2), v.total_down,
+        sems_of(0),
+    )
+    sum_tail = Sum(
+        blk, chunk, v.w_out, stack_in(v.got_tail, 0, slice(None)), stack_in(v.got_tail, chips * chunk, slice(None)),
+        stack_in(v.got_tail, (chips + 2) * chunk, slice(None)), v.total_tail, sems_of(3),
+    )
+    first_two, third_one, fourth = seq < 2, seq == 2, seq == 3
+
+    def spread(owner, kind, src, dst):
+        return Spread(seq, n_seq, owner, kind, src, dst, sem.gsend, sem.grecv, sem.glocal)
+
+    spreads = [
+        [
+            spread(
+                owner,
+                3 * owner + index,
+                v.total.at[:, edges[index] * TILE : edges[index + 1] * TILE],
+                o_gu.at[:, cuts[owner] + edges[index] * TILE : cuts[owner] + edges[index + 1] * TILE],
+            )
+            for index in range(3)
+        ]
+        for owner in range(2)
+    ] + [
+        [
+            spread(2, 6, v.total.at[:, :last], o_gu.at[:, cuts[2] : cuts[3]]),
+            spread(2, 7, v.total.at[:, last : last + width], o_out),
+        ],
+        [spread(3, 8, v.total_down, o_down)],
+    ]
+    tails = [
+        spread(0, 9, v.total_tail, o_query),
+        spread(1, 10, v.total_tail, o_key),
+        spread(2, 11, v.total_tail, o_value),
+    ]
+
+    def products(item, turned, rhs, tiles, rhs_at, part_at):
+        def one(step):
+            chip = item.order(step)
+            outer_tiles(turned, rhs, v.w_gate, chip, tiles, rhs_at, part_at)
+            item.swap(chip).start()
+
+        loop(0, chips, one)
+        item.begin()
+
+    def gate_up_piece(index):
+        gift_gu.arrived(edges[index], edges[index + 1])
+        at = edges[index] * TILE
+        products(thirds[index], v.turned, v.buf_b, edges[index + 1] - edges[index], at, at)
+
+    def down_products():
+        gift_act.arrived(0, hidden)
+
+        def one(index):
+            at = span(index * TILE, TILE, TILE)
+            v.turned[:TILE, :] = v.buf_b[:, at].T
+            v.w_down[at, :] = times(v.turned[:TILE, :], v.buf_a[...]).astype(BF16)
+
+        loop(0, hidden, one)
+        loop(0, chips, lambda step: sum_down.swap(sum_down.order(step)).start())
+        sum_down.begin()
+
+    for owner in range(n_seq):
+
+        @pl.when(seq == owner)
+        def _(owner=owner):
+            (gifts_two + [gift_cot])[owner].arrived()
+
+    @pl.when(first_two)
+    def _():
+        turn_over(v.buf_a, v.turned)
+        gate_up_piece(0)
 
     give_out.all_arrived()
 
@@ -578,77 +800,28 @@
 
     loop(0, chips, key_block)
 
-    chunk, down = width // n_blk, ff // n_blk
-    sems = tuple(item.at[0] for item in (sem.csend, sem.crecv, sem.zsend, sem.zrecv))
-    tail_sems = tuple(item.at[1] for item in (sem.csend, sem.crecv, sem.zsend, sem.zrecv))
-
-    def stack_in(ref, size, columns, top):
-        return lambda index: ref.at[span(top + index * size, size, 32), :columns]
-
-    def square_in(ref):
-        def place(index):
-            return ref.at[
-                span(lax.rem(index, 2) * down, down, 32), span(lax.div(index, 2) * width, width, width)
-            ]
-
-        return place
-
-    part = v.w_gate.at[:, :wide]
-    sum_gu = Sum(
-        blk, n_blk, chunk, part,
-        stack_in(v.w_up, chunk, wide, 0), stack_in(v.w_up, chunk, wide, chips * chunk), v.total, sems,
-    )
-    sum_down = Sum(
-        blk, n_blk, down, v.w_down, square_in(v.w_up), square_in(v.w_gate), v.total_down, sems
-    )
-    sum_tail = Sum(
-        blk, n_blk, chunk, v.w_out,
-        stack_in(v.got_tail, chunk, width, 0), stack_in(v.got_tail, chunk, width, chips * chunk),
-        v.total_tail, tail_sems,
-    )
-    early = [[gifts_two[0], gifts_gu[0]], [gifts_two[1], gifts_gu[1]], [gifts_two[2], gifts_gu[2], gift_att, gift_mid],
-             [gift_cot, gift_act]]
-    for owner in range(n_seq):
-
-        @pl.when(seq == owner)
-        def _(owner=owner):
-            for item in early[owner]:
-                item.arrived()
-
-    @pl.when(seq < 3)
-    def _():
-        def one(step):
-            chip = turned_chip(step)
-
-            @pl.when(seq < 2)
-            def _():
-                outer_tiles(v.buf_a, v.buf_b, v.w_gate, v.turned, chip, split[0], 0)
-
-            @pl.when(seq == 2)
-            def _():
-                spare = wide - split[2] * TILE - width
-                if spare:
-                    v.w_gate[span(chip * TILE, TILE, TILE), wide - spare : wide] = jnp.zeros((TILE, spare), BF16)
-                outer_tiles(v.buf_a, v.buf_b, v.w_gate, v.turned, chip, split[2], 0)
-                outer_tiles(
-                    v.buf_att, v.buf_mid, v.w_gate, v.turned, chip, width // TILE, split[2] * TILE
-                )
-
-            sum_gu.swap(chip).start()
-
-        loop(1, chips + 1, one)
-        sum_gu.begin()
-
-    @pl.when(seq == 3)
-    def _():
-        def one(index):
-            at = span(index * TILE, TILE, TILE)
-            v.turned[...] = v.buf_b[:, at].T
-            v.w_down[at, :] = times(v.turned[...], v.buf_a[...]).astype(BF16)
-
-        loop(0, ff // TILE, one)
-        loop(1, chips + 1, lambda step: sum_down.swap(turned_chip(step)).start())
-        sum_down.begin()
+    @pl.when(first_two)
+    def _():
+        thirds[0].relay()
+        gate_up_piece(1)
+        gate_up_piece(2)
+        thirds[1].relay()
+
+    @pl.when(third_one)
+    def _():
+        turn_over(v.buf_a, v.turned)
+        gift_gu.arrived(0, split[2])
+        products(halves[0], v.turned, v.buf_b, split[2], 0, 0)
+        gift_att.arrived()
+        gift_mid.arrived()
+        turn_over(v.buf_att, v.turned)
+        products(halves[1], v.turned, v.buf_mid, width // TILE, 0, last)
+        halves[0].relay()
+
+    @pl.when(fourth)
+    def _():
+        down_products()
+        sum_down.relay()
 
     give_grads.all_arrived()
 
@@ -698,6 +871,28 @@
     for step in range(1, n_blk):
         gain_copy(step).start()
 
+    @pl.when(first_two)
+    def _():
+        thirds[2].relay()
+        thirds[0].end()
+
+    for owner in range(2):
+        spreads[owner][0].start()
+
+    @pl.when(first_two)
+    def _():
+        thirds[1].end()
+
+    for owner in range(2):
+        spreads[owner][1].start()
+
+    @pl.when(third_one)
+    def _():
+        halves[1].relay()
+        halves[0].end()
+
+    spreads[2][0].start()
+
     for owner in range(3):
 
         @pl.when(seq == owner)
@@ -707,41 +902,35 @@
 
     @pl.when(seq < 3)
     def _():
+        turn_over(v.buf_n, v.turned)
+
         def one(step):
-            chip = turned_chip(step)
-            outer_tiles(v.buf_n, v.buf_t, v.w_out, v.turned, chip, width // TILE, 0)
+            chip = sum_tail.order(step)
+            outer_tiles(v.turned, v.buf_t, v.w_out, chip, width // TILE, 0, 0)
             sum_tail.swap(chip).start()
 
-        loop(1, chips + 1, one)
+        loop(0, chips, one)
         sum_tail.begin()
-
-    def spread(owner, kind, src, dst):
-        return Spread(seq, n_seq, owner, kind, src, dst, sem.gsend, sem.grecv, sem.glocal)
-
-    last = cuts[3] - cuts[2]
-    spreads = [
-        spread(0, 0, v.total.at[:, : cuts[1] - cuts[0]], o_gu.at[:, cuts[0] : cuts[1]]),
-        spread(1, 1, v.total.at[:, : cuts[2] - cuts[1]], o_gu.at[:, cuts[1] : cuts[2]]),
-        spread(2, 2, v.total.at[:, :last], o_gu.at[:, cuts[2] : cuts[3]]),
-        spread(2, 3, v.total.at[:, last : last + width], o_out),
-        spread(3, 4, v.total_down, o_down),
-    ]
-    tails = [
-        spread(0, 5, v.total_tail, o_query),
-        spread(1, 6, v.total_tail, o_key),
-        spread(2, 7, v.total_tail, o_value),
-    ]
-
-    @pl.when(seq < 3)
-    def _():
-        sum_gu.end()
-
-    @pl.when(seq == 3)
+        sum_tail.relay()
+
+    @pl.when(first_two)
+    def _():
+        thirds[2].end()
+
+    for owner in range(2):
+        spreads[owner][2].start()
+
+    @pl.when(third_one)
+    def _():
+        halves[1].end()
+
+    spreads[2][1].start()
+
+    @pl.when(fourth)
     def _():
         sum_down.end()
 
-    for item in spreads:
-        item.start()
+    spreads[3][0].start()
 
     value = v.gains[blk]
     for step in range(1, n_blk):
@@ -770,14 +959,98 @@
     o_gain[0:8, :] = jnp.broadcast_to(jnp.sum(value[:8], axis=0, keepdims=True), (8, LANES))
     o_gain[8:16, :] = jnp.broadcast_to(jnp.sum(value[8:], axis=0, keepdims=True), (8, LANES))
 
-    for item in spreads + tails:
+    for item in sum(spreads, []) + tails:
         item.finish()
-    for item in (
-        [gift_cot, gift_act, gift_att, gift_mid] + gifts_two + gifts_gu + gifts_normed + gifts_pre
-    ):
+    for item in [gift_cot, gift_att, gift_mid] + gifts_two + gifts_normed + gifts_pre:
         item.left()
+    gift_gu.left(2 * hidden)
+    gift_act.left(hidden)
     for item in (give_att, give_out, give_grads):
         item.all_left()
+
+    @pl.when(first_two)
+    def _():
+        for item in thirds:
+            item.left()
+
+    @pl.when(third_one)
+    def _():
+        for item in halves:
+            item.left()
+
+    @pl.when(fourth)
+    def _():
+        sum_down.left()
+
+    @pl.when(seq < 3)
+    def _():
+        sum_tail.left()
+
+
+def finish_kernel(
+    layer, tokens, first, gu, down, out, query, key, value, gain,
+    o_layer, o_tokens, o_first, o_gain, o_gain_two, o_query, o_key, o_value, o_out, o_gate, o_up, o_down,
+    kept, small, large, sem_kept_in, sem_kept_out, sem_in, sem_out,
+):
+    kept_in = [
+        pltpu.make_async_copy(src, kept[index], sem_kept_in.at[index])
+        for index, src in enumerate((layer, tokens, first))
+    ]
+    kept_out = [
+        pltpu.make_async_copy(kept[index], dst, sem_kept_out.at[index])
+        for index, dst in enumerate((o_layer, o_tokens, o_first))
+    ]
+    ff = o_gate.shape[1]
+    sources = [gu.at[:, :ff], gu.at[:, ff:], down, query, key, value, out]
+    targets = [o_gate, o_up, o_down, o_query, o_key, o_value, o_out]
+    loads = [pltpu.make_async_copy(src, small[index], sem_in.at[index]) for index, src in enumerate(sources)]
+    stores = [pltpu.make_async_copy(large[index], dst, sem_out.at[index]) for index, dst in enumerate(targets)]
+    for item in kept_in + loads:
+        item.start()
+    for coming, going in zip(kept_in, kept_out):
+        coming.wait()
+        going.start()
+    for index in range(len(sources)):
+        loads[index].wait()
+
+        def group(step, index=index):
+            at = span(step * GROUP, GROUP, GROUP)
+            large[index][at, :] = small[index][at, :].astype(F32)
+
+        loop(0, targets[index].shape[0] // GROUP, group)
+        stores[index].start()
+    o_gain[...] = gain[0:1, :]
+    o_gain_two[...] = gain[8:9, :]
+    for item in stores + kept_out:
+        item.wait()
+
+
+def finish(layer, tokens, first, gu, down, out, query, key, value, gain):
+    hbm, vmem = pl.BlockSpec(memory_space=pl.ANY), pl.BlockSpec(memory_space=pltpu.VMEM)
+    shape = jax.ShapeDtypeStruct
+    ff = gu.shape[1] // 2
+    dims = [(gu.shape[0], ff), (gu.shape[0], ff), down.shape, query.shape, key.shape, value.shape, out.shape]
+    dma = pltpu.SemaphoreType.DMA
+    results = pl.pallas_call(
+        finish_kernel,
+        out_shape=tuple(
+            shape(each, F32)
+            for each in (
+                layer.shape, tokens.shape, first.shape, (1, LANES), (1, LANES), dims[3], dims[4], dims[5], dims[6], dims[0], dims[1], dims[2]
+            )
+        ),
+        in_specs=[hbm] * 9 + [vmem],
+        out_specs=(hbm,) * 3 + (vmem,) * 2 + (hbm,) * 7,
+        scratch_shapes=(
+            [pltpu.VMEM(each.shape, F32) for each in (layer, tokens, first)],
+            [pltpu.VMEM(each, BF16) for each in dims],
+            [pltpu.VMEM(each, F32) for each in dims],
+            dma((3,)), dma((3,)), dma((7,)), dma((7,)),
+        ),
+        compiler_params=pltpu.CompilerParams(vmem_limit_bytes=63 * 1024 * 1024),
+        name="finish",
+    )(layer, tokens, first, gu, down, out, query, key, value, gain)
+    return results[:3] + (results[3][0],) + results[5:9] + (results[4][0],) + results[9:]
 
 
 def tile_split(width, ff):
@@ -795,7 +1068,7 @@
         and ff % TILE == 0
         and (ff // n_blk) % 32 == 0
         and 2 * (ff // n_blk) <= width
-        and n_blk // 2 <= 4
+        and n_blk == 8
     )
 
 
@@ -821,8 +1094,8 @@
     split = tile_split(width, ff)
     sizes = (rows, width, ff, n_seq, n_blk, split)
     half = HEAD_DIM // 2
-    freq = THETA ** (-(jnp.arange(half).astype(jnp.float32) * 2.0 / HEAD_DIM))
-    freq = jnp.tile(freq, LANES // half)[None, :]
+    freq = THETA ** (-(np.arange(half) * 2.0 / HEAD_DIM))
+    freq = np.tile(freq, LANES // half)[None, :].astype(np.float32)
     wide = max(split) * TILE
     chunk, down, chips = width // n_blk, ff // n_blk, n_blk // 2
     all_rows, group = n_seq * rows, n_blk * rows
@@ -855,8 +1128,8 @@
         grads=half_type(3, rows, width), pre_grad=half_type(3, rows, width),
         buf_a=half_type(all_rows, width), buf_b=half_type(all_rows, ff), buf_att=half_type(all_rows, width),
         buf_mid=half_type(all_rows, width), buf_n=half_type(all_rows, width), buf_t=half_type(all_rows, width),
-        turned=half_type(TILE, all_rows),
-        got_tail=half_type((2 * chips - 1) * chunk, width),
+        turned=half_type(width, all_rows),
+        got_tail=half_type(2 * chips * chunk, width),
         total=half_type(chunk, wide), total_down=half_type(down, width), total_tail=half_type(chunk, width),
         gain_rows=full_type(16, width), gains=full_type(n_blk, 16, LANES), gain_got=full_type(n_blk - 1, 16, LANES),
         gain_sum=full_type(n_seq, 16, LANES),
@@ -864,8 +1137,10 @@
     dma = pltpu.SemaphoreType.DMA
     sems = dict(
         load=dma((7,)), asend=dma((4, n_blk)), arecv=dma((4, n_blk)), xsend=dma((6, n_seq)), xrecv=dma((6, n_seq)),
-        csend=dma((2, chips)), crecv=dma((2, chips)), zsend=dma((2, chips - 1)), zrecv=dma((2, chips - 1)),
-        gsend=dma((8, n_seq)), grecv=dma((8,)), glocal=dma((8,)),
+        gusend=dma((2 * ff // TILE,)), gurecv=dma((split[0], n_seq)), actsend=dma((ff // TILE,)),
+        actrecv=dma((ff // TILE, n_seq)), ready=pltpu.SemaphoreType.REGULAR,
+        csend=dma((4, chips)), crecv=dma((4, chips)), rsend=dma((4, 2)), rrecv=dma((4, 2)), zsend=dma((4, 3)),
+        zrecv=dma((4, 2)), gsend=dma((12, n_seq)), grecv=dma((12,)), glocal=dma((12,)),
         hsend=dma((n_blk - 1,)), hrecv=dma((n_blk - 1,)), isend=dma((n_seq - 1,)), irecv=dma((n_seq,)),
     )
     layer, grad_tokens, grad_first, out_gu, out_down, out_out, out_query, out_key, out_value, out_gain = pl.pallas_call(
@@ -893,20 +1168,7 @@
         freq, tokens, first_values, doc_lengths, attn_gain[None, :], ffn_gain[None, :], cotangent,
         query_weight, key_weight, value_weight, out_weight, gate_weight, up_weight, down_weight,
     )
-    return (
-        layer,
-        grad_tokens,
-        grad_first,
-        out_gain[0],
-        out_query.astype(F32),
-        out_key.astype(F32),
-        out_value.astype(F32),
-        out_out.astype(F32),
-        out_gain[8],
-        out_gu[:, :ff].astype(F32),
-        out_gu[:, ff:].astype(F32),
-        out_down.astype(F32),
-    )
+    return finish(layer, grad_tokens, grad_first, out_gu, out_down, out_out, out_query, out_key, out_value, out_gain)
 
 
 def local(

time: 204 us -> 175 us (0.86)
  Pallas kernels: 191 us -> 174 us
  other arithmetic: 7.8 us -> 0 us
  local copies, waits for them, and re-layouts: 4.28 us -> 0 us
    pallas_call x1, Pallas kernels: 191 us -> 168 us  [local_fast(): pl.pallas_call(functools.partial(layer_kernel, sizes), out_shape=(shape((...]
    convert_element_type x6 -> x0, other arithmetic: 7.79 us -> none  [the longest x1 3.16 us: local_fast(): out_gu[:, ff:].astype(F32)]
    pallas_call x0 -> x1, Pallas kernels: none -> 6.46 us  [finish(): pl.pallas_call(finish_kernel, out_shape=tuple((shape(each, F32) for each...]
    unnamed x19 -> x0, local copies, waits for them, and re-layouts: 2.41 us -> none
where the time goes in v3:
time: 175 us
  Pallas kernels  174 us (99%)
    pallas_call x1, Pallas kernels, local_fast(): pl.pallas_call(functools.partial(layer_kernel, sizes), out_shape=(shape((...  168 us
    pallas_call x1, Pallas kernels, finish(): pl.pallas_call(finish_kernel, out_shape=tuple((shape(each, F32) for each...  6.46 us

profile of v3, /device:TPU:8, one launch (start us, length us, event | category | flops | bytes accessed | tf_op | source)
XLA Modules:
  0.0 175.1 jit_solution(12813160989213303399)
XLA Ops:
  0.6 168.0 %layer.1 = (f32[128,1024]{1,0:T(8,128)}, f32[128,1024]{1,0:T(8,128)}, f32[128,1024]{1,0:T(8,128)}, bf16[128,5632]{1,0:T(8,128)(2,1)}, bf16[352,1024]{1,0:T(8,128...) custom-call(f32[1,128]{1,0:T(1,128)} %constant.2.clone.freq, ...), custom_call_target="tpu_custom_call" | custom-call | tf_op jit(solution)/shard_map/layer/pallas_call | solution.py:1146
  168.6 6.5 %finish.1 = (f32[128,1024]{1,0:T(8,128)}, f32[128,1024]{1,0:T(8,128)}, f32[128,1024]{1,0:T(8,128)}, f32[1,128]{1,0:T(1,128)}, f32[1,128]{1,0:T(1,128)}, /*index=...) custom-call(f32[128,1024]{1,0:T(8,128)} %get-tuple-element.34.layer,, ...), custom_call_target="tpu_custom_call" | custom-call | tf_op jit(solution)/shard_map/finish/pallas_call | solution.py:1034

commit v4 on v3

--- a/solution.py
+++ b/solution.py
@@ -451,22 +451,25 @@
             start = jnp.where(index >= end, end, start)
         return start
 
-    my_index = blk * rows + iota((rows, LANES), 0)
-    low_half = lax.rem(iota((rows, LANES), 1), HEAD_DIM) < HEAD_DIM // 2
-    angle = (my_index - doc_start(my_index)).astype(F32) * freq[...]
-    v.cos[...] = jnp.cos(angle)
-    sine = jnp.sin(angle)
-    v.sin[...] = jnp.where(low_half, -sine, sine)
+    half = HEAD_DIM // 2
+
+    def low_half(count):
+        return lax.rem(iota((count, LANES), 1), HEAD_DIM) < half
+
+    def set_tables(start, count, cosine_ref, sine_ref):
+        index = start + iota((count, LANES), 0)
+        angle = (index - doc_start(index)).astype(F32) * freq[...]
+        cosine_ref[...] = jnp.cos(angle)
+        sine = jnp.sin(angle)
+        sine_ref[...] = jnp.where(low_half(count), -sine, sine)
 
     def halves_changed(u):
-        half = HEAD_DIM // 2
-        return jnp.where(low_half, pltpu.roll(u, LANES - half, 1), pltpu.roll(u, half, 1))
+        return jnp.where(low_half(u.shape[0]), pltpu.roll(u, LANES - half, 1), pltpu.roll(u, half, 1))
+
+    set_tables(blk * rows, rows, v.cos, v.sin)
 
     def rotated(u):
         return u * v.cos[...] + halves_changed(u) * v.sin[...]
-
-    def rotated_back(u):
-        return u * v.cos[...] - halves_changed(u) * v.sin[...]
 
     cuts = [0]
     for tiles in split:
@@ -486,9 +489,6 @@
     gift_act = TileGift(seq, n_seq, rows, v.act, v.buf_b, sem.actsend, sem.actrecv, lambda index: (3, index))
     gift_att = gift(2, 2, v.att, v.buf_att)
     gift_mid = gift(2, 3, v.mid_b, v.buf_mid)
-    gifts_normed = [gift(owner, 4, v.normed, v.buf_n) for owner in range(3)]
-    gifts_pre = [gift(owner, 5, v.pre_grad.at[owner], v.buf_t) for owner in range(3)]
-
     def trade(phase, source, place):
         return Trade(blk, n_blk, phase, sem.asend, sem.arecv, source, place)
 
@@ -505,10 +505,33 @@
         3, lambda peer: v.pack.at[peer], lambda peer: v.grads.at[:, :, span(peer * LANES, LANES, LANES)]
     )
 
+    give_tail = trade(4, lambda peer: v.tail_sum.at[peer], lambda peer: v.tail_got.at[peer])
+    core = lax.rem(blk, 2)
+    mate = blk + 1 - 2 * core
+
+    def block_of(step):
+        return 2 * turned_chip(step) + core
+
+    def rows_of(block):
+        return v.normed_all.at[span(block * rows, rows, rows)]
+
+    def normed_out(step):
+        return remote(
+            v.normed, rows_of(blk), sem.nsend.at[step - 1], sem.nrecv.at[step - 1], {"blk": block_of(step)}
+        )
+
+    def normed_over(step):
+        there = rows_of(block_of(step))
+        return remote(there, there, sem.fsend.at[step], sem.frecv.at[step], {"blk": mate})
+
+    def mates_normed(step):
+        there = rows_of(2 * turned_chip(step) + 1 - core)
+        return remote(there, there, sem.fsend.at[step], sem.frecv.at[step], {"blk": mate})
+
     pl.semaphore_wait(barrier, n_seq + n_blk - 2)
     gift_cot.start()
-    for item in gifts_normed:
-        item.start()
+    own_normed = pltpu.make_async_copy(v.normed, rows_of(blk), sem.nlocal.at[0])
+    own_normed.start()
 
     for item in (load_query, load_key, load_value):
         item.wait()
@@ -577,8 +600,20 @@
             give_att.start(2 * block + core)
 
     loop(0, chips, attend)
+    loop(
+        0,
+        chips,
+        lambda block: set_tables(
+            block * TILE,
+            TILE,
+            v.score.at[:TILE, span(block * TILE, LANES, LANES)],
+            v.score.at[:TILE, span(block * TILE + LANES, LANES, LANES)],
+        ),
+    )
     give_att.all_arrived()
     gift_att.start()
+    for step in range(1, chips):
+        normed_out(step).start()
 
     load_out.wait()
 
@@ -652,6 +687,11 @@
             give_out.start(2 * chip + core)
 
     loop(1, chips + 1, out_back)
+    own_normed.wait()
+    normed_over(0).start()
+    for step in range(1, chips):
+        normed_out(chips - step).wait_recv()
+        normed_over(step).start()
 
     pl.semaphore_wait(sem.ready, n_blk - 1)
     chunk, down = width // n_blk, ff // n_blk
@@ -664,11 +704,11 @@
     def stack_in(ref, top, cols):
         return lambda index: ref.at[span(top + index * chunk, chunk, 32), cols]
 
-    def square_in(ref, more):
+    def square_in(ref, more, low):
         def place(index):
             index = index + more
             return ref.at[
-                span(lax.rem(index, 2) * down, down, 32), span(lax.div(index, 2) * width, width, width)
+                span(lax.rem(index, 2) * down, down, 32), span(lax.div(index, 2) * width + low, TILE, TILE)
             ]
 
         return place
@@ -685,14 +725,14 @@
     thirds = [piece(index, edges[index] * TILE, edges[index + 1] * TILE) for index in range(3)]
     last = split[2] * TILE
     halves = [piece(0, 0, last), piece(1, last, last + width)]
-    sum_down = Sum(
-        blk, down, v.w_down, square_in(v.w_up, 0), square_in(v.w_gate, 0), square_in(v.w_gate, 2), v.total_down,
-        sems_of(0),
-    )
-    sum_tail = Sum(
-        blk, chunk, v.w_out, stack_in(v.got_tail, 0, slice(None)), stack_in(v.got_tail, chips * chunk, slice(None)),
-        stack_in(v.got_tail, (chips + 2) * chunk, slice(None)), v.total_tail, sems_of(3),
-    )
+    quarters = [
+        Sum(
+            blk, down, v.w_down.at[:, low : low + TILE], square_in(v.w_up, 0, low), square_in(v.w_gate, 0, low),
+            square_in(v.w_gate, 2, low), v.total_down.at[:, low : low + TILE], sems_of(low // TILE),
+        )
+        for low in range(0, width, TILE)
+    ]
+
     first_two, third_one, fourth = seq < 2, seq == 2, seq == 3
 
     def spread(owner, kind, src, dst):
@@ -714,14 +754,11 @@
             spread(2, 6, v.total.at[:, :last], o_gu.at[:, cuts[2] : cuts[3]]),
             spread(2, 7, v.total.at[:, last : last + width], o_out),
         ],
-        [spread(3, 8, v.total_down, o_down)],
+        [
+            spread(3, 8 + index, v.total_down.at[:, low : low + TILE], o_down.at[:, low : low + TILE])
+            for index, low in enumerate(range(0, width, TILE))
+        ],
     ]
-    tails = [
-        spread(0, 9, v.total_tail, o_query),
-        spread(1, 10, v.total_tail, o_key),
-        spread(2, 11, v.total_tail, o_value),
-    ]
-
     def products(item, turned, rhs, tiles, rhs_at, part_at):
         def one(step):
             chip = item.order(step)
@@ -737,16 +774,18 @@
         products(thirds[index], v.turned, v.buf_b, edges[index + 1] - edges[index], at, at)
 
     def down_products():
-        gift_act.arrived(0, hidden)
-
-        def one(index):
+        def one(step):
+            index = lax.rem(split[0] + step, hidden)
+            gift_act.arrived(index, index + 1)
             at = span(index * TILE, TILE, TILE)
             v.turned[:TILE, :] = v.buf_b[:, at].T
             v.w_down[at, :] = times(v.turned[:TILE, :], v.buf_a[...]).astype(BF16)
 
         loop(0, hidden, one)
-        loop(0, chips, lambda step: sum_down.swap(sum_down.order(step)).start())
-        sum_down.begin()
+        for item in quarters:
+            loop(0, chips, lambda step, item=item: item.swap(item.order(step)).start())
+        for item in quarters:
+            item.begin()
 
     for owner in range(n_seq):
 
@@ -788,27 +827,64 @@
             v.dq[both, :] += times(score_grad, v.qkv[1, at, :])
 
         loop(block, chips, query_block)
-        dq = (unstacked(v.dq[span(block * 2 * TILE, 2 * TILE, 2 * TILE), :]) * scale).astype(BF16)
-        dk, dv = v.dk[...].astype(BF16), v.dv[...].astype(BF16)
-        for core in range(2):
-            peer = 2 * block + core
-            part = slice(core * rows, (core + 1) * rows)
-            v.pack[peer, 0] = dq[part]
-            v.pack[peer, 1] = dk[part]
-            v.pack[peer, 2] = dv[part]
-            give_grads.start(peer)
+        cosine = v.score[:TILE, span(block * TILE, LANES, LANES)]
+        sine = v.score[:TILE, span(block * TILE + LANES, LANES, LANES)]
+
+        def rotated_back(u):
+            u = u.astype(BF16).astype(F32)
+            return (u * cosine - halves_changed(u) * sine).astype(BF16)
+
+        dq = rotated_back(unstacked(v.dq[span(block * 2 * TILE, 2 * TILE, 2 * TILE), :]) * scale)
+        dk = rotated_back(v.dk[...])
+        dv = (MIX * v.dv[...].astype(BF16).astype(F32)).astype(BF16)
+        for index, value in enumerate((dq, dk, dv)):
+            v.heads_grad[at, index * LANES : (index + 1) * LANES] = value
+            for half_at in range(2):
+                v.pack[2 * block + half_at, index] = value[half_at * rows : (half_at + 1) * rows]
+        for half_at in range(2):
+            give_grads.start(2 * block + half_at)
 
     loop(0, chips, key_block)
 
-    @pl.when(first_two)
-    def _():
-        thirds[0].relay()
-        gate_up_piece(1)
-        gate_up_piece(2)
-        thirds[1].relay()
-
-    @pl.when(third_one)
-    def _():
+    for step in range(chips):
+        mates_normed(step).wait_recv()
+
+    def project_back(index):
+        value = outer(v.normed_all[:, span(index * TILE, TILE, TILE)], v.heads_grad[...]).astype(BF16)
+        v.tail_part[2 * index] = value[:LANES]
+        v.tail_part[2 * index + 1] = value[LANES:]
+
+    loop(0, width // TILE, project_back)
+    quarter = LANES // n_seq
+
+    def tail_share(step):
+        other = lax.rem(seq + step, n_seq)
+        return remote(
+            v.tail_part.at[:, span(other * quarter, quarter, quarter)],
+            v.tail_shares.at[step - 1],
+            sem.qsend.at[step - 1],
+            sem.qrecv.at[step - 1],
+            {"seq": other},
+        )
+
+    for step in range(1, n_seq):
+        tail_share(step).start()
+
+    def when(which, *steps):
+        @pl.when(which)
+        def _():
+            for step in steps:
+                step()
+
+    def ended(item, goes):
+        def step():
+            item.end()
+            for other in goes:
+                other.start()
+
+        return step
+
+    def third_products():
         turn_over(v.buf_a, v.turned)
         gift_gu.arrived(0, split[2])
         products(halves[0], v.turned, v.buf_b, split[2], 0, 0)
@@ -816,36 +892,43 @@
         gift_mid.arrived()
         turn_over(v.buf_att, v.turned)
         products(halves[1], v.turned, v.buf_mid, width // TILE, 0, last)
-        halves[0].relay()
-
-    @pl.when(fourth)
-    def _():
-        down_products()
-        sum_down.relay()
+
+    when(first_two, lambda: gate_up_piece(1), thirds[0].relay, lambda: gate_up_piece(2))
+    when(third_one, third_products)
+    when(fourth, down_products)
+
+    def tail_add(index):
+        value = v.tail_part[index, span(seq * quarter, quarter, quarter), :].astype(F32)
+        for step in range(1, n_seq):
+            value = value + v.tail_shares[step - 1, index].astype(F32)
+        v.tail_sum[index] = value.astype(BF16)
+        give_tail.start(index)
+
+    for step in range(1, n_seq):
+        tail_share(step).wait()
+    loop(0, n_blk, tail_add)
 
     give_grads.all_arrived()
 
-    def rotate_back(index):
-        cols = span(index * LANES, LANES, LANES)
-        v.pre_grad[0, :, cols] = rotated_back(v.grads[0, :, cols].astype(F32)).astype(BF16)
-        v.pre_grad[1, :, cols] = rotated_back(v.grads[1, :, cols].astype(F32)).astype(BF16)
-        value = MIX * v.grads[2, :, cols].astype(F32)
-        v.pre_grad[2, :, cols] = value.astype(BF16)
-        o_first[:, cols] = value
-
-    loop(0, width // LANES, rotate_back)
-    for item in gifts_pre:
+    def gone(index, *owners):
+        return [spreads[owner][index] for owner in owners]
+
+    when(first_two, thirds[1].relay, ended(thirds[0], []))
+    for item in gone(0, 0, 1):
         item.start()
+    when(fourth, quarters[0].relay)
 
     def normed_back(tile):
         at = span(tile * TILE, TILE, TILE)
         o_tokens[:, at] = (
-            back(v.pre_grad[0], v.w_query[at, :])
-            + back(v.pre_grad[1], v.w_key[at, :])
-            + back(v.pre_grad[2], v.w_value[at, :])
+            back(v.grads[0], v.w_query[at, :])
+            + back(v.grads[1], v.w_key[at, :])
+            + back(v.grads[2], v.w_value[at, :])
         )
 
     loop(0, width // TILE, normed_back)
+    o_first[...] = v.grads[2].astype(F32)
+    when(fourth, ended(quarters[0], gone(0, 3)), quarters[1].relay)
 
     def norm_back(group):
         at = span(group * GROUP, GROUP, GROUP)
@@ -871,66 +954,54 @@
     for step in range(1, n_blk):
         gain_copy(step).start()
 
-    @pl.when(first_two)
-    def _():
-        thirds[2].relay()
-        thirds[0].end()
-
-    for owner in range(2):
-        spreads[owner][0].start()
-
-    @pl.when(first_two)
-    def _():
-        thirds[1].end()
-
-    for owner in range(2):
-        spreads[owner][1].start()
-
-    @pl.when(third_one)
-    def _():
-        halves[1].relay()
-        halves[0].end()
-
-    spreads[2][0].start()
-
-    for owner in range(3):
-
-        @pl.when(seq == owner)
-        def _(owner=owner):
-            gifts_normed[owner].arrived()
-            gifts_pre[owner].arrived()
-
-    @pl.when(seq < 3)
-    def _():
-        turn_over(v.buf_n, v.turned)
-
-        def one(step):
-            chip = sum_tail.order(step)
-            outer_tiles(v.turned, v.buf_t, v.w_out, chip, width // TILE, 0, 0)
-            sum_tail.swap(chip).start()
-
-        loop(0, chips, one)
-        sum_tail.begin()
-        sum_tail.relay()
-
-    @pl.when(first_two)
-    def _():
-        thirds[2].end()
-
-    for owner in range(2):
-        spreads[owner][2].start()
-
-    @pl.when(third_one)
-    def _():
-        halves[1].end()
-
-    spreads[2][1].start()
-
-    @pl.when(fourth)
-    def _():
-        sum_down.end()
-
-    spreads[3][0].start()
+    when(
+        first_two,
+        ended(thirds[1], gone(1, 0, 1)),
+        thirds[2].relay,
+        ended(thirds[2], gone(2, 0, 1)),
+    )
+    when(
+        third_one,
+        halves[0].relay,
+        ended(halves[0], gone(0, 2)),
+        halves[1].relay,
+        ended(halves[1], gone(1, 2)),
+    )
+    when(
+        fourth,
+        ended(quarters[1], gone(1, 3)),
+        quarters[2].relay,
+        ended(quarters[2], gone(2, 3)),
+        quarters[3].relay,
+        ended(quarters[3], gone(3, 3)),
+    )
+    give_tail.all_arrived()
+    for index in range(3):
+        for peer in range(n_blk):
+            v.tail_done[index, :, peer * LANES : (peer + 1) * LANES] = v.tail_got[
+                peer, :, index * LANES : (index + 1) * LANES
+            ]
+
+    def tail_spread(index, step, owner):
+        at = span(owner * quarter, quarter, quarter)
+        return remote(
+            v.tail_done.at[index],
+            (o_query, o_key, o_value)[index].at[at],
+            sem.tsend.at[index, step - 1],
+            sem.trecv.at[index, owner],
+            {"seq": lax.rem(seq + step, n_seq)},
+        )
+
+    def tail_own(index):
+        at = span(seq * quarter, quarter, quarter)
+        return pltpu.make_async_copy(
+            v.tail_done.at[index], (o_query, o_key, o_value)[index].at[at], sem.trecv.at[index, seq]
+        )
+
+    for index in range(3):
+        tail_own(index).start()
+        for step in range(1, n_seq):
+            tail_spread(index, step, seq).start()
 
     value = v.gains[blk]
     for step in range(1, n_blk):
@@ -942,13 +1013,6 @@
         mine = v.gain_sum.at[seq]
         remote(mine, mine, sem.isend.at[step - 1], sem.irecv.at[seq], {"seq": other}).start()
 
-    @pl.when(seq < 3)
-    def _():
-        sum_tail.end()
-
-    for item in tails:
-        item.start()
-
     for step in range(1, n_seq):
         other = lax.rem(seq + step, n_seq)
         theirs = v.gain_sum.at[other]
@@ -959,14 +1023,23 @@
     o_gain[0:8, :] = jnp.broadcast_to(jnp.sum(value[:8], axis=0, keepdims=True), (8, LANES))
     o_gain[8:16, :] = jnp.broadcast_to(jnp.sum(value[8:], axis=0, keepdims=True), (8, LANES))
 
-    for item in sum(spreads, []) + tails:
+    for index in range(3):
+        tail_own(index).wait()
+        for step in range(1, n_seq):
+            tail_spread(index, step, seq).wait_send()
+            tail_spread(index, step, lax.rem(seq + step, n_seq)).wait_recv()
+    for item in sum(spreads, []):
         item.finish()
-    for item in [gift_cot, gift_att, gift_mid] + gifts_two + gifts_normed + gifts_pre:
+    for item in [gift_cot, gift_att, gift_mid] + gifts_two:
         item.left()
     gift_gu.left(2 * hidden)
     gift_act.left(hidden)
-    for item in (give_att, give_out, give_grads):
+    for item in (give_att, give_out, give_grads, give_tail):
         item.all_left()
+    for step in range(chips):
+        normed_over(step).wait_send()
+        if step:
+            normed_out(step).wait_send()
 
     @pl.when(first_two)
     def _():
@@ -980,11 +1053,8 @@
 
     @pl.when(fourth)
     def _():
-        sum_down.left()
-
-    @pl.when(seq < 3)
-    def _():
-        sum_tail.left()
+        for item in quarters:
+            item.left()
 
 
 def finish_kernel(
@@ -1069,6 +1139,7 @@
         and (ff // n_blk) % 32 == 0
         and 2 * (ff // n_blk) <= width
         and n_blk == 8
+        and width == n_seq * TILE
     )
 
 
@@ -1125,22 +1196,26 @@
         act=half_type(rows, ff), gate_up=half_type(rows, 2 * ff), two_grad=full_type(rows, width),
         mid_grad=full_type(rows, width), mid_b=half_type(rows, width),
         out_pack=half_type(n_blk, rows, LANES), out_grad=half_type(group, LANES),
-        grads=half_type(3, rows, width), pre_grad=half_type(3, rows, width),
+        grads=half_type(3, rows, width),
         buf_a=half_type(all_rows, width), buf_b=half_type(all_rows, ff), buf_att=half_type(all_rows, width),
-        buf_mid=half_type(all_rows, width), buf_n=half_type(all_rows, width), buf_t=half_type(all_rows, width),
+        buf_mid=half_type(all_rows, width), normed_all=half_type(group, width), heads_grad=half_type(group, 3 * LANES),
+        tail_part=half_type(n_blk, chunk, 3 * LANES), tail_shares=half_type(n_seq - 1, n_blk, chunk // n_seq, 3 * LANES),
+        tail_sum=half_type(n_blk, chunk // n_seq, 3 * LANES), tail_got=half_type(n_blk, chunk // n_seq, 3 * LANES),
+        tail_done=half_type(3, chunk // n_seq, width),
         turned=half_type(width, all_rows),
-        got_tail=half_type(2 * chips * chunk, width),
-        total=half_type(chunk, wide), total_down=half_type(down, width), total_tail=half_type(chunk, width),
+        total=half_type(chunk, wide), total_down=half_type(down, width),
         gain_rows=full_type(16, width), gains=full_type(n_blk, 16, LANES), gain_got=full_type(n_blk - 1, 16, LANES),
         gain_sum=full_type(n_seq, 16, LANES),
     )
     dma = pltpu.SemaphoreType.DMA
     sems = dict(
-        load=dma((7,)), asend=dma((4, n_blk)), arecv=dma((4, n_blk)), xsend=dma((6, n_seq)), xrecv=dma((6, n_seq)),
+        load=dma((7,)), asend=dma((5, n_blk)), arecv=dma((5, n_blk)), xsend=dma((4, n_seq)), xrecv=dma((4, n_seq)),
         gusend=dma((2 * ff // TILE,)), gurecv=dma((split[0], n_seq)), actsend=dma((ff // TILE,)),
         actrecv=dma((ff // TILE, n_seq)), ready=pltpu.SemaphoreType.REGULAR,
         csend=dma((4, chips)), crecv=dma((4, chips)), rsend=dma((4, 2)), rrecv=dma((4, 2)), zsend=dma((4, 3)),
         zrecv=dma((4, 2)), gsend=dma((12, n_seq)), grecv=dma((12,)), glocal=dma((12,)),
+        nsend=dma((chips - 1,)), nrecv=dma((chips - 1,)), fsend=dma((chips,)), frecv=dma((chips,)), nlocal=dma((1,)),
+        qsend=dma((n_seq - 1,)), qrecv=dma((n_seq - 1,)), tsend=dma((3, n_seq - 1)), trecv=dma((3, n_seq)),
         hsend=dma((n_blk - 1,)), hrecv=dma((n_blk - 1,)), isend=dma((n_seq - 1,)), irecv=dma((n_seq,)),
     )
     layer, grad_tokens, grad_first, out_gu, out_down, out_out, out_query, out_key, out_value, out_gain = pl.pallas_call(

time: 175 us -> 164 us (0.937)
  Pallas kernels: 174 us -> 162 us
    pallas_call x1, Pallas kernels: 168 us -> 156 us  [local_fast(): pl.pallas_call(functools.partial(layer_kernel, sizes), out_shape=(shape((...]
where the time goes in v4:
time: 164 us; the launch traced here: 163 us
  Pallas kernels  162 us (99%)
    pallas_call x1, Pallas kernels, local_fast(): pl.pallas_call(functools.partial(layer_kernel, sizes), out_shape=(shape((...  156 us
    pallas_call x1, Pallas kernels, finish(): pl.pallas_call(finish_kernel, out_shape=tuple((shape(each, F32) for each...  6.46 us

profile of v4, /device:TPU:8, one launch (start us, length us, event | category | flops | bytes accessed | tf_op | source)
XLA Modules:
  0.0 163.1 jit_solution(5272934472844093927)
XLA Ops:
  0.6 155.9 %layer.1 = (f32[128,1024]{1,0:T(8,128)}, f32[128,1024]{1,0:T(8,128)}, f32[128,1024]{1,0:T(8,128)}, bf16[128,5632]{1,0:T(8,128)(2,1)}, bf16[352,1024]{1,0:T(8,128...) custom-call(f32[1,128]{1,0:T(1,128)} %constant.2.clone.freq, ...), custom_call_target="tpu_custom_call" | custom-call | tf_op jit(solution)/shard_map/layer/pallas_call | solution.py:1221
  156.6 6.5 %finish.1 = (f32[128,1024]{1,0:T(8,128)}, f32[128,1024]{1,0:T(8,128)}, f32[128,1024]{1,0:T(8,128)}, f32[1,128]{1,0:T(1,128)}, f32[1,128]{1,0:T(1,128)}, /*index=...) custom-call(f32[128,1024]{1,0:T(8,128)} %get-tuple-element.34.layer,, ...), custom_call_target="tpu_custom_call" | custom-call | tf_op jit(solution)/shard_map/finish/pallas_call | solution.py:1104

commit v5 on v4

--- a/solution.py
+++ b/solution.py
@@ -349,12 +349,21 @@
 
 
 class Spread:
-    def __init__(self, seq, n_seq, owner, kind, src, dst, send, recv, local):
-        self.seq, self.n_seq, self.owner, self.kind, self.src, self.dst = seq, n_seq, owner, kind, src, dst
-        self.send, self.recv, self.local = send, recv, local
-
-    def copy(self, other):
-        return remote(self.src, self.dst, self.send.at[self.kind, other], self.recv.at[self.kind], {"seq": other})
+    def __init__(self, seq, owner, kind, src, dst, send, recv, local, on_send, on_recv):
+        self.seq, self.owner, self.kind, self.src, self.dst = seq, owner, kind, src, dst
+        self.send, self.recv, self.local, self.on_send, self.on_recv = send, recv, local, on_send, on_recv
+        self.half = src.shape[0] // 2
+
+    def copy(self, bit):
+        return remote(
+            self.src, self.dst, self.send.at[self.kind, bit], self.recv.at[self.kind], {"seq": self.owner ^ (bit + 1)}
+        )
+
+    def onward(self, bit):
+        part = self.dst.at[bit * self.half : (bit + 1) * self.half]
+        return remote(
+            part, part, self.on_send.at[self.kind, bit], self.on_recv.at[self.kind, bit], {"seq": self.owner ^ 3}
+        )
 
     def own(self):
         return pltpu.make_async_copy(self.src, self.dst, self.local.at[self.kind])
@@ -362,22 +371,35 @@
     def start(self):
         @pl.when(self.seq == self.owner)
         def _():
-            for other in range(self.n_seq):
-                if other != self.owner:
-                    self.copy(other).start()
+            for bit in range(2):
+                self.copy(bit).start()
             self.own().start()
+
+    def pass_on(self):
+        for bit in range(2):
+
+            @pl.when(self.seq == self.owner ^ (bit + 1))
+            def _(bit=bit):
+                self.copy(bit).wait_recv()
+                self.onward(bit).start()
 
     def finish(self):
         @pl.when(self.seq == self.owner)
         def _():
-            for other in range(self.n_seq):
-                if other != self.owner:
-                    self.copy(other).wait_send()
+            for bit in range(2):
+                self.copy(bit).wait_send()
             self.own().wait()
 
-        @pl.when(self.seq != self.owner)
+        for bit in range(2):
+
+            @pl.when(self.seq == self.owner ^ (bit + 1))
+            def _(bit=bit):
+                self.onward(bit).wait_send()
+
+        @pl.when(self.seq == self.owner ^ 3)
         def _():
-            self.copy(self.owner).wait_recv()
+            for bit in range(2):
+                self.onward(bit).wait_recv()
 
 
 def turn_over(src, dst):
@@ -564,7 +586,9 @@
         for core in range(2):
             give_qkv.arrived(2 * block + core)
         at, both = span(block * TILE, TILE, TILE), span(block * 2 * TILE, 2 * TILE, 2 * TILE)
-        v.q2[both, :] = stacked(v.qkv[0, at, :].astype(F32)).astype(BF16)
+        queries = stacked(v.qkv[0, at, :].astype(F32)).astype(BF16)
+        v.q2[both, :] = queries
+        v.q2_turned[:, both] = queries.T
         index = block * TILE + lax.rem(iota((2 * TILE, 1), 0), TILE)
         start = doc_start(index)
         v.top[...] = jnp.full((2 * TILE, LANES), NEG, F32)
@@ -612,8 +636,8 @@
     )
     give_att.all_arrived()
     gift_att.start()
-    for step in range(1, chips):
-        normed_out(step).start()
+    normed_out(1).start()
+    normed_out(3).start()
 
     load_out.wait()
 
@@ -621,7 +645,6 @@
         cols = span(tile * TILE, TILE, TILE)
         value = tokens[:, cols].astype(F32) + times(v.att[...], v.w_out[:, cols])
         v.mid[:, cols] = value
-        o_layer[:, cols] = value
 
     loop(0, width // TILE, middle)
 
@@ -657,12 +680,9 @@
         gift_gu.start(tile)
         gift_gu.start(hidden + tile)
         gift_act.start(tile)
-        o_layer[...] += times(act, v.w_down[cols, :])
         v.two_grad[...] += back(gate_grad, v.w_gate[:, cols]) + back(up_grad, v.w_up[:, cols])
 
     loop(0, hidden, feed)
-    for step in range(1, n_blk):
-        pl.semaphore_signal(sem.ready, inc=1, device_id={"blk": lax.rem(blk + step, n_blk)}, device_id_type=MESH)
     v.gain_rows[...] = jnp.zeros((16, width), F32)
 
     def norm_two_back(group):
@@ -687,13 +707,19 @@
             give_out.start(2 * chip + core)
 
     loop(1, chips + 1, out_back)
+    normed_out(2).start()
+
+    def layer_out(tile):
+        cols = span(tile * TILE, TILE, TILE)
+        o_layer[:, cols] = v.mid[:, cols] + times(v.act[...], v.w_down[:, cols])
+
+    loop(0, width // TILE, layer_out)
     own_normed.wait()
     normed_over(0).start()
-    for step in range(1, chips):
+    for step in (1, 3):
         normed_out(chips - step).wait_recv()
         normed_over(step).start()
 
-    pl.semaphore_wait(sem.ready, n_blk - 1)
     chunk, down = width // n_blk, ff // n_blk
 
     def sems_of(index):
@@ -704,11 +730,11 @@
     def stack_in(ref, top, cols):
         return lambda index: ref.at[span(top + index * chunk, chunk, 32), cols]
 
-    def square_in(ref, more, low):
+    def square_in(ref, more, low, high):
         def place(index):
             index = index + more
             return ref.at[
-                span(lax.rem(index, 2) * down, down, 32), span(lax.div(index, 2) * width + low, TILE, TILE)
+                span(lax.rem(index, 2) * down, down, 32), span(lax.div(index, 2) * width + low, high - low, LANES)
             ]
 
         return place
@@ -720,23 +746,24 @@
             stack_in(v.w_up, (chips + 2) * chunk, cols), v.total.at[:, cols], sems_of(index),
         )
 
-    third = -(-each // 3)
-    edges = [0, third, 2 * third, each]
+    edges = [0, each // 3, 7 * each // 9, each]
     thirds = [piece(index, edges[index] * TILE, edges[index + 1] * TILE) for index in range(3)]
     last = split[2] * TILE
     halves = [piece(0, 0, last), piece(1, last, last + width)]
-    quarters = [
+    bounds = [0, width // 4, width // 2, 3 * width // 4, 7 * width // 8, width]
+    fifths = [
         Sum(
-            blk, down, v.w_down.at[:, low : low + TILE], square_in(v.w_up, 0, low), square_in(v.w_gate, 0, low),
-            square_in(v.w_gate, 2, low), v.total_down.at[:, low : low + TILE], sems_of(low // TILE),
+            blk, down, v.w_down.at[:, low:high], square_in(v.w_up, 0, low, high), square_in(v.w_gate, 0, low, high),
+            square_in(v.w_gate, 2, low, high), v.total_down.at[:, low:high], sems_of(index),
         )
-        for low in range(0, width, TILE)
+        for index, (low, high) in enumerate(zip(bounds[:-1], bounds[1:]))
     ]
-
     first_two, third_one, fourth = seq < 2, seq == 2, seq == 3
 
     def spread(owner, kind, src, dst):
-        return Spread(seq, n_seq, owner, kind, src, dst, sem.gsend, sem.grecv, sem.glocal)
+        return Spread(
+            seq, owner, kind, src, dst, sem.gsend, sem.grecv, sem.glocal, sem.onsend, sem.onrecv
+        )
 
     spreads = [
         [
@@ -755,25 +782,26 @@
             spread(2, 7, v.total.at[:, last : last + width], o_out),
         ],
         [
-            spread(3, 8 + index, v.total_down.at[:, low : low + TILE], o_down.at[:, low : low + TILE])
-            for index, low in enumerate(range(0, width, TILE))
+            spread(3, 8 + index, v.total_down.at[:, low:high], o_down.at[:, low:high])
+            for index, (low, high) in enumerate(zip(bounds[:-1], bounds[1:]))
         ],
     ]
     def products(item, turned, rhs, tiles, rhs_at, part_at):
         def one(step):
             chip = item.order(step)
             outer_tiles(turned, rhs, v.w_gate, chip, tiles, rhs_at, part_at)
-            item.swap(chip).start()
 
         loop(0, chips, one)
-        item.begin()
+
+    def swaps(item):
+        loop(0, chips, lambda step: item.swap(item.order(step)).start())
 
     def gate_up_piece(index):
         gift_gu.arrived(edges[index], edges[index + 1])
         at = edges[index] * TILE
         products(thirds[index], v.turned, v.buf_b, edges[index + 1] - edges[index], at, at)
 
-    def down_products():
+    def down_products(low, high):
         def one(step):
             index = lax.rem(split[0] + step, hidden)
             gift_act.arrived(index, index + 1)
@@ -781,11 +809,11 @@
             v.turned[:TILE, :] = v.buf_b[:, at].T
             v.w_down[at, :] = times(v.turned[:TILE, :], v.buf_a[...]).astype(BF16)
 
-        loop(0, hidden, one)
-        for item in quarters:
-            loop(0, chips, lambda step, item=item: item.swap(item.order(step)).start())
-        for item in quarters:
-            item.begin()
+        loop(low, high, one)
+
+    def down_swaps():
+        for item in fifths:
+            swaps(item)
 
     for owner in range(n_seq):
 
@@ -796,14 +824,23 @@
     @pl.when(first_two)
     def _():
         turn_over(v.buf_a, v.turned)
-        gate_up_piece(0)
+
+    @pl.when(third_one)
+    def _():
+        turn_over(v.buf_a, v.turned)
+
+    @pl.when(fourth)
+    def _():
+        down_products(0, hidden // 2)
 
     give_out.all_arrived()
+
 
     def prepare(block):
         at, both = span(block * TILE, TILE, TILE), span(block * 2 * TILE, 2 * TILE, 2 * TILE)
         grad = (stacked(v.out_grad[at, :].astype(F32)) * v.row[both, :]).astype(BF16)
         v.do2[both, :] = grad
+        v.do2_turned[:, both] = grad.T
         attended = v.o32[at, :]
         delta = jnp.sum(grad.astype(F32) * jnp.concatenate([attended, attended], axis=0), axis=1, keepdims=True)
         v.row[both, :] = jnp.broadcast_to(delta, (2 * TILE, LANES))
@@ -814,16 +851,16 @@
 
     def key_block(block):
         at = span(block * TILE, TILE, TILE)
-        v.dk[...] = jnp.zeros((TILE, LANES), F32)
-        v.dv[...] = jnp.zeros((TILE, LANES), F32)
+        v.dk[...] = jnp.zeros((LANES, TILE), F32)
+        v.dv[...] = jnp.zeros((LANES, TILE), F32)
 
         def query_block(other):
             both = span(other * 2 * TILE, 2 * TILE, 2 * TILE)
             prob = v.prob[both, at]
             grad = back(v.do2[both, :], v.qkv[2, at, :])
             score_grad = (prob.astype(F32) * (grad - v.row[both, :1])).astype(BF16)
-            v.dk[...] += outer(score_grad, v.q2[both, :])
-            v.dv[...] += outer(prob, v.do2[both, :])
+            v.dk[...] += times(v.q2_turned[:, both], score_grad)
+            v.dv[...] += times(v.do2_turned[:, both], prob)
             v.dq[both, :] += times(score_grad, v.qkv[1, at, :])
 
         loop(block, chips, query_block)
@@ -835,8 +872,8 @@
             return (u * cosine - halves_changed(u) * sine).astype(BF16)
 
         dq = rotated_back(unstacked(v.dq[span(block * 2 * TILE, 2 * TILE, 2 * TILE), :]) * scale)
-        dk = rotated_back(v.dk[...])
-        dv = (MIX * v.dv[...].astype(BF16).astype(F32)).astype(BF16)
+        dk = rotated_back(v.dk[...].T)
+        dv = (MIX * v.dv[...].T.astype(BF16).astype(F32)).astype(BF16)
         for index, value in enumerate((dq, dk, dv)):
             v.heads_grad[at, index * LANES : (index + 1) * LANES] = value
             for half_at in range(2):
@@ -846,6 +883,43 @@
 
     loop(0, chips, key_block)
 
+    def when(which, *steps):
+        @pl.when(which)
+        def _():
+            for step in steps:
+                step()
+
+    def ended(item, goes):
+        def step():
+            item.end()
+            for other in goes:
+                other.start()
+
+        return step
+
+    def first_half():
+        gift_gu.arrived(0, split[2])
+        products(halves[0], v.turned, v.buf_b, split[2], 0, 0)
+        swaps(halves[0])
+        halves[0].begin()
+
+    def second_half():
+        gift_att.arrived()
+        gift_mid.arrived()
+        turn_over(v.buf_att, v.turned)
+        products(halves[1], v.turned, v.buf_mid, width // TILE, 0, last)
+        swaps(halves[1])
+
+    def gate_up_gone(index):
+        gate_up_piece(index)
+        swaps(thirds[index])
+
+    when(first_two, lambda: gate_up_gone(0), thirds[0].begin)
+    when(third_one, first_half)
+    when(fourth, lambda: down_products(hidden // 2, hidden), down_swaps, fifths[0].begin)
+
+    normed_out(2).wait_recv()
+    normed_over(2).start()
     for step in range(chips):
         mates_normed(step).wait_recv()
 
@@ -870,32 +944,8 @@
     for step in range(1, n_seq):
         tail_share(step).start()
 
-    def when(which, *steps):
-        @pl.when(which)
-        def _():
-            for step in steps:
-                step()
-
-    def ended(item, goes):
-        def step():
-            item.end()
-            for other in goes:
-                other.start()
-
-        return step
-
-    def third_products():
-        turn_over(v.buf_a, v.turned)
-        gift_gu.arrived(0, split[2])
-        products(halves[0], v.turned, v.buf_b, split[2], 0, 0)
-        gift_att.arrived()
-        gift_mid.arrived()
-        turn_over(v.buf_att, v.turned)
-        products(halves[1], v.turned, v.buf_mid, width // TILE, 0, last)
-
-    when(first_two, lambda: gate_up_piece(1), thirds[0].relay, lambda: gate_up_piece(2))
-    when(third_one, third_products)
-    when(fourth, down_products)
+    when(first_two, lambda: gate_up_gone(1), thirds[1].begin, thirds[0].relay, lambda: gate_up_gone(2))
+    when(third_one, second_half)
 
     def tail_add(index):
         value = v.tail_part[index, span(seq * quarter, quarter, quarter), :].astype(F32)
@@ -907,6 +957,9 @@
     for step in range(1, n_seq):
         tail_share(step).wait()
     loop(0, n_blk, tail_add)
+    when(first_two, thirds[2].begin)
+    when(third_one, halves[1].begin)
+    when(fourth, fifths[1].begin)
 
     give_grads.all_arrived()
 
@@ -916,7 +969,7 @@
     when(first_two, thirds[1].relay, ended(thirds[0], []))
     for item in gone(0, 0, 1):
         item.start()
-    when(fourth, quarters[0].relay)
+    when(fourth, fifths[0].relay, fifths[2].begin)
 
     def normed_back(tile):
         at = span(tile * TILE, TILE, TILE)
@@ -928,7 +981,6 @@
 
     loop(0, width // TILE, normed_back)
     o_first[...] = v.grads[2].astype(F32)
-    when(fourth, ended(quarters[0], gone(0, 3)), quarters[1].relay)
 
     def norm_back(group):
         at = span(group * GROUP, GROUP, GROUP)
@@ -953,28 +1005,12 @@
 
     for step in range(1, n_blk):
         gain_copy(step).start()
-
-    when(
-        first_two,
-        ended(thirds[1], gone(1, 0, 1)),
-        thirds[2].relay,
-        ended(thirds[2], gone(2, 0, 1)),
-    )
-    when(
-        third_one,
-        halves[0].relay,
-        ended(halves[0], gone(0, 2)),
-        halves[1].relay,
-        ended(halves[1], gone(1, 2)),
-    )
-    when(
-        fourth,
-        ended(quarters[1], gone(1, 3)),
-        quarters[2].relay,
-        ended(quarters[2], gone(2, 3)),
-        quarters[3].relay,
-        ended(quarters[3], gone(3, 3)),
-    )
+    when(fourth, ended(fifths[0], gone(0, 3)), fifths[1].relay, fifths[3].begin, fifths[4].begin)
+
+    when(first_two, ended(thirds[1], gone(1, 0, 1)))
+    when(third_one, halves[0].relay, ended(halves[0], gone(0, 2)))
+    when(fourth, ended(fifths[1], gone(1, 3)))
+
     give_tail.all_arrived()
     for index in range(3):
         for peer in range(n_blk):
@@ -1003,6 +1039,21 @@
         for step in range(1, n_seq):
             tail_spread(index, step, seq).start()
 
+    def pass_on(*items):
+        for item in items:
+            item.pass_on()
+
+    pass_on(*gone(0, 0, 1, 3))
+    when(first_two, thirds[2].relay, ended(thirds[2], gone(2, 0, 1)))
+    when(third_one, halves[1].relay, ended(halves[1], gone(1, 2)))
+    when(
+        fourth,
+        fifths[2].relay,
+        ended(fifths[2], gone(2, 3)),
+        fifths[3].relay,
+        ended(fifths[3], gone(3, 3)),
+    )
+    pass_on(*gone(0, 2), *gone(1, 3, 0, 1))
     value = v.gains[blk]
     for step in range(1, n_blk):
         gain_copy(step).wait()
@@ -1012,6 +1063,9 @@
         other = lax.rem(seq + step, n_seq)
         mine = v.gain_sum.at[seq]
         remote(mine, mine, sem.isend.at[step - 1], sem.irecv.at[seq], {"seq": other}).start()
+
+    when(fourth, fifths[4].relay, ended(fifths[4], gone(4, 3)))
+    pass_on(*gone(1, 2), *gone(2, 3, 0, 1), *gone(3, 3), *gone(4, 3))
 
     for step in range(1, n_seq):
         other = lax.rem(seq + step, n_seq)
@@ -1053,7 +1107,7 @@
 
     @pl.when(fourth)
     def _():
-        for item in quarters:
+        for item in fifths:
             item.left()
 
 
@@ -1191,7 +1245,8 @@
         q2=half_type(2 * group, LANES), do2=half_type(2 * group, LANES), prob=half_type(2 * group, group),
         score=full_type(2 * TILE, group), top=full_type(2 * TILE, LANES), o2=full_type(2 * TILE, LANES),
         row=full_type(2 * group, LANES), o32=full_type(group, LANES), ob=half_type(group, LANES),
-        dq=full_type(2 * group, LANES), dk=full_type(TILE, LANES), dv=full_type(TILE, LANES),
+        dq=full_type(2 * group, LANES), dk=full_type(LANES, TILE), dv=full_type(LANES, TILE),
+        q2_turned=half_type(LANES, 2 * group), do2_turned=half_type(LANES, 2 * group),
         att=half_type(rows, width), mid=full_type(rows, width), two=half_type(rows, width),
         act=half_type(rows, ff), gate_up=half_type(rows, 2 * ff), two_grad=full_type(rows, width),
         mid_grad=full_type(rows, width), mid_b=half_type(rows, width),
@@ -1211,9 +1266,9 @@
     sems = dict(
         load=dma((7,)), asend=dma((5, n_blk)), arecv=dma((5, n_blk)), xsend=dma((4, n_seq)), xrecv=dma((4, n_seq)),
         gusend=dma((2 * ff // TILE,)), gurecv=dma((split[0], n_seq)), actsend=dma((ff // TILE,)),
-        actrecv=dma((ff // TILE, n_seq)), ready=pltpu.SemaphoreType.REGULAR,
-        csend=dma((4, chips)), crecv=dma((4, chips)), rsend=dma((4, 2)), rrecv=dma((4, 2)), zsend=dma((4, 3)),
-        zrecv=dma((4, 2)), gsend=dma((12, n_seq)), grecv=dma((12,)), glocal=dma((12,)),
+        actrecv=dma((ff // TILE, n_seq)),
+        csend=dma((5, chips)), crecv=dma((5, chips)), rsend=dma((5, 2)), rrecv=dma((5, 2)), zsend=dma((5, 3)),
+        zrecv=dma((5, 2)), gsend=dma((13, 2)), grecv=dma((13,)), glocal=dma((13,)), onsend=dma((13, 2)), onrecv=dma((13, 2)),
         nsend=dma((chips - 1,)), nrecv=dma((chips - 1,)), fsend=dma((chips,)), frecv=dma((chips,)), nlocal=dma((1,)),
         qsend=dma((n_seq - 1,)), qrecv=dma((n_seq - 1,)), tsend=dma((3, n_seq - 1)), trecv=dma((3, n_seq)),
         hsend=dma((n_blk - 1,)), hrecv=dma((n_blk - 1,)), isend=dma((n_seq - 1,)), irecv=dma((n_seq,)),

time: 164 us -> 156 us (0.951)
  Pallas kernels: 162 us -> 154 us
    pallas_call x1, Pallas kernels: 156 us -> 148 us  [local_fast(): pl.pallas_call(functools.partial(layer_kernel, sizes), out_shape=(shape((...]
where the time goes in v5:
time: 156 us; the launch traced here: 155 us
  Pallas kernels  154 us (99%)
    pallas_call x1, Pallas kernels, local_fast(): pl.pallas_call(functools.partial(layer_kernel, sizes), out_shape=(shape((...  148 us
    pallas_call x1, Pallas kernels, finish(): pl.pallas_call(finish_kernel, out_shape=tuple((shape(each, F32) for each...  6.46 us

profile of v5, /device:TPU:8, one launch (start us, length us, event | category | flops | bytes accessed | tf_op | source)
XLA Modules:
  0.0 154.7 jit_solution(15091433443651814309)
XLA Ops:
  0.6 147.6 %layer.1 = (f32[128,1024]{1,0:T(8,128)}, f32[128,1024]{1,0:T(8,128)}, f32[128,1024]{1,0:T(8,128)}, bf16[128,5632]{1,0:T(8,128)(2,1)}, bf16[352,1024]{1,0:T(8,128...) custom-call(f32[1,128]{1,0:T(1,128)} %constant.2.clone.freq, ...), custom_call_target="tpu_custom_call" | custom-call | tf_op jit(solution)/shard_map/layer/pallas_call | solution.py:1276
  148.3 6.5 %finish.1 = (f32[128,1024]{1,0:T(8,128)}, f32[128,1024]{1,0:T(8,128)}, f32[128,1024]{1,0:T(8,128)}, f32[1,128]{1,0:T(1,128)}, f32[1,128]{1,0:T(1,128)}, /*index=...) custom-call(f32[128,1024]{1,0:T(8,128)} %get-tuple-element.34.layer,, ...), custom_call_target="tpu_custom_call" | custom-call | tf_op jit(solution)/shard_map/finish/pallas_call | solution.py:1158

commit v6 on v5

--- a/solution.py
+++ b/solution.py
@@ -574,6 +574,14 @@
 
     loop(1, chips + 1, project)
 
+    load_down.wait()
+
+    def act_back(tile):
+        cols = span(tile * TILE, TILE, TILE)
+        v.act_grad[:, cols] = back(cot[...], v.w_down[cols, :])
+
+    loop(0, ff // TILE, act_back)
+
     first_head = iota((TILE, LANES), 1) < HEAD_DIM
 
     def stacked(values):
@@ -659,7 +667,7 @@
     for item in gifts_two:
         item.start()
 
-    for item in (load_gate, load_up, load_down):
+    for item in (load_gate, load_up):
         item.wait()
     v.two_grad[...] = jnp.zeros((rows, width), F32)
 
@@ -668,7 +676,7 @@
         cols = span(tile * TILE, TILE, TILE)
         gate = times(v.two[...], v.w_gate[:, cols])
         up = times(v.two[...], v.w_up[:, cols])
-        act_grad = back(cot[...], v.w_down[cols, :])
+        act_grad = v.act_grad[:, cols]
         sigma = jax.nn.sigmoid(gate)
         silu = gate * sigma
         act = (silu * up).astype(BF16)
@@ -707,7 +715,6 @@
             give_out.start(2 * chip + core)
 
     loop(1, chips + 1, out_back)
-    normed_out(2).start()
 
     def layer_out(tile):
         cols = span(tile * TILE, TILE, TILE)
@@ -815,25 +822,20 @@
         for item in fifths:
             swaps(item)
 
-    for owner in range(n_seq):
+    for owner in range(2):
 
         @pl.when(seq == owner)
         def _(owner=owner):
-            (gifts_two + [gift_cot])[owner].arrived()
-
-    @pl.when(first_two)
-    def _():
-        turn_over(v.buf_a, v.turned)
-
-    @pl.when(third_one)
-    def _():
-        turn_over(v.buf_a, v.turned)
+            gifts_two[owner].arrived()
+            turn_over(v.buf_a, v.turned)
 
     @pl.when(fourth)
     def _():
-        down_products(0, hidden // 2)
+        gift_cot.arrived()
+        down_products(0, hidden // 4)
 
     give_out.all_arrived()
+    normed_out(2).start()
 
 
     def prepare(block):
@@ -898,6 +900,8 @@
         return step
 
     def first_half():
+        gifts_two[2].arrived()
+        turn_over(v.buf_a, v.turned)
         gift_gu.arrived(0, split[2])
         products(halves[0], v.turned, v.buf_b, split[2], 0, 0)
         swaps(halves[0])
@@ -914,9 +918,9 @@
         gate_up_piece(index)
         swaps(thirds[index])
 
-    when(first_two, lambda: gate_up_gone(0), thirds[0].begin)
+    when(first_two, lambda: gate_up_gone(0), thirds[0].begin, lambda: gate_up_gone(1), thirds[1].begin)
     when(third_one, first_half)
-    when(fourth, lambda: down_products(hidden // 2, hidden), down_swaps, fifths[0].begin)
+    when(fourth, lambda: down_products(hidden // 4, hidden), down_swaps, fifths[0].begin, fifths[1].begin)
 
     normed_out(2).wait_recv()
     normed_over(2).start()
@@ -944,7 +948,7 @@
     for step in range(1, n_seq):
         tail_share(step).start()
 
-    when(first_two, lambda: gate_up_gone(1), thirds[1].begin, thirds[0].relay, lambda: gate_up_gone(2))
+    when(first_two, thirds[0].relay, lambda: gate_up_gone(2))
     when(third_one, second_half)
 
     def tail_add(index):
@@ -959,7 +963,6 @@
     loop(0, n_blk, tail_add)
     when(first_two, thirds[2].begin)
     when(third_one, halves[1].begin)
-    when(fourth, fifths[1].begin)
 
     give_grads.all_arrived()
 
@@ -1046,13 +1049,8 @@
     pass_on(*gone(0, 0, 1, 3))
     when(first_two, thirds[2].relay, ended(thirds[2], gone(2, 0, 1)))
     when(third_one, halves[1].relay, ended(halves[1], gone(1, 2)))
-    when(
-        fourth,
-        fifths[2].relay,
-        ended(fifths[2], gone(2, 3)),
-        fifths[3].relay,
-        ended(fifths[3], gone(3, 3)),
-    )
+    when(fourth, fifths[2].relay, fifths[3].relay, ended(fifths[2], gone(2, 3)))
+    when(fourth, fifths[4].relay, ended(fifths[3], gone(3, 3)), ended(fifths[4], gone(4, 3)))
     pass_on(*gone(0, 2), *gone(1, 3, 0, 1))
     value = v.gains[blk]
     for step in range(1, n_blk):
@@ -1064,7 +1062,6 @@
         mine = v.gain_sum.at[seq]
         remote(mine, mine, sem.isend.at[step - 1], sem.irecv.at[seq], {"seq": other}).start()
 
-    when(fourth, fifths[4].relay, ended(fifths[4], gone(4, 3)))
     pass_on(*gone(1, 2), *gone(2, 3, 0, 1), *gone(3, 3), *gone(4, 3))
 
     for step in range(1, n_seq):
@@ -1125,24 +1122,24 @@
         for index, dst in enumerate((o_layer, o_tokens, o_first))
     ]
     ff = o_gate.shape[1]
-    sources = [gu.at[:, :ff], gu.at[:, ff:], down, query, key, value, out]
-    targets = [o_gate, o_up, o_down, o_query, o_key, o_value, o_out]
+    sources = [query, key, value, out, down, gu.at[:, :ff], gu.at[:, ff:]]
+    targets = [o_query, o_key, o_value, o_out, o_down, o_gate, o_up]
     loads = [pltpu.make_async_copy(src, small[index], sem_in.at[index]) for index, src in enumerate(sources)]
     stores = [pltpu.make_async_copy(large[index], dst, sem_out.at[index]) for index, dst in enumerate(targets)]
-    for item in kept_in + loads:
+    for item in loads + kept_in:
         item.start()
+    for index in range(len(sources)):
+        loads[index].wait()
+
+        def group(step, index=index):
+            at = span(step * GROUP, GROUP, GROUP)
+            large[index][at, :] = small[index][at, :].astype(F32)
+
+        loop(0, targets[index].shape[0] // GROUP, group)
+        stores[index].start()
     for coming, going in zip(kept_in, kept_out):
         coming.wait()
         going.start()
-    for index in range(len(sources)):
-        loads[index].wait()
-
-        def group(step, index=index):
-            at = span(step * GROUP, GROUP, GROUP)
-            large[index][at, :] = small[index][at, :].astype(F32)
-
-        loop(0, targets[index].shape[0] // GROUP, group)
-        stores[index].start()
     o_gain[...] = gain[0:1, :]
     o_gain_two[...] = gain[8:9, :]
     for item in stores + kept_out:
@@ -1153,14 +1150,14 @@
     hbm, vmem = pl.BlockSpec(memory_space=pl.ANY), pl.BlockSpec(memory_space=pltpu.VMEM)
     shape = jax.ShapeDtypeStruct
     ff = gu.shape[1] // 2
-    dims = [(gu.shape[0], ff), (gu.shape[0], ff), down.shape, query.shape, key.shape, value.shape, out.shape]
+    dims = [query.shape, key.shape, value.shape, out.shape, down.shape, (gu.shape[0], ff), (gu.shape[0], ff)]
     dma = pltpu.SemaphoreType.DMA
     results = pl.pallas_call(
         finish_kernel,
         out_shape=tuple(
             shape(each, F32)
             for each in (
-                layer.shape, tokens.shape, first.shape, (1, LANES), (1, LANES), dims[3], dims[4], dims[5], dims[6], dims[0], dims[1], dims[2]
+                layer.shape, tokens.shape, first.shape, (1, LANES), (1, LANES), dims[0], dims[1], dims[2], dims[3], dims[5], dims[6], dims[4]
             )
         ),
         in_specs=[hbm] * 9 + [vmem],
@@ -1248,7 +1245,7 @@
         dq=full_type(2 * group, LANES), dk=full_type(LANES, TILE), dv=full_type(LANES, TILE),
         q2_turned=half_type(LANES, 2 * group), do2_turned=half_type(LANES, 2 * group),
         att=half_type(rows, width), mid=full_type(rows, width), two=half_type(rows, width),
-        act=half_type(rows, ff), gate_up=half_type(rows, 2 * ff), two_grad=full_type(rows, width),
+        act=half_type(rows, ff), act_grad=full_type(rows, ff), gate_up=half_type(rows, 2 * ff), two_grad=full_type(rows, width),
         mid_grad=full_type(rows, width), mid_b=half_type(rows, width),
         out_pack=half_type(n_blk, rows, LANES), out_grad=half_type(group, LANES),
         grads=half_type(3, rows, width),

time: 156 us -> 153 us (0.981)
  Pallas kernels: 154 us -> 152 us
where the time goes in v6:
time: 153 us
  Pallas kernels  152 us (99%)
    pallas_call x1, Pallas kernels, local_fast(): pl.pallas_call(functools.partial(layer_kernel, sizes), out_shape=(shape((...  146 us
    pallas_call x1, Pallas kernels, finish(): pl.pallas_call(finish_kernel, out_shape=tuple((shape(each, F32) for each...  5.58 us

profile of v6, /device:TPU:8, one launch (start us, length us, event | category | flops | bytes accessed | tf_op | source)
XLA Modules:
  0.0 152.7 jit_solution(9468734728670137528)
XLA Ops:
  0.6 146.5 %layer.1 = (f32[128,1024]{1,0:T(8,128)}, f32[128,1024]{1,0:T(8,128)}, f32[128,1024]{1,0:T(8,128)}, bf16[128,5632]{1,0:T(8,128)(2,1)}, bf16[352,1024]{1,0:T(8,128...) custom-call(f32[1,128]{1,0:T(1,128)} %constant.2.clone.freq, ...), custom_call_target="tpu_custom_call" | custom-call | tf_op jit(solution)/shard_map/layer/pallas_call | solution.py:1273
  147.1 5.6 %finish.1 = (f32[128,1024]{1,0:T(8,128)}, f32[128,1024]{1,0:T(8,128)}, f32[128,1024]{1,0:T(8,128)}, f32[1,128]{1,0:T(1,128)}, f32[1,128]{1,0:T(1,128)}, /*index=...) custom-call(f32[128,1024]{1,0:T(8,128)} %get-tuple-element.34.layer,, ...), custom_call_target="tpu_custom_call" | custom-call | tf_op jit(solution)/shard_map/finish/pallas_call | solution.py:1155

commit v7 on v6

--- a/solution.py
+++ b/solution.py
@@ -753,7 +753,7 @@
             stack_in(v.w_up, (chips + 2) * chunk, cols), v.total.at[:, cols], sems_of(index),
         )
 
-    edges = [0, each // 3, 7 * each // 9, each]
+    edges = [0, each // 3, 2 * each // 3, each]
     thirds = [piece(index, edges[index] * TILE, edges[index + 1] * TILE) for index in range(3)]
     last = split[2] * TILE
     halves = [piece(0, 0, last), piece(1, last, last + width)]
@@ -1050,8 +1050,6 @@
     when(first_two, thirds[2].relay, ended(thirds[2], gone(2, 0, 1)))
     when(third_one, halves[1].relay, ended(halves[1], gone(1, 2)))
     when(fourth, fifths[2].relay, fifths[3].relay, ended(fifths[2], gone(2, 3)))
-    when(fourth, fifths[4].relay, ended(fifths[3], gone(3, 3)), ended(fifths[4], gone(4, 3)))
-    pass_on(*gone(0, 2), *gone(1, 3, 0, 1))
     value = v.gains[blk]
     for step in range(1, n_blk):
         gain_copy(step).wait()
@@ -1062,7 +1060,9 @@
         mine = v.gain_sum.at[seq]
         remote(mine, mine, sem.isend.at[step - 1], sem.irecv.at[seq], {"seq": other}).start()
 
-    pass_on(*gone(1, 2), *gone(2, 3, 0, 1), *gone(3, 3), *gone(4, 3))
+    when(fourth, fifths[4].relay, ended(fifths[3], gone(3, 3)), ended(fifths[4], gone(4, 3)))
+    pass_on(*gone(0, 2), *gone(1, 3, 0, 1))
+    pass_on(*gone(2, 0, 1, 3), *gone(1, 2), *gone(3, 3), *gone(4, 3))
 
     for step in range(1, n_seq):
         other = lax.rem(seq + step, n_seq)

time: 153 us -> 150 us (0.980)
  Pallas kernels: 152 us -> 149 us
    pallas_call x1, Pallas kernels: 146 us -> 143 us  [local_fast(): pl.pallas_call(functools.partial(layer_kernel, sizes), out_shape=(shape((...]
where the time goes in v7:
time: 150 us
  Pallas kernels  149 us (99%)
    pallas_call x1, Pallas kernels, local_fast(): pl.pallas_call(functools.partial(layer_kernel, sizes), out_shape=(shape((...  143 us
    pallas_call x1, Pallas kernels, finish(): pl.pallas_call(finish_kernel, out_shape=tuple((shape(each, F32) for each...  5.58 us

profile of v7, /device:TPU:8, one launch (start us, length us, event | category | flops | bytes accessed | tf_op | source)
XLA Modules:
  0.0 149.7 jit_solution(3928433296678954964)
XLA Ops:
  0.6 143.5 %layer.1 = (f32[128,1024]{1,0:T(8,128)}, f32[128,1024]{1,0:T(8,128)}, f32[128,1024]{1,0:T(8,128)}, bf16[128,5632]{1,0:T(8,128)(2,1)}, bf16[352,1024]{1,0:T(8,128...) custom-call(f32[1,128]{1,0:T(1,128)} %constant.2.clone.freq, ...), custom_call_target="tpu_custom_call" | custom-call | tf_op jit(solution)/shard_map/layer/pallas_call | solution.py:1273
  144.1 5.6 %finish.1 = (f32[128,1024]{1,0:T(8,128)}, f32[128,1024]{1,0:T(8,128)}, f32[128,1024]{1,0:T(8,128)}, f32[1,128]{1,0:T(1,128)}, f32[1,128]{1,0:T(1,128)}, /*index=...) custom-call(f32[128,1024]{1,0:T(8,128)} %get-tuple-element.34.layer,, ...), custom_call_target="tpu_custom_call" | custom-call | tf_op jit(solution)/shard_map/finish/pallas_call | solution.py:1155

commit v8 on v7

--- a/solution.py
+++ b/solution.py
@@ -757,7 +757,7 @@
     thirds = [piece(index, edges[index] * TILE, edges[index + 1] * TILE) for index in range(3)]
     last = split[2] * TILE
     halves = [piece(0, 0, last), piece(1, last, last + width)]
-    bounds = [0, width // 4, width // 2, 3 * width // 4, 7 * width // 8, width]
+    bounds = [0, width // 8, 3 * width // 8, 5 * width // 8, 7 * width // 8, width]
     fifths = [
         Sum(
             blk, down, v.w_down.at[:, low:high], square_in(v.w_up, 0, low, high), square_in(v.w_gate, 0, low, high),
@@ -834,9 +834,6 @@
         gift_cot.arrived()
         down_products(0, hidden // 4)
 
-    give_out.all_arrived()
-    normed_out(2).start()
-
 
     def prepare(block):
         at, both = span(block * TILE, TILE, TILE), span(block * 2 * TILE, 2 * TILE, 2 * TILE)
@@ -848,7 +845,12 @@
         v.row[both, :] = jnp.broadcast_to(delta, (2 * TILE, LANES))
         v.dq[both, :] = jnp.zeros((2 * TILE, LANES), F32)
 
-    loop(0, chips, prepare)
+    for chip in (0, 2, 3, 1):
+        for side in range(2):
+            give_out.arrived(2 * chip + side)
+        if chip == 1:
+            normed_out(2).start()
+        prepare(chip)
     give_qkv.all_left()
 
     def key_block(block):
@@ -969,9 +971,6 @@
     def gone(index, *owners):
         return [spreads[owner][index] for owner in owners]
 
-    when(first_two, thirds[1].relay, ended(thirds[0], []))
-    for item in gone(0, 0, 1):
-        item.start()
     when(fourth, fifths[0].relay, fifths[2].begin)
 
     def normed_back(tile):
@@ -984,6 +983,9 @@
 
     loop(0, width // TILE, normed_back)
     o_first[...] = v.grads[2].astype(F32)
+    when(first_two, thirds[1].relay, ended(thirds[0], []))
+    for item in gone(0, 0, 1):
+        item.start()
 
     def norm_back(group):
         at = span(group * GROUP, GROUP, GROUP)

time: 150 us -> 150 us (level)
  no operation moved by 1% of the time
where the time goes in v8:
time: 150 us; the launch traced here: 149 us
  Pallas kernels  149 us (99%)
    pallas_call x1, Pallas kernels, local_fast(): pl.pallas_call(functools.partial(layer_kernel, sizes), out_shape=(shape((...  143 us
    pallas_call x1, Pallas kernels, finish(): pl.pallas_call(finish_kernel, out_shape=tuple((shape(each, F32) for each...  5.58 us

profile of v8, /device:TPU:8, one launch (start us, length us, event | category | flops | bytes accessed | tf_op | source)
XLA Modules:
  0.0 149.4 jit_solution(13853858707548463433)
XLA Ops:
  0.6 143.1 %layer.1 = (f32[128,1024]{1,0:T(8,128)}, f32[128,1024]{1,0:T(8,128)}, f32[128,1024]{1,0:T(8,128)}, bf16[128,5632]{1,0:T(8,128)(2,1)}, bf16[352,1024]{1,0:T(8,128...) custom-call(f32[1,128]{1,0:T(1,128)} %constant.2.clone.freq, ...), custom_call_target="tpu_custom_call" | custom-call | tf_op jit(solution)/shard_map/layer/pallas_call | solution.py:1275
  143.8 5.6 %finish.1 = (f32[128,1024]{1,0:T(8,128)}, f32[128,1024]{1,0:T(8,128)}, f32[128,1024]{1,0:T(8,128)}, f32[1,128]{1,0:T(1,128)}, f32[1,128]{1,0:T(1,128)}, /*index=...) custom-call(f32[128,1024]{1,0:T(8,128)} %get-tuple-element.34.layer,, ...), custom_call_target="tpu_custom_call" | custom-call | tf_op jit(solution)/shard_map/finish/pallas_call | solution.py:1157

commit v9 on v8

--- a/solution.py
+++ b/solution.py
@@ -756,7 +756,8 @@
     edges = [0, each // 3, 2 * each // 3, each]
     thirds = [piece(index, edges[index] * TILE, edges[index + 1] * TILE) for index in range(3)]
     last = split[2] * TILE
-    halves = [piece(0, 0, last), piece(1, last, last + width)]
+    half_out = last + width // 2
+    halves = [piece(0, 0, last), piece(1, last, half_out), piece(2, half_out, last + width)]
     bounds = [0, width // 8, 3 * width // 8, 5 * width // 8, 7 * width // 8, width]
     fifths = [
         Sum(
@@ -786,7 +787,8 @@
     ] + [
         [
             spread(2, 6, v.total.at[:, :last], o_gu.at[:, cuts[2] : cuts[3]]),
-            spread(2, 7, v.total.at[:, last : last + width], o_out),
+            spread(2, 7, v.total.at[:, last:half_out], o_out.at[:, : width // 2]),
+            spread(2, 13, v.total.at[:, half_out : last + width], o_out.at[:, width // 2 :]),
         ],
         [
             spread(3, 8 + index, v.total_down.at[:, low:high], o_down.at[:, low:high])
@@ -913,8 +915,10 @@
         gift_att.arrived()
         gift_mid.arrived()
         turn_over(v.buf_att, v.turned)
-        products(halves[1], v.turned, v.buf_mid, width // TILE, 0, last)
+        products(halves[1], v.turned, v.buf_mid, width // 2 // TILE, 0, last)
         swaps(halves[1])
+        products(halves[2], v.turned, v.buf_mid, width // 2 // TILE, width // 2, half_out)
+        swaps(halves[2])
 
     def gate_up_gone(index):
         gate_up_piece(index)
@@ -964,7 +968,7 @@
         tail_share(step).wait()
     loop(0, n_blk, tail_add)
     when(first_two, thirds[2].begin)
-    when(third_one, halves[1].begin)
+    when(third_one, halves[1].begin, halves[2].begin)
 
     give_grads.all_arrived()
 
@@ -1050,7 +1054,13 @@
 
     pass_on(*gone(0, 0, 1, 3))
     when(first_two, thirds[2].relay, ended(thirds[2], gone(2, 0, 1)))
-    when(third_one, halves[1].relay, ended(halves[1], gone(1, 2)))
+    when(
+        third_one,
+        halves[1].relay,
+        ended(halves[1], gone(1, 2)),
+        halves[2].relay,
+        ended(halves[2], gone(2, 2)),
+    )
     when(fourth, fifths[2].relay, fifths[3].relay, ended(fifths[2], gone(2, 3)))
     value = v.gains[blk]
     for step in range(1, n_blk):
@@ -1064,7 +1074,7 @@
 
     when(fourth, fifths[4].relay, ended(fifths[3], gone(3, 3)), ended(fifths[4], gone(4, 3)))
     pass_on(*gone(0, 2), *gone(1, 3, 0, 1))
-    pass_on(*gone(2, 0, 1, 3), *gone(1, 2), *gone(3, 3), *gone(4, 3))
+    pass_on(*gone(2, 0, 1, 3), *gone(1, 2), *gone(2, 2), *gone(3, 3), *gone(4, 3))
 
     for step in range(1, n_seq):
         other = lax.rem(seq + step, n_seq)
@@ -1267,7 +1277,7 @@
         gusend=dma((2 * ff // TILE,)), gurecv=dma((split[0], n_seq)), actsend=dma((ff // TILE,)),
         actrecv=dma((ff // TILE, n_seq)),
         csend=dma((5, chips)), crecv=dma((5, chips)), rsend=dma((5, 2)), rrecv=dma((5, 2)), zsend=dma((5, 3)),
-        zrecv=dma((5, 2)), gsend=dma((13, 2)), grecv=dma((13,)), glocal=dma((13,)), onsend=dma((13, 2)), onrecv=dma((13, 2)),
+        zrecv=dma((5, 2)), gsend=dma((14, 2)), grecv=dma((14,)), glocal=dma((14,)), onsend=dma((14, 2)), onrecv=dma((14, 2)),
         nsend=dma((chips - 1,)), nrecv=dma((chips - 1,)), fsend=dma((chips,)), frecv=dma((chips,)), nlocal=dma((1,)),
         qsend=dma((n_seq - 1,)), qrecv=dma((n_seq - 1,)), tsend=dma((3, n_seq - 1)), trecv=dma((3, n_seq)),
         hsend=dma((n_blk - 1,)), hrecv=dma((n_blk - 1,)), isend=dma((n_seq - 1,)), irecv=dma((n_seq,)),

time: 150 us -> 150 us (level)
  no operation moved by 1% of the time
where the time goes in v9:
time: 150 us; the launch traced here: 149 us
  Pallas kernels  149 us (99%)
    pallas_call x1, Pallas kernels, local_fast(): pl.pallas_call(functools.partial(layer_kernel, sizes), out_shape=(shape((...  143 us
    pallas_call x1, Pallas kernels, finish(): pl.pallas_call(finish_kernel, out_shape=tuple((shape(each, F32) for each...  5.58 us

profile of v9, /device:TPU:8, one launch (start us, length us, event | category | flops | bytes accessed | tf_op | source)
XLA Modules:
  0.0 149.4 jit_solution(5427290313970366499)
XLA Ops:
  0.6 143.2 %layer.1 = (f32[128,1024]{1,0:T(8,128)}, f32[128,1024]{1,0:T(8,128)}, f32[128,1024]{1,0:T(8,128)}, bf16[128,5632]{1,0:T(8,128)(2,1)}, bf16[352,1024]{1,0:T(8,128...) custom-call(f32[1,128]{1,0:T(1,128)} %constant.2.clone.freq, ...), custom_call_target="tpu_custom_call" | custom-call | tf_op jit(solution)/shard_map/layer/pallas_call | solution.py:1285
  143.9 5.6 %finish.1 = (f32[128,1024]{1,0:T(8,128)}, f32[128,1024]{1,0:T(8,128)}, f32[128,1024]{1,0:T(8,128)}, f32[1,128]{1,0:T(1,128)}, f32[1,128]{1,0:T(1,128)}, /*index=...) custom-call(f32[128,1024]{1,0:T(8,128)} %get-tuple-element.34.layer,, ...), custom_call_target="tpu_custom_call" | custom-call | tf_op jit(solution)/shard_map/finish/pallas_call | solution.py:1167
